TPU v7x, 128 devices: a whole 4x4x4 slice. The times are simulated.
128 devices in a mesh: tensor: 4 (over z), dp: 32 (over y, x, core).
Axes of the slice: x: 4, y: 4, z: 4, core: 2. Of those that a mesh axis runs over, the one named last changes fastest.
Arguments:
- text_in: bfloat16 [2, 96, 36, 768], P(None, 'dp', None, 'tensor'), may hold values from -6 to 6
- image_in: bfloat16 [2, 96, 101, 1024], P(None, 'dp', None, 'tensor'), may hold values from -6 to 6
- caption_len: int32 [2, 96], P(None, 'dp'), may hold values from 8 to 36, as said below
- region_count: int32 [2, 96], P(None, 'dp'), may hold values from 10 to 101, as said below
- text_cot: bfloat16 [2, 96, 36, 768], P(None, 'dp', None, 'tensor'), may hold values from -6 to 6
- image_cot: bfloat16 [2, 96, 101, 1024], P(None, 'dp', None, 'tensor'), may hold values from -6 to 6
- co_text_qkv: bfloat16 [3, 768, 1024], P(None, None, 'tensor'), may hold values from -0.21875 to 0.21875
- co_image_qkv: bfloat16 [3, 1024, 1024], P(None, None, 'tensor'), may hold values from -0.1875 to 0.1875
- co_text_out: bfloat16 [1024, 768], P('tensor'), may hold values from -0.5 to 0.5
- co_image_out: bfloat16 [1024, 1024], P('tensor'), may hold values from -0.5 to 0.5
- co_text_up: bfloat16 [768, 3072], P(None, 'tensor'), may hold values from -0.21875 to 0.21875
- co_text_down: bfloat16 [3072, 768], P('tensor'), may hold values from -0.109375 to 0.109375
- co_image_up: bfloat16 [1024, 1024], P(None, 'tensor'), may hold values from -0.1875 to 0.1875
- co_image_down: bfloat16 [1024, 1024], P('tensor'), may hold values from -0.1875 to 0.1875
- self_text_qkv: bfloat16 [3, 768, 768], P(None, None, 'tensor'), may hold values from -0.21875 to 0.21875
- self_image_qkv: bfloat16 [3, 1024, 1024], P(None, None, 'tensor'), may hold values from -0.1875 to 0.1875
- self_text_out: bfloat16 [768, 768], P('tensor'), may hold values from -0.625 to 0.625
- self_image_out: bfloat16 [1024, 1024], P('tensor'), may hold values from -0.5 to 0.5
- text_up: bfloat16 [768, 3072], P(None, 'tensor'), may hold values from -0.21875 to 0.21875
- text_down: bfloat16 [3072, 768], P('tensor'), may hold values from -0.109375 to 0.109375
- image_up: bfloat16 [1024, 1024], P(None, 'tensor'), may hold values from -0.1875 to 0.1875
- image_down: bfloat16 [1024, 1024], P('tensor'), may hold values from -0.1875 to 0.1875
- text_gains: float32 [4, 768], replicated, may hold values from 0.5 to 1.5
- text_shifts: float32 [4, 768], replicated, may hold values from -1.75 to 1.75
- image_gains: float32 [4, 1024], replicated, may hold values from 0.5 to 1.5
- image_shifts: float32 [4, 1024], replicated, may hold values from -1.75 to 1.75
Outputs:
- text_out: float32 [2, 96, 36, 768], P(None, 'dp', None, 'tensor')
- image_out: float32 [2, 96, 101, 1024], P(None, 'dp', None, 'tensor')
- text_grad: float32 [2, 96, 36, 768], P(None, 'dp', None, 'tensor')
- image_grad: float32 [2, 96, 101, 1024], P(None, 'dp', None, 'tensor')
- co_text_qkv_grad: float32 [3, 768, 1024], P(None, None, 'tensor')
- co_image_qkv_grad: float32 [3, 1024, 1024], P(None, None, 'tensor')
- co_text_out_grad: float32 [1024, 768], P('tensor')
- co_image_out_grad: float32 [1024, 1024], P('tensor')
- co_text_up_grad: float32 [768, 3072], P(None, 'tensor')
- co_text_down_grad: float32 [3072, 768], P('tensor')
- co_image_up_grad: float32 [1024, 1024], P(None, 'tensor')
- co_image_down_grad: float32 [1024, 1024], P('tensor')
- self_text_qkv_grad: float32 [3, 768, 768], P(None, None, 'tensor')
- self_image_qkv_grad: float32 [3, 1024, 1024], P(None, None, 'tensor')
- self_text_out_grad: float32 [768, 768], P('tensor')
- self_image_out_grad: float32 [1024, 1024], P('tensor')
- text_up_grad: float32 [768, 3072], P(None, 'tensor')
- text_down_grad: float32 [3072, 768], P('tensor')
- image_up_grad: float32 [1024, 1024], P(None, 'tensor')
- image_down_grad: float32 [1024, 1024], P('tensor')
- text_gains_grad: float32 [4, 768], replicated
- text_shifts_grad: float32 [4, 768], replicated
- image_gains_grad: float32 [4, 1024], replicated
- image_shifts_grad: float32 [4, 1024], replicated
Inputs may be any that keep to these rules, and one draw needn't show every extreme that they name: `caption_len`: A sample's live caption tokens come first; in every draw some sample has all 36. `region_count`: A sample's live region slots come first; in every draw some sample has all 101.
All inputs are finite; a program needn't handle non-finite values.
Results may differ from a plain program's by a relative error of at most 0.023.
Values may be sent and summed in bfloat16 or wider, within the bound.
No kernel may reach another device: no remote copies, remote signals or barrier semaphores. Data moves between devices by JAX's collectives and lax.ppermute only.
A program may use at most 256 MiB of HBM per device.

v0:
```python
import jax
import jax.numpy as jnp
from jax import lax
from jax.sharding import PartitionSpec as P

CO_HEAD = 128
TEXT_HEAD = 64
IMAGE_HEAD = 128


norm_eps = 1e-05
mask_fill = -1000000000.0


def plain_round(values):
    return lax.optimization_barrier(values.astype(jnp.bfloat16)).astype(jnp.float32)


def rounding_pair():
    round_value = jax.custom_vjp(plain_round)
    round_value.defvjp(lambda values: (plain_round(values), None), lambda kept, grad: (grad,))
    round_grad = jax.custom_vjp(lambda values: values)
    round_grad.defvjp(lambda values: (values, None), lambda kept, grad: (plain_round(grad),))
    return (round_value, round_grad)


def low(values):
    return rounding_pair()[0](values)


def low_back(values):
    return rounding_pair()[1](values)


def multiply(left_side, right_side, form):
    return jnp.einsum(form, left_side, right_side)


def normed(values, gain_vec, shift_vec):
    centre = values - jnp.mean(values, axis=-1, keepdims=True)
    spread = jnp.mean(centre * centre, axis=-1, keepdims=True)
    return centre * lax.rsqrt(spread + norm_eps) * gain_vec + shift_vec


def residual_norm(norm_set, text_base, image_base, text_branch, image_branch):
    text_gain, text_shift, image_gain, image_shift = norm_set
    return (
        normed(text_base + text_branch, text_gain, text_shift),
        normed(image_base + image_branch, image_gain, image_shift),
    )


def norm_row(norm_set, position):
    return tuple((member[position] for member in norm_set))


def project(rounded, stacked):
    triple = low(low_back(multiply(rounded, stacked, "bsd,ide->ibse")))
    return (triple[0], triple[1], triple[2])


def attend(query_rows, key_rows, value_rows, key_mask, head_size):
    sample_count, query_count, feature_width = query_rows.shape
    key_count = key_rows.shape[1]
    head_count = feature_width // head_size
    query_heads = query_rows.reshape(sample_count, query_count, head_count, head_size)
    key_heads = key_rows.reshape(sample_count, key_count, head_count, head_size)
    value_heads = value_rows.reshape(sample_count, key_count, head_count, head_size)
    scores = low_back(multiply(query_heads, key_heads, "bqhd,bkhd->bhqk") * head_size ** (-0.5))
    scores = jnp.where(key_mask[:, None, None, :] > 0, scores, mask_fill)
    row_top = jnp.max(scores, axis=-1, keepdims=True)
    exponent = jnp.exp(scores - row_top)
    probability = exponent / jnp.sum(exponent, axis=-1, keepdims=True)
    attended = multiply(low(probability), value_heads, "bhqk,bkhd->bqhd")
    return low(low_back(attended.reshape(sample_count, query_count, feature_width)))


def co_branch(weight_set, text_base, image_base, text_mask, image_mask):
    text_qkv, image_qkv, text_proj, image_proj = weight_set
    text_query, text_key, text_value = project(low(text_base), text_qkv)
    image_query, image_key, image_value = project(low(image_base), image_qkv)
    text_mixed = attend(text_query, image_key, image_value, image_mask, CO_HEAD)
    image_mixed = attend(image_query, text_key, text_value, text_mask, CO_HEAD)
    return (
        low_back(multiply(text_mixed, text_proj, "bse,ed->bsd")),
        low_back(multiply(image_mixed, image_proj, "bse,ed->bsd")),
    )


def self_branch(weight_set, text_base, image_base, text_mask, image_mask):
    text_qkv, image_qkv, text_proj, image_proj = weight_set
    text_query, text_key, text_value = project(low(text_base), text_qkv)
    image_query, image_key, image_value = project(low(image_base), image_qkv)
    text_mixed = attend(text_query, text_key, text_value, text_mask, TEXT_HEAD)
    image_mixed = attend(image_query, image_key, image_value, image_mask, IMAGE_HEAD)
    return (
        low_back(multiply(text_mixed, text_proj, "bse,ed->bsd")),
        low_back(multiply(image_mixed, image_proj, "bse,ed->bsd")),
    )


def mlp_branch(weight_set, text_base, image_base):
    text_up_w, text_down_w, image_up_w, image_down_w = weight_set
    text_hidden = low_back(multiply(low(text_base), text_up_w, "bsd,df->bsf"))
    text_branch = low_back(
        multiply(low(jax.nn.gelu(text_hidden, approximate=False)), text_down_w, "bsf,fd->bsd")
    )
    image_hidden = low_back(multiply(low(image_base), image_up_w, "bsd,df->bsf"))
    image_branch = low_back(
        multiply(low(jax.nn.gelu(image_hidden, approximate=False)), image_down_w, "bsf,fd->bsd")
    )
    return (text_branch, image_branch)


def shards(
    text_in,
    image_in,
    caption_len,
    region_count,
    text_cot,
    image_cot,
    co_text_qkv,
    co_image_qkv,
    co_text_out,
    co_image_out,
    co_text_up,
    co_text_down,
    co_image_up,
    co_image_down,
    self_text_qkv,
    self_image_qkv,
    self_text_out,
    self_image_out,
    text_up,
    text_down,
    image_up,
    image_down,
    text_gains,
    text_shifts,
    image_gains,
    image_shifts,
):
    own_rank = lax.axis_index("tensor")
    text_slice = text_in.shape[3]
    image_slice = image_in.shape[3]
    arrays = [
        co_text_qkv,
        co_image_qkv,
        co_text_out,
        co_image_out,
        co_text_up,
        co_text_down,
        co_image_up,
        co_image_down,
        self_text_qkv,
        self_image_qkv,
        self_text_out,
        self_image_out,
        text_up,
        text_down,
        image_up,
        image_down,
        text_gains,
        text_shifts,
        image_gains,
        image_shifts,
    ]
    arrays = [member.astype(jnp.float32) for member in arrays]
    co_set = tuple(arrays[0:4])
    co_mlp_set = tuple(arrays[4:8])
    self_set = tuple(arrays[8:12])
    mlp_set = tuple(arrays[12:16])
    norm_set = tuple(arrays[16:20])
    text_mask = (
        jnp.arange(text_in.shape[2], dtype=jnp.int32)[None, None, :] < caption_len[:, :, None]
    ).astype(jnp.int32)
    image_mask = (
        jnp.arange(image_in.shape[2], dtype=jnp.int32)[None, None, :] < region_count[:, :, None]
    ).astype(jnp.int32)
    gathered = (
        lax.all_gather(text_in, "tensor", axis=3, tiled=True),
        lax.all_gather(image_in, "tensor", axis=3, tiled=True),
        lax.all_gather(text_cot, "tensor", axis=3, tiled=True),
        lax.all_gather(image_cot, "tensor", axis=3, tiled=True),
    )
    running = None
    text_outs = []
    image_outs = []
    text_grads = []
    image_grads = []
    for micro_index in range(text_in.shape[0]):
        text_keys = text_mask[micro_index]
        image_keys = image_mask[micro_index]

        def co_fn(weight_set, text_arg, image_arg):
            return co_branch(weight_set, text_arg, image_arg, text_keys, image_keys)

        def self_fn(weight_set, text_arg, image_arg):
            return self_branch(weight_set, text_arg, image_arg, text_keys, image_keys)

        blocks = [
            (co_fn, co_set),
            (mlp_branch, co_mlp_set),
            (self_fn, self_set),
            (mlp_branch, mlp_set),
        ]
        block_grads = [None, None, None, None]
        norm_grads = [None, None, None, None]
        kept = []
        text_base = gathered[0][micro_index].astype(jnp.float32)
        image_base = gathered[1][micro_index].astype(jnp.float32)
        for position in range(4):
            branch_fn, weight_set = blocks[position]
            (part_text, part_image), back_branch = jax.vjp(
                branch_fn, weight_set, text_base, image_base
            )
            sum_text, sum_image = lax.psum((part_text, part_image), "tensor")
            (text_base, image_base), back_norm = jax.vjp(
                residual_norm,
                norm_row(norm_set, position),
                text_base,
                image_base,
                sum_text,
                sum_image,
            )
            kept.append((back_branch, back_norm))
        text_outs.append(lax.dynamic_slice_in_dim(text_base, own_rank * text_slice, text_slice, 2))
        image_outs.append(
            lax.dynamic_slice_in_dim(image_base, own_rank * image_slice, image_slice, 2)
        )
        grad_text = gathered[2][micro_index].astype(jnp.float32)
        grad_image = gathered[3][micro_index].astype(jnp.float32)
        for position in (3, 2, 1, 0):
            back_branch, back_norm = kept[position]
            norm_grads[position], base_text, base_image, branch_text, branch_image = back_norm(
                (grad_text, grad_image)
            )
            block_grads[position], part_text, part_image = back_branch((branch_text, branch_image))
            if position > 0:
                extra_text, extra_image = lax.psum((part_text, part_image), "tensor")
                grad_text = base_text + extra_text
                grad_image = base_image + extra_image
            else:
                share_text, share_image = (
                    lax.psum_scatter(part_text, "tensor", scatter_dimension=2, tiled=True),
                    lax.psum_scatter(part_image, "tensor", scatter_dimension=2, tiled=True),
                )
                text_grads.append(
                    share_text
                    + lax.dynamic_slice_in_dim(base_text, own_rank * text_slice, text_slice, 2)
                )
                image_grads.append(
                    share_image
                    + lax.dynamic_slice_in_dim(base_image, own_rank * image_slice, image_slice, 2)
                )
        norm_members = [
            jnp.stack([norm_grads[position][member] for position in range(4)])
            for member in range(4)
        ]
        micro_grads = (
            list(block_grads[0])
            + list(block_grads[1])
            + list(block_grads[2])
            + list(block_grads[3])
            + norm_members
        )
        running = (
            micro_grads
            if running is None
            else [earlier + latest for earlier, latest in zip(running, micro_grads)]
        )
    summed = list(
        lax.psum(
            (
                running[0],
                running[1],
                running[2],
                running[3],
                running[4],
                running[5],
                running[6],
                running[7],
                running[8],
                running[9],
                running[10],
                running[11],
                running[12],
                running[13],
                running[14],
                running[15],
                running[16],
                running[17],
                running[18],
                running[19],
            ),
            "dp",
        )
    )
    return (
        jnp.stack(text_outs),
        jnp.stack(image_outs),
        jnp.stack(text_grads),
        jnp.stack(image_grads),
        summed[0],
        summed[1],
        summed[2],
        summed[3],
        summed[4],
        summed[5],
        summed[6],
        summed[7],
        summed[8],
        summed[9],
        summed[10],
        summed[11],
        summed[12],
        summed[13],
        summed[14],
        summed[15],
        summed[16],
        summed[17],
        summed[18],
        summed[19],
    )


def solution(mesh):
    in_specs = (
        P(None, "dp", None, "tensor"),
        P(None, "dp", None, "tensor"),
        P(None, "dp"),
        P(None, "dp"),
        P(None, "dp", None, "tensor"),
        P(None, "dp", None, "tensor"),
        P(None, None, "tensor"),
        P(None, None, "tensor"),
        P("tensor", None),
        P("tensor", None),
        P(None, "tensor"),
        P("tensor", None),
        P(None, "tensor"),
        P("tensor", None),
        P(None, None, "tensor"),
        P(None, None, "tensor"),
        P("tensor", None),
        P("tensor", None),
        P(None, "tensor"),
        P("tensor", None),
        P(None, "tensor"),
        P("tensor", None),
        P(),
        P(),
        P(),
        P(),
    )
    out_specs = (
        P(None, "dp", None, "tensor"),
        P(None, "dp", None, "tensor"),
        P(None, "dp", None, "tensor"),
        P(None, "dp", None, "tensor"),
        P(None, None, "tensor"),
        P(None, None, "tensor"),
        P("tensor", None),
        P("tensor", None),
        P(None, "tensor"),
        P("tensor", None),
        P(None, "tensor"),
        P("tensor", None),
        P(None, None, "tensor"),
        P(None, None, "tensor"),
        P("tensor", None),
        P("tensor", None),
        P(None, "tensor"),
        P("tensor", None),
        P(None, "tensor"),
        P("tensor", None),
        P(),
        P(),
        P(),
        P(),
    )
    return jax.shard_map(shards, mesh=mesh, in_specs=in_specs, out_specs=out_specs, check_vma=False)
```

profile of v0, /device:TPU:0, one launch (start us, length us, event | category | flops | bytes accessed | tf_op | source)
XLA Modules:
  0.0 1299.0 jit_solution(587747733238959479)
XLA Ops:
  10.8 19.0 %all_gather.12 = bf16[2,3,36,768]{2,0,1,3:T(2,128)(2,1)S(1)} all-gather(bf16[2,3,36,192]{2,0,1,3:T(2,128)(2,1)S(1)} %copy.248), channel_id=1, replica_groups=mesh['tensor'=4,'dp'=32] {'tensor'}, dimensions={3}, use_global_device_ids=true | all-gather | bytes 414720 | tf_op jit(solution)/shard_map/all_gather | solution.py:181
  29.8 3.0 fusion.554
  32.8 3.5 copy.389
  36.4 3.5 copy.390
  44.7 2.4 slice_bitcast_fusion.1
  80.4 76.7 %all-reduce.56.cloned.1.call-done = (f32[3,36,768]{2,1,0:T(8,128)}, f32[3,36,768]{2,1,0:T(8,128)}, f32[3,101,1024]{2,1,0:T(8,128)}, f32[3,101,1024]{2,1,0:T(8,128)}) async-done(((f32[3,36,768]{2,1,0:T(8,128)}, f32[3,36,768]{2,1,0:T(8,128)}, f32[3,101,1024]{2,1,0:T(8,128)}, f32[3,101,1024]{2,1,0:T(8,128)}), (f32[3,36,768]{2,1,0:T(8,128)}, f32[3,36,768]{2,1,0:T(8,128)}, f32[3,101,1024]{2,1,0:T(8,128)}, ...) | async-done | bytes 3145744 | tf_op jit(solution)/shard_map/psum | solution.py:217
  175.4 78.6 %all-reduce.54.cloned.1.call-done = (f32[3,36,768]{2,1,0:T(8,128)}, f32[3,36,768]{2,1,0:T(8,128)}, f32[3,101,1024]{2,1,0:T(8,128)}, f32[3,101,1024]{2,1,0:T(8,128)}) async-done(((f32[3,36,768]{2,1,0:T(8,128)}, f32[3,36,768]{2,1,0:T(8,128)}, f32[3,101,1024]{2,1,0:T(8,128)}, f32[3,101,1024]{2,1,0:T(8,128)}), (f32[3,36,768]{2,1,0:T(8,128)}, f32[3,36,768]{2,1,0:T(8,128)}, f32[3,101,1024]{2,1,0:T(8,128)}, ...) | async-done | bytes 3145744 | tf_op jit(solution)/shard_map/psum | solution.py:217
  280.9 2.5 fusion.542
  310.7 2.6 fusion.190
  315.2 78.4 %all-reduce.52.cloned.1.call-done = (f32[3,36,768]{2,1,0:T(8,128)}, f32[3,36,768]{2,1,0:T(8,128)}, f32[3,101,1024]{2,1,0:T(8,128)}, f32[3,101,1024]{2,1,0:T(8,128)}) async-done(((f32[3,36,768]{2,1,0:T(8,128)}, f32[3,36,768]{2,1,0:T(8,128)}, f32[3,101,1024]{2,1,0:T(8,128)}, f32[3,101,1024]{2,1,0:T(8,128)}), (f32[3,36,768]{2,1,0:T(8,128)}, f32[3,36,768]{2,1,0:T(8,128)}, f32[3,101,1024]{2,1,0:T(8,128)}, ...) | async-done | bytes 3145744 | tf_op jit(solution)/shard_map/psum | solution.py:217
  416.5 21.4 %all_gather.15 = bf16[2,3,36,768]{2,0,1,3:T(2,128)(2,1)S(1)} all-gather(bf16[2,3,36,192]{2,0,1,3:T(2,128)(2,1)} %copy.302), channel_id=1, replica_groups=mesh['tensor'=4,'dp'=32] {'tensor'}, dimensions={3}, use_global_device_ids=true | all-gather | bytes 414720 | tf_op jit(solution)/shard_map/all_gather | solution.py:183
  438.0 3.1 fusion.555
  441.0 4.6 copy.391
  445.7 4.5 copy.392
  450.2 48.0 %all-reduce.50.cloned.1.call-done = (f32[3,36,768]{2,1,0:T(8,128)}, f32[3,36,768]{2,1,0:T(8,128)}, f32[3,101,1024]{2,1,0:T(8,128)}, f32[3,101,1024]{2,1,0:T(8,128)}) async-done(((f32[3,36,768]{2,1,0:T(8,128)}, f32[3,36,768]{2,1,0:T(8,128)}, f32[3,101,1024]{2,1,0:T(8,128)}, f32[3,101,1024]{2,1,0:T(8,128)}), (f32[3,36,768]{2,1,0:T(8,128)}, f32[3,36,768]{2,1,0:T(8,128)}, f32[3,101,1024]{2,1,0:T(8,128)}, ...) | async-done | bytes 3145744 | tf_op jit(solution)/shard_map/psum | solution.py:217
  507.8 2.1 fusion.526
  513.5 13.8 %all-gather.5.cloned.1.call-done = bf16[2,3,101,1024]{3,2,1,0:T(8,128)(2,1)} async-done(((bf16[2,3,101,256]{3,2,1,0:T(8,128)(2,1)}), bf16[2,3,101,1024]{3,2,1,0:T(8,128)(2,1)}) %all-gather.5.cloned.1.call-update) | async-done | bytes 1241104 | tf_op jit(solution)/shard_map/all_gather | solution.py:184
  527.4 2.0 fusion.59
  529.4 2.7 fusion.508
  532.2 3.3 fusion.61
  547.1 74.5 %all-reduce.48.cloned.1.call-done = (f32[3,36,768]{2,1,0:T(8,128)}, f32[3,101,1024]{2,1,0:T(8,128)}, f32[3,36,768]{2,1,0:T(8,128)}, f32[3,101,1024]{2,1,0:T(8,128)}) async-done(((f32[3,36,768]{2,1,0:T(8,128)}, f32[3,101,1024]{2,1,0:T(8,128)}, f32[3,36,768]{2,1,0:T(8,128)}, f32[3,101,1024]{2,1,0:T(8,128)}), (f32[3,36,768]{2,1,0:T(8,128)}, f32[3,101,1024]{2,1,0:T(8,128)}, f32[3,36,768]{2,1,0:T(8,128)}, ...) | async-done | bytes 3145744 | tf_op jit(solution)/shard_map/psum | solution.py:240
  621.6 2.3 multiply_reduce_fusion.23
  653.7 3.0 multiply_reduce_fusion.3
  665.0 2.0 convolution_bitcast_fusion.28
  667.0 2.0 multiply_reduce_fusion.40
  673.4 2.0 convolution_bitcast_fusion.29
  697.0 2.4 convolution_bitcast_fusion.18
  701.4 1.9 reshape.872
  705.1 2.1 reshape.859
  710.9 1.9 reshape.860
  712.9 1.9 reshape.861
  714.8 2.0 add_convert_fusion.9
  720.6 1.9 reshape.874
  737.8 68.4 %all-reduce.46.cloned.1.call-done = (f32[3,36,768]{2,1,0:T(8,128)}, f32[3,101,1024]{2,1,0:T(8,128)}, f32[3,36,768]{2,1,0:T(8,128)}, f32[3,101,1024]{2,1,0:T(8,128)}) async-done(((f32[3,36,768]{2,1,0:T(8,128)}, f32[3,101,1024]{2,1,0:T(8,128)}, f32[3,36,768]{2,1,0:T(8,128)}, f32[3,101,1024]{2,1,0:T(8,128)}), (f32[3,36,768]{2,1,0:T(8,128)}, f32[3,101,1024]{2,1,0:T(8,128)}, f32[3,36,768]{2,1,0:T(8,128)}, ...) | async-done | bytes 3145744 | tf_op jit(solution)/shard_map/psum | solution.py:240
  806.3 2.7 multiply_reduce_fusion.24
  810.4 4.0 multiply_reduce_fusion.4
  839.1 2.7 fusion
  845.2 61.9 %all-reduce.44.cloned.1.call-done = (f32[3,36,768]{2,1,0:T(8,128)}, f32[3,101,1024]{2,1,0:T(8,128)}, f32[3,36,768]{2,1,0:T(8,128)}, f32[3,101,1024]{2,1,0:T(8,128)}) async-done(((f32[3,36,768]{2,1,0:T(8,128)}, f32[3,101,1024]{2,1,0:T(8,128)}, f32[3,36,768]{2,1,0:T(8,128)}, f32[3,101,1024]{2,1,0:T(8,128)}), (f32[3,36,768]{2,1,0:T(8,128)}, f32[3,101,1024]{2,1,0:T(8,128)}, f32[3,36,768]{2,1,0:T(8,128)}, ...) | async-done | bytes 3145744 | tf_op jit(solution)/shard_map/psum | solution.py:240
  907.1 2.6 fusion.513
  909.8 3.7 fusion.511
  915.3 2.6 fusion.514
  960.6 2.7 fusion.41
  970.8 2.7 fusion.1
  981.0 129.7 %all-reduce.24 = (f32[4,768]{1,0:T(4,128)}, f32[4,768]{1,0:T(4,128)}, f32[4,1024]{1,0:T(4,128)}, f32[4,1024]{1,0:T(4,128)}) all-reduce(f32[4,768]{1,0:T(4,128)S(1)} %maximum_add_fusion.2, f32[4,768]{1,0:T(4,128)S(1)} %maximum_add_fusion.3, f32[4,1024]{1,0:T(4,128)S(1)} %maximum_add_fusion, ...), channel_id=1, replica_groups=mesh['tensor'=4,'dp'=32] {'dp'}, use_global_device_ids=true, to_apply=%region_160.161 | all-reduce | flops 14336 | bytes 114688 | tf_op jit(solution)/shard_map/psum | solution.py:273
  1119.6 141.3 %all-reduce.42.cloned.1.call-done = (f32[3,768,256]{1,2,0:T(8,128)}, f32[3,1024,256]{1,2,0:T(8,128)}, f32[256,768]{1,0:T(8,128)}, f32[256,1024]{1,0:T(8,128)}, f...) async-done(((f32[3,768,256]{1,2,0:T(8,128)}, ...) | async-done | bytes 27525136 | tf_op jit(solution)/shard_map/psum | solution.py:273
  1260.9 3.0 copy.358
  1264.0 3.5 copy.359
  1267.5 3.6 copy.360
  (1534 shorter events, 367.3 us)
Async XLA Ops:
  7.2 279.1 %copy-start = (bf16[3,1024,256]{2,1,0:T(8,128)(2,1)S(1)}, bf16[3,1024,256]{2,1,0:T(8,128)(2,1)}, u32[]{:S(2)}) copy-start(bf16[3,1024,256]{2,1,0:T(8,128)(2,1)} %param.41) | copy-start | bytes 4718596
  7.2 37.5 %all-gather.3.cloned.1.call-start = ((), (), s32[]{:S(2)}) async-start(), calls=%async_computation.4 | async-start | bytes 1597440 | tf_op jit(solution)/shard_map/all_gather | solution.py:182
  9.1 148.0 %all-reduce.56.cloned.1.call-start = ((), (), s32[]{:S(2)}) async-start(), calls=%async_computation.17 | async-start | bytes 6586368 | tf_op jit(solution)/shard_map/psum | solution.py:217
  36.4 122.2 %copy-start.101 = (bf16[1,3,36,768]{3,2,1,0:T(8,128)(2,1)}, bf16[1,3,36,768]{3,2,1,0:T(8,128)(2,1)S(1)}, u32[]{:S(2)}) copy-start(bf16[1,3,36,768]{3,2,1,0:T(8,128)(2,1)S(1)} %copy.389) | copy-start | bytes 497668
  39.9 117.2 %copy-start.99 = (bf16[1,3,36,768]{3,2,1,0:T(8,128)(2,1)}, bf16[1,3,36,768]{3,2,1,0:T(8,128)(2,1)S(1)}, u32[]{:S(2)}) copy-start(bf16[1,3,36,768]{3,2,1,0:T(8,128)(2,1)S(1)} %copy.390) | copy-start | bytes 497668
  44.6 23.5 %copy-start.491 = (pred[3,36]{1,0:T(4,128)(4,1)}, pred[3,36]{1,0:T(4,128)(4,1)S(1)}, u32[]{:S(2)}) copy-start(pred[3,36]{1,0:T(4,128)(4,1)S(1)} %get-tuple-element.405) | copy-start | bytes 328
  44.7 10.1 copy-start.494
  44.7 25.5 %copy-start.497 = (pred[3,101]{1,0:T(4,128)(4,1)}, pred[3,101]{1,0:T(4,128)(4,1)S(1)}, u32[]{:S(2)}) copy-start(pred[3,101]{1,0:T(4,128)(4,1)S(1)} %get-tuple-element.407) | copy-start | bytes 913
  77.2 176.7 %all-reduce.54.cloned.1.call-start = ((), (), s32[]{:S(2)}) async-start(), calls=%async_computation.16 | async-start | bytes 6586368 | tf_op jit(solution)/shard_map/psum | solution.py:217
  78.5 175.4 %copy-start.296 = (f32[768]{0:T(1024)}, f32[768]{0:T(1024)S(1)}, u32[]{:S(2)}) copy-start(f32[768]{0:T(1024)S(1)} %get-tuple-element.156) | copy-start | bytes 9220
  78.5 177.6 %copy-start.305 = (f32[768]{0:T(1024)}, f32[768]{0:T(1024)S(1)}, u32[]{:S(2)}) copy-start(f32[768]{0:T(1024)S(1)} %get-tuple-element.155) | copy-start | bytes 9220
  79.2 80.1 %copy-start.403 = (f32[768]{0:T(1024)}, f32[768]{0:T(1024)S(1)}, u32[]{:S(2)}) copy-start(f32[768]{0:T(1024)S(1)} %get-tuple-element.160) | copy-start | bytes 9220
  79.2 176.9 %copy-start.402 = (f32[768]{0:T(1024)}, f32[768]{0:T(1024)S(1)}, u32[]{:S(2)}) copy-start(f32[768]{0:T(1024)S(1)} %get-tuple-element.159) | copy-start | bytes 9220
  79.8 201.1 %copy-start.300 = (f32[1,1024]{1,0:T(1,128)}, f32[1,1024]{1,0:T(1,128)S(1)}, u32[]{:S(2)}) copy-start(f32[1,1024]{1,0:T(1,128)S(1)} %get-tuple-element.347) | copy-start | bytes 12292
  79.8 205.2 %copy-start.302 = (f32[1,1024]{1,0:T(1,128)}, f32[1,1024]{1,0:T(1,128)S(1)}, u32[]{:S(2)}) copy-start(f32[1,1024]{1,0:T(1,128)S(1)} %get-tuple-element.346) | copy-start | bytes 12292
  80.4 86.9 %copy-start.400 = (f32[1,1024]{1,0:T(1,128)}, f32[1,1024]{1,0:T(1,128)S(1)}, u32[]{:S(2)}) copy-start(f32[1,1024]{1,0:T(1,128)S(1)} %get-tuple-element.343) | copy-start | bytes 12292
  158.3 95.7 %copy-start.307 = (f32[3,36]{1,0:T(4,128)}, f32[3,36]{1,0:T(4,128)S(1)}, u32[]{:S(2)}) copy-start(f32[3,36]{1,0:T(4,128)S(1)} %broadcast_multiply_fusion.11) | copy-start | bytes 1300
  158.5 95.5 %copy-start.372 = (f32[3,36]{1,0:T(4,128)}, f32[3,36]{1,0:T(4,128)S(1)}, u32[]{:S(2)}) copy-start(f32[3,36]{1,0:T(4,128)S(1)} %fusion.470) | copy-start | bytes 1300
  159.1 94.9 %copy-start.309 = (f32[3,36]{1,0:T(4,128)}, f32[3,36]{1,0:T(4,128)S(1)}, u32[]{:S(2)}) copy-start(f32[3,36]{1,0:T(4,128)S(1)} %broadcast_multiply_fusion.15) | copy-start | bytes 1300
  159.3 94.7 %copy-start.374 = (f32[3,36]{1,0:T(4,128)}, f32[3,36]{1,0:T(4,128)S(1)}, u32[]{:S(2)}) copy-start(f32[3,36]{1,0:T(4,128)S(1)} %fusion.466) | copy-start | bytes 1300
  175.1 79.0 %copy-start.404 = (f32[768]{0:T(1024)S(1)}, f32[768]{0:T(1024)}, u32[]{:S(2)}) copy-start(f32[768]{0:T(1024)} %copy-done.403) | copy-start | bytes 9220
  175.1 218.6 %all-reduce.52.cloned.1.call-start = ((), (), s32[]{:S(2)}) async-start(), calls=%async_computation.15 | async-start | bytes 6586368 | tf_op jit(solution)/shard_map/psum | solution.py:217
  266.4 10.9 copy-start.287
  267.1 10.2 copy-start.73
  273.1 10.3 copy-start.289
  314.7 183.4 %all-reduce.50.cloned.1.call-start = ((), (), s32[]{:S(2)}) async-start(), calls=%async_computation.14 | async-start | bytes 6586368 | tf_op jit(solution)/shard_map/psum | solution.py:217
  412.8 114.5 %all-gather.5.cloned.1.call-start = ((), (), s32[]{:S(2)}) async-start(), calls=%async_computation.5 | async-start | bytes 1597440 | tf_op jit(solution)/shard_map/all_gather | solution.py:184
  414.6 207.0 %all-reduce.48.cloned.1.call-start = ((), (), s32[]{:S(2)}) async-start(), calls=%async_computation.13 | async-start | bytes 6586368 | tf_op jit(solution)/shard_map/psum | solution.py:240
  541.5 264.6 %all-reduce.46.cloned.1.call-start = ((), (), s32[]{:S(2)}) async-start(), calls=%async_computation.12 | async-start | bytes 6586368 | tf_op jit(solution)/shard_map/psum | solution.py:240
  642.3 11.2 copy-start.23
  727.3 179.8 %all-reduce.44.cloned.1.call-start = ((), (), s32[]{:S(2)}) async-start(), calls=%async_computation.11 | async-start | bytes 6586368 | tf_op jit(solution)/shard_map/psum | solution.py:240
  735.8 70.4 %copy-start.306 = (f32[768]{0:T(1024)S(1)}, f32[768]{0:T(1024)}, u32[]{:S(2)}) copy-start(f32[768]{0:T(1024)} %copy-done.305) | copy-start | bytes 9220
  735.8 70.4 %copy-start.354 = (f32[3,36]{1,0:T(4,128)S(1)}, f32[3,36]{1,0:T(4,128)}, u32[]{:S(2)}) copy-start(f32[3,36]{1,0:T(4,128)} %copy-done.353) | copy-start | bytes 1300
  735.8 70.4 %copy-start.356 = (f32[3,36]{1,0:T(4,128)S(1)}, f32[3,36]{1,0:T(4,128)}, u32[]{:S(2)}) copy-start(f32[3,36]{1,0:T(4,128)} %copy-done.355) | copy-start | bytes 1300
  735.8 70.4 %copy-start.385 = (f32[3,36]{1,0:T(4,128)S(1)}, f32[3,36]{1,0:T(4,128)}, u32[]{:S(2)}) copy-start(f32[3,36]{1,0:T(4,128)} %copy-done.384) | copy-start | bytes 1300
  735.8 70.4 %copy-start.387 = (f32[3,36]{1,0:T(4,128)S(1)}, f32[3,36]{1,0:T(4,128)}, u32[]{:S(2)}) copy-start(f32[3,36]{1,0:T(4,128)} %copy-done.386) | copy-start | bytes 1300
  735.9 70.4 %copy-start.449 = (f32[3,36]{1,0:T(4,128)S(1)}, f32[3,36]{1,0:T(4,128)}, u32[]{:S(2)}) copy-start(f32[3,36]{1,0:T(4,128)} %negate_multiply_fusion.18) | copy-start | bytes 1300
  735.9 70.4 %copy-start.451 = (f32[3,36]{1,0:T(4,128)S(1)}, f32[3,36]{1,0:T(4,128)}, u32[]{:S(2)}) copy-start(f32[3,36]{1,0:T(4,128)} %copy-done.450) | copy-start | bytes 1300
  735.9 73.2 %copy-start.435 = (f32[3,36]{1,0:T(4,128)S(1)}, f32[3,36]{1,0:T(4,128)}, u32[]{:S(2)}) copy-start(f32[3,36]{1,0:T(4,128)} %copy-done.434) | copy-start | bytes 1300
  735.9 73.2 %copy-start.437 = (f32[3,36]{1,0:T(4,128)S(1)}, f32[3,36]{1,0:T(4,128)}, u32[]{:S(2)}) copy-start(f32[3,36]{1,0:T(4,128)} %copy-done.436) | copy-start | bytes 1300
  828.2 282.4 %reduce-scatter.13.cloned.1.call-start = ((), (), s32[]{:S(2)}) async-start(), calls=%async_computation.8 | async-start | bytes 491520
  843.3 63.8 %copy-start.297 = (f32[768]{0:T(1024)S(1)}, f32[768]{0:T(1024)}, u32[]{:S(2)}) copy-start(f32[768]{0:T(1024)} %copy-done.296) | copy-start | bytes 9220
  843.3 63.8 %copy-start.308 = (f32[3,36]{1,0:T(4,128)S(1)}, f32[3,36]{1,0:T(4,128)}, u32[]{:S(2)}) copy-start(f32[3,36]{1,0:T(4,128)} %copy-done.307) | copy-start | bytes 1300
  843.3 63.8 %copy-start.310 = (f32[3,36]{1,0:T(4,128)S(1)}, f32[3,36]{1,0:T(4,128)}, u32[]{:S(2)}) copy-start(f32[3,36]{1,0:T(4,128)} %copy-done.309) | copy-start | bytes 1300
  933.2 178.7 %reduce-scatter.15.cloned.1.call-start = ((), (), s32[]{:S(2)}) async-start(), calls=%async_computation.9 | async-start | bytes 491520
  937.1 179.1 %reduce-scatter.9.cloned.1.call-start = ((), (), s32[]{:S(2)}) async-start(), calls=%async_computation.6 | async-start | bytes 1597440 | tf_op jit(solution)/shard_map/reduce_scatter | solution.py:246
  942.6 174.6 %reduce-scatter.11.cloned.1.call-start = ((), (), s32[]{:S(2)}) async-start(), calls=%async_computation.7 | async-start | bytes 1597440 | tf_op jit(solution)/shard_map/reduce_scatter | solution.py:246
  959.5 301.4 %all-reduce.42.cloned.1.call-start = ((), (), s32[]{:S(2)}) async-start(), calls=%async_computation.10 | async-start | bytes 55050240 | tf_op jit(solution)/shard_map/psum | solution.py:273
  (478 other events, 1092.8 us)
Sparse Core Ops, SparseCore 0:
  10.3 31.9 all-gather.2
  77.4 79.6 all-reduce.55
  175.2 78.7 all-reduce.53
  314.8 78.7 all-reduce.51
  413.0 85.1 all-reduce.49
  499.7 27.6 all-gather.4
  541.7 79.9 all-reduce.47
  727.4 78.7 all-reduce.45
  828.3 78.7 all-reduce.43
  933.3 20.8 reduce-scatter.12
  957.2 20.7 reduce-scatter.14
  980.4 24.1 reduce-scatter.8
  1006.9 24.1 reduce-scatter.10
  1040.1 220.7 all-reduce.41
where the time goes:
time: 1310 us; the launch traced here: 1300 us
  waiting for transfers between devices  642 us (49%)
  local copies, waits for them, and re-layouts  204 us (16%)
  blocking collectives  170 us (13%)
  matrix products  162 us (12%)
  other arithmetic  97.2 us (7%)
  between operations  20.5 us (2%)
    psum x4, waiting for transfers between devices, shards(): sum_text, sum_image = lax.psum((part_text, part_image), 'tensor')  282 us
    psum x3, waiting for transfers between devices, shards(): extra_text, extra_image = lax.psum((part_text, part_image), 'tensor')  205 us
    dot_general x144, matrix products, multiply(): return jnp.einsum(form, left_side, right_side)  162 us
    psum x1, waiting for transfers between devices, shards(): lax.psum((running[0], running[1], running[2], running[3], running[4], run...  141 us
    psum x1, blocking collectives, shards(): lax.psum((running[0], running[1], running[2], running[3], running[4], run...  130 us
    unnamed x1060, local copies, waits for them, and re-layouts  102 us
    reduce_sum x18, other arithmetic, normed(): return centre * lax.rsqrt(spread + norm_eps) * gain_vec + shift_vec  33.4 us
  transfers between devices with their start and end apart: 14, of which 9 were waited for; matrix products, arithmetic and copies ran while one was open for 10% of the time, Pallas kernels for 0%

commit v1 on v0

v1 whole, which is shorter than its diff:
```python
import functools

import jax
import jax.numpy as jnp
from jax import lax
from jax.experimental import pallas as pl
from jax.experimental.pallas import tpu as pltpu
from jax.sharding import PartitionSpec as P

CO_HEAD = 128
TEXT_HEAD = 64
IMAGE_HEAD = 128
EPS = 1e-05
FILL = -1000000000.0
ROOT_HALF = 0.7071067811865476
INV_ROOT_TWO_PI = 0.3989422804014327
F32 = jnp.float32
BF = jnp.bfloat16
Z = 4


def dot(a, b):
    return lax.dot_general(a, b, (((1,), (0,)), ((), ())), preferred_element_type=F32)


def dot_nt(a, b):
    return lax.dot_general(a, b, (((1,), (1,)), ((), ())), preferred_element_type=F32)


def dot_tn(a, b):
    return lax.dot_general(a, b, (((0,), (0,)), ((), ())), preferred_element_type=F32)


def part(index, size):
    return pl.ds(pl.multiple_of(index * size, size), size)


def row_ids(count, step, samples):
    place = lax.broadcasted_iota(jnp.int32, (count, 1), 0)
    ids = jnp.zeros((count, 1), jnp.int32)
    for s in range(1, samples):
        ids = ids + (place >= s * step).astype(jnp.int32)
    return ids


def probabilities(q, k, same, scale):
    s = jnp.where(same, dot_nt(q, k) * scale, FILL)
    e = jnp.exp(s - jnp.max(s, axis=-1, keepdims=True))
    return e / jnp.sum(e, axis=-1, keepdims=True)


def head_fwd(q, k, v, same, scale):
    return dot(probabilities(q, k, same, scale).astype(BF), v).astype(BF)


def head_bwd(q, k, v, same, scale, do):
    p = probabilities(q, k, same, scale)
    dv = dot_tn(p.astype(BF), do)
    dp = dot_nt(do, v)
    ds = (p * (dp - jnp.sum(dp * p, axis=-1, keepdims=True))).astype(BF)
    dq = dot(ds, k) * scale
    dk = dot_tn(ds, q) * scale
    return dq.astype(BF), dk.astype(BF), dv.astype(BF)


def gelu(u):
    return u * (1.0 + lax.erf(u * ROOT_HALF)) * 0.5


def gelu_slope(u):
    return (1.0 + lax.erf(u * ROOT_HALF)) * 0.5 + u * jnp.exp(u * u * -0.5) * INV_ROOT_TWO_PI


def normalise(z):
    centre = z - jnp.mean(z, axis=-1, keepdims=True)
    rstd = lax.rsqrt(jnp.mean(centre * centre, axis=-1, keepdims=True) + EPS)
    return centre * rstd, rstd


def norm_back(z, gain, dy):
    xhat, rstd = normalise(z)
    dxh = dy * gain
    dz = rstd * (
        dxh
        - jnp.mean(dxh, axis=-1, keepdims=True)
        - xhat * jnp.mean(dxh * xhat, axis=-1, keepdims=True)
    )
    return dz, jnp.sum(dy * xhat, axis=0, keepdims=True), jnp.sum(dy, axis=0, keepdims=True)


def tiles(count, tile, body):
    def step(i, carry):
        body(part(i, tile))
        return carry

    lax.fori_loop(0, count // tile, step, 0)


def total(refs, rows):
    acc = refs[0][rows, :].astype(F32)
    for ref in refs[1:]:
        acc = acc + ref[rows, :].astype(F32)
    return acc


def lanes_in_order(refs, r, width):
    near = [refs[0], refs[3], refs[2], refs[1]]
    joined = jnp.concatenate([ref[...].astype(F32) for ref in near], axis=1)
    return pltpu.roll(joined, r * width, 1)


def lanes_from_own(values, r, width):
    return pltpu.roll(values, ((Z - r) & 3) * width, 1)


def rows_in_order(full, refs, r):
    size = refs[0].shape[0]
    for k, ref in enumerate(refs):
        full[part((r - k) & 3, size), :] = ref[...]


def split(refs, *counts):
    found, at = [], 0
    for count in counts:
        found.append(refs[at] if count == 0 else list(refs[at : at + count]))
        at += max(count, 1)
    assert at == len(refs)
    return found


def co_fwd(dims, *refs):
    rank, tin, vin, kt, kv, wt, wv, pt, pv, xt, xv, bt, bv, qt, qv, ot, ov, st, sv = split(
        refs, 0, 4, 4, 0, 0, 0, 0, 0, 0, 0, 0, 0, 0, 0, 0, 0, 0, 4, 4
    )
    samples, text, regions, nt, nv = dims
    r = rank[0]
    width_t, width_v = tin[0].shape[1], vin[0].shape[1]
    ct, cv = bt.shape[0], bv.shape[0]
    xt[...] = lanes_in_order(tin, r, width_t).astype(BF)
    for k, ref in enumerate(vin):
        xv[:, part((r - k) & 3, width_v)] = ref[...]
    bt[...] = xt[part(r, ct), :]
    bv[...] = xv[part(r, cv), :]
    for i in range(3):
        qt[i] = dot(xt[...], wt[i]).astype(BF)

    def project(rows):
        for i in range(3):
            qv[i, rows, :] = dot(xv[rows, :], wv[i]).astype(BF)

    tiles(xv.shape[0], cv, project)
    scale = CO_HEAD ** (-0.5)
    rid_t, rid_v = row_ids(nt, text, samples), row_ids(nv, regions, samples)
    for m in range(2):
        rt, rv = slice(m * nt, (m + 1) * nt), slice(m * nv, (m + 1) * nv)
        same_tv = rid_t == kv[m : m + 1, :]
        same_vt = rid_v == kt[m : m + 1, :]
        for h in range(qt.shape[2] // CO_HEAD):
            c = slice(h * CO_HEAD, (h + 1) * CO_HEAD)
            ot[rt, c] = head_fwd(qt[0, rt, c], qv[1, rv, c], qv[2, rv, c], same_tv, scale)
            ov[rv, c] = head_fwd(qv[0, rv, c], qt[1, rt, c], qt[2, rt, c], same_vt, scale)
    for k in range(Z):
        c = (r + k) & 3
        st[k][...] = dot(ot[part(c, ct), :], pt[...]).astype(BF)
        sv[k][...] = dot(ov[part(c, cv), :], pv[...]).astype(BF)


def co_bwd(dims, *refs):
    (rank, dt, dv, kt, kv, qt, qv, wt, wv, pt, pv, gt, gv,
     zt, zv, dqt, dqv, st, sv, dot_s, dov_s, acc_t, acc_v) = split(
        refs, 0, 4, 4, 0, 0, 0, 0, 0, 0, 0, 0, 0, 0, 0, 0, 0, 0, 4, 4, 0, 0, 0, 0
    )
    samples, text, regions, nt, nv = dims
    r = rank[0]
    ct, cv = dt[0].shape[0], dv[0].shape[0]
    rows_in_order(zt, dt, r)
    rows_in_order(zv, dv, r)
    dot_s[...] = dot_nt(zt[...], pt[...]).astype(BF)

    def back_out(rows):
        dov_s[rows, :] = dot_nt(zv[rows, :], pv[...]).astype(BF)

    tiles(zv.shape[0], cv, back_out)
    scale = CO_HEAD ** (-0.5)
    rid_t, rid_v = row_ids(nt, text, samples), row_ids(nv, regions, samples)
    for m in range(2):
        rt, rv = slice(m * nt, (m + 1) * nt), slice(m * nv, (m + 1) * nv)
        same_tv = rid_t == kv[m : m + 1, :]
        same_vt = rid_v == kt[m : m + 1, :]
        for h in range(qt.shape[2] // CO_HEAD):
            c = slice(h * CO_HEAD, (h + 1) * CO_HEAD)
            a, b, d = head_bwd(
                qt[0, rt, c], qv[1, rv, c], qv[2, rv, c], same_tv, scale, dot_s[rt, c]
            )
            dqt[0, rt, c], dqv[1, rv, c], dqv[2, rv, c] = a, b, d
            a, b, d = head_bwd(
                qv[0, rv, c], qt[1, rt, c], qt[2, rt, c], same_vt, scale, dov_s[rv, c]
            )
            dqv[0, rv, c], dqt[1, rt, c], dqt[2, rt, c] = a, b, d
    width_t, width_v = st[0].shape[1], sv[0].shape[1]
    own_t = lanes_from_own(gt[...], r, width_t)
    for k in range(Z):
        c = (r + k) & 3
        acc_t[...] = sum(dot_nt(dqt[i], wt[i, part(c, width_t), :]) for i in range(3))
        acc_t[part(r, ct), :] += own_t[:, k * width_t : (k + 1) * width_t]
        st[k][...] = acc_t[...].astype(BF)

        def back_in(rows):
            acc_v[rows, :] = sum(
                dot_nt(dqv[i, rows, :], wv[i, part(c, width_v), :]) for i in range(3)
            )

        tiles(acc_v.shape[0], cv, back_in)
        acc_v[part(r, cv), :] += gv[:, part(c, width_v)]
        sv[k][...] = acc_v[...].astype(BF)


def self_fwd(dims, *refs):
    rank, xin, kid, w, po, x, q, o, s = split(refs, 0, 4, 0, 0, 0, 0, 0, 0, 4)
    samples, step, n, head = dims
    r = rank[0]
    size = xin[0].shape[0]
    rows_in_order(x, xin, r)

    def project(rows):
        for i in range(3):
            q[i, rows, :] = dot(x[rows, :], w[i]).astype(BF)

    tiles(x.shape[0], size, project)
    rid = row_ids(n, step, samples)
    for m in range(2):
        rm = slice(m * n, (m + 1) * n)
        same = rid == kid[m : m + 1, :]
        for h in range(q.shape[2] // head):
            c = slice(h * head, (h + 1) * head)
            o[rm, c] = head_fwd(q[0, rm, c], q[1, rm, c], q[2, rm, c], same, head ** (-0.5))
    for k in range(Z):
        s[k][...] = dot(o[part((r + k) & 3, size), :], po[...]).astype(BF)


def self_bwd(dims, *refs):
    rank, din, kid, q, w, po, z, dq, s, do = split(refs, 0, 4, 0, 0, 0, 0, 0, 0, 4, 0)
    samples, step, n, head = dims
    r = rank[0]
    size = din[0].shape[0]
    rows_in_order(z, din, r)

    def back_out(rows):
        do[rows, :] = dot_nt(z[rows, :], po[...]).astype(BF)

    tiles(z.shape[0], size, back_out)
    rid = row_ids(n, step, samples)
    for m in range(2):
        rm = slice(m * n, (m + 1) * n)
        same = rid == kid[m : m + 1, :]
        for h in range(q.shape[2] // head):
            c = slice(h * head, (h + 1) * head)
            a, b, d = head_bwd(
                q[0, rm, c], q[1, rm, c], q[2, rm, c], same, head ** (-0.5), do[rm, c]
            )
            dq[0, rm, c], dq[1, rm, c], dq[2, rm, c] = a, b, d
    for k in range(Z):
        rows = part((r + k) & 3, size)
        s[k][...] = sum(dot_nt(dq[i, rows, :], w[i]) for i in range(3)).astype(BF)


def text_norm(position, *refs):
    rank, s, base, gains, shifts, z, y, yb = split(refs, 0, 4, 0, 0, 0, 0, 0, 0)
    g, b = gains[position : position + 1, :], shifts[position : position + 1, :]

    def step(rows):
        zz = base[rows, :].astype(F32) + total(s, rows)
        z[rows, :] = zz
        yy = normalise(zz)[0] * g + b
        y[rows, :] = yy
        yb[rows, :] = yy.astype(BF)

    tiles(z.shape[0], 32, step)


def text_norm_back(position, *refs):
    rank, s, base, z, gains, dz, dzb, stat = split(refs, 0, 4, 0, 0, 0, 0, 0, 0)
    g = gains[position : position + 1, :]
    stat[...] = jnp.zeros_like(stat)

    def step(rows):
        d, dg, ds = norm_back(z[rows, :], g, base[rows, :] + total(s, rows))
        dz[rows, :] = d
        dzb[rows, :] = d.astype(BF)
        stat[0:1, :] += dg
        stat[1:2, :] += ds

    tiles(z.shape[0], 32, step)


def text_turn(position, *refs):
    rank, s, base, cot, gains, shifts, out, dz, dzb, stat = split(
        refs, 0, 4, 0, 4, 0, 0, 4, 0, 0, 0
    )
    r = rank[0]
    g, b = gains[position : position + 1, :], shifts[position : position + 1, :]
    width = cot[0].shape[1]
    dy = lanes_in_order(cot, r, width)
    z = base[...] + total(s, slice(None))
    y = lanes_from_own(normalise(z)[0] * g + b, r, width)
    for k in range(Z):
        out[k][...] = y[:, k * width : (k + 1) * width].astype(BF)
    d, dg, ds = norm_back(z, g, dy)
    dz[...] = d
    dzb[...] = d.astype(BF)
    stat[0:1, :] = dg
    stat[1:2, :] = ds


def text_ffn(*refs):
    rank, xin, up, down, x, u, g, s = split(refs, 0, 4, 0, 0, 0, 0, 0, 4)
    r = rank[0]
    size = xin[0].shape[0]
    rows_in_order(x, xin, r)

    def hidden(rows):
        uu = dot(x[rows, :], up[...])
        u[rows, :] = uu
        g[rows, :] = gelu(uu).astype(BF)

    tiles(x.shape[0], size, hidden)
    for k in range(Z):
        s[k][...] = dot(g[part((r + k) & 3, size), :], down[...]).astype(BF)


def text_ffn_back(*refs):
    rank, din, up, down, u, z, du, s = split(refs, 0, 4, 0, 0, 0, 0, 0, 4)
    r = rank[0]
    size = din[0].shape[0]
    rows_in_order(z, din, r)

    def hidden(rows):
        du[rows, :] = (dot_nt(z[rows, :], down[...]) * gelu_slope(u[rows, :])).astype(BF)

    tiles(z.shape[0], size, hidden)
    for k in range(Z):
        s[k][...] = dot_nt(du[part((r + k) & 3, size), :], up[...]).astype(BF)


def image_hidden(a, w, u, g):
    width = w.shape[2]
    depth = w.shape[1] // Z
    for c in range(Z):
        cols = slice(c * width, (c + 1) * width)
        uu = dot(a[...], w[0, c * depth : (c + 1) * depth, :])
        u[:, cols] = uu
        g[:, cols] = gelu(uu).astype(BF)


def image_down(af, g, w, z):
    width = w.shape[2]
    depth = w.shape[1] // Z
    for n in range(Z):
        out = slice(n * width, (n + 1) * width)
        acc = af[:, out]
        for c in range(Z):
            cols = slice(c * width, (c + 1) * width)
            rows = slice(c * depth + n * width, c * depth + (n + 1) * width)
            acc = acc + dot_nt(g[:, cols], w[1, rows, :])
        z[:, out] = acc


def image_hidden_back(dzb, w, u, du):
    width = w.shape[2]
    depth = w.shape[1] // Z
    for c in range(Z):
        cols = slice(c * width, (c + 1) * width)
        dg = dot(dzb[...], w[1, c * depth : (c + 1) * depth, :])
        du[:, cols] = (dg * gelu_slope(u[:, cols])).astype(BF)


def image_up_back(dz, du, w, da):
    width = w.shape[2]
    depth = w.shape[1] // Z
    for n in range(Z):
        out = slice(n * width, (n + 1) * width)
        acc = dz[:, out]
        for c in range(Z):
            cols = slice(c * width, (c + 1) * width)
            rows = slice(c * depth + n * width, c * depth + (n + 1) * width)
            acc = acc + dot_nt(du[:, cols], w[0, rows, :])
        da[:, out] = acc


def image_mid(position, *refs):
    rank, s, base, w, gains, shifts, z0, a, u, g, z1, y, yb, af = split(
        refs, 0, 4, 0, 0, 0, 0, 0, 0, 0, 0, 0, 0, 0, 0
    )
    g0, b0 = gains[position : position + 1, :], shifts[position : position + 1, :]
    g1, b1 = gains[position + 1 : position + 2, :], shifts[position + 1 : position + 2, :]

    def first(rows):
        zz = base[rows, :].astype(F32) + total(s, rows)
        z0[rows, :] = zz
        aa = normalise(zz)[0] * g0 + b0
        af[rows, :] = aa
        a[rows, :] = aa.astype(BF)

    tiles(z0.shape[0], 32, first)
    image_hidden(a, w, u, g)
    image_down(af, g, w, z1)

    def second(rows):
        yy = normalise(z1[rows, :])[0] * g1 + b1
        y[rows, :] = yy
        yb[rows, :] = yy.astype(BF)

    tiles(z0.shape[0], 32, second)


def image_mid_back(position, *refs):
    rank, s, base, z1, z0, u, w, gains, d1b, du, d0, d0b, stat, d1, da = split(
        refs, 0, 4, 0, 0, 0, 0, 0, 0, 0, 0, 0, 0, 0, 0, 0
    )
    g0 = gains[position : position + 1, :]
    g1 = gains[position + 1 : position + 2, :]
    stat[...] = jnp.zeros_like(stat)

    def first(rows):
        d, dg, ds = norm_back(z1[rows, :], g1, base[rows, :] + total(s, rows))
        d1[rows, :] = d
        d1b[rows, :] = d.astype(BF)
        stat[2:3, :] += dg
        stat[3:4, :] += ds

    tiles(z0.shape[0], 32, first)
    image_hidden_back(d1b, w, u, du)
    image_up_back(d1, du, w, da)

    def second(rows):
        d, dg, ds = norm_back(z0[rows, :], g0, da[rows, :])
        d0[rows, :] = d
        d0b[rows, :] = d.astype(BF)
        stat[0:1, :] += dg
        stat[1:2, :] += ds

    tiles(z0.shape[0], 32, second)


def image_turn(position, *refs):
    (rank, s, base, cot, w, gains, shifts, out, a, g, d1b, du, d0, d0b, stat,
     z0, af, u, z1, y, dy, d1, da) = split(
        refs, 0, 4, 0, 4, 0, 0, 0, 4, 0, 0, 0, 0, 0, 0, 0, 0, 0, 0, 0, 0, 0, 0, 0
    )
    r = rank[0]
    g0, b0 = gains[position : position + 1, :], shifts[position : position + 1, :]
    g1, b1 = gains[position + 1 : position + 2, :], shifts[position + 1 : position + 2, :]
    width = cot[0].shape[1]
    stat[...] = jnp.zeros_like(stat)
    for k, ref in enumerate(cot):
        dy[:, part((r - k) & 3, width)] = ref[...].astype(F32)

    def first(rows):
        zz = base[rows, :] + total(s, rows)
        z0[rows, :] = zz
        aa = normalise(zz)[0] * g0 + b0
        af[rows, :] = aa
        a[rows, :] = aa.astype(BF)

    tiles(z0.shape[0], 32, first)
    image_hidden(a, w, u, g)
    image_down(af, g, w, z1)

    def second(rows):
        zz = z1[rows, :]
        y[rows, :] = normalise(zz)[0] * g1 + b1
        d, dg, ds = norm_back(zz, g1, dy[rows, :])
        d1[rows, :] = d
        d1b[rows, :] = d.astype(BF)
        stat[2:3, :] += dg
        stat[3:4, :] += ds

    tiles(z0.shape[0], 32, second)
    for k in range(Z):
        out[k][...] = y[:, part((r + k) & 3, width)].astype(BF)
    image_hidden_back(d1b, w, u, du)
    image_up_back(d1, du, w, da)

    def third(rows):
        d, dg, ds = norm_back(z0[rows, :], g0, da[rows, :])
        d0[rows, :] = d
        d0b[rows, :] = d.astype(BF)
        stat[0:1, :] += dg
        stat[1:2, :] += ds

    tiles(z0.shape[0], 32, third)


def image_ffn_weights(*refs):
    rank, a, du, g, dz, out = split(refs, 0, 0, 0, 0, 0, 4)
    r = rank[0]
    width = out[0].shape[2]
    for k in range(Z):
        cols = part((r + k) & 3, width)
        right_up, right_down = du[:, cols], g[:, cols]
        for n in range(Z):
            rows = slice(n * width, (n + 1) * width)
            out[k][0, rows, :] = dot_tn(a[:, rows], right_up).astype(BF)
            out[k][1, rows, :] = dot_tn(dz[:, rows], right_down).astype(BF)


def run(name, body, outs, args, scratch=()):
    flat = []
    for arg in args:
        flat.extend(arg if isinstance(arg, (list, tuple)) else [arg])
    vmem = pl.BlockSpec(memory_space=pltpu.VMEM)
    shapes, groups = [], []
    for shape, dtype, count in outs:
        groups.append(count)
        shapes.extend([jax.ShapeDtypeStruct(shape, dtype)] * max(count, 1))
    results = pl.pallas_call(
        body,
        out_shape=shapes,
        in_specs=[pl.BlockSpec(memory_space=pltpu.SMEM)] + [vmem] * (len(flat) - 1),
        out_specs=[vmem] * len(shapes),
        scratch_shapes=[pltpu.VMEM(shape, dtype) for shape, dtype in scratch],
        compiler_params=pltpu.CompilerParams(vmem_limit_bytes=48 * 1024 * 1024),
        name=name,
    )(*flat)
    return split(list(results), *groups)


def shift(values, k):
    return lax.ppermute(values, "tensor", [(i, (i + k) % Z) for i in range(Z)])


def spread(own):
    return [own] + [shift(own, k) for k in (1, 2, 3)]


def swap(chunks):
    return [chunks[0]] + [shift(chunks[k], k) for k in (1, 2, 3)]


def pad_rows(values, n):
    micro, samples, rows, width = values.shape
    flat = values.reshape(micro, samples * rows, width)
    flat = jnp.pad(flat, ((0, 0), (0, n - samples * rows), (0, 0)))
    return flat.reshape(micro * n, width)


def unpad_rows(values, shape, n):
    micro, samples, rows, width = shape
    return values.reshape(micro, n, width)[:, : samples * rows].reshape(shape)


def key_ids(lengths, rows, n):
    micro, samples = lengths.shape
    live = jnp.arange(rows, dtype=jnp.int32)[None, None, :] < lengths[:, :, None]
    ids = jnp.where(live, jnp.arange(samples, dtype=jnp.int32)[None, :, None], -1)
    ids = ids.reshape(micro, samples * rows)
    return jnp.pad(ids, ((0, 0), (0, n - samples * rows)), constant_values=-1)


def row_chunks(values, rank):
    size = values.shape[0] // Z
    return [lax.dynamic_slice_in_dim(values, ((rank + k) & 3) * size, size, 0) for k in range(Z)]


def from_row_chunks(chunks, rank, shape, n):
    joined = jnp.concatenate(
        [chunks[0], chunks[3], chunks[2], chunks[1]] * 2, axis=0
    )
    size = chunks[0].shape[0]
    ordered = lax.dynamic_slice_in_dim(joined, ((Z - rank) & 3) * size, size * Z, 0)
    return unpad_rows(ordered, shape, n).astype(F32)


def weight_grad(left, right):
    return dot_tn(left, right).astype(BF)


def shards(
    text_in, image_in, caption_len, region_count, text_cot, image_cot,
    co_text_qkv, co_image_qkv, co_text_out, co_image_out,
    co_text_up, co_text_down, co_image_up, co_image_down,
    self_text_qkv, self_image_qkv, self_text_out, self_image_out,
    text_up, text_down, image_up, image_down,
    text_gains, text_shifts, image_gains, image_shifts,
):
    rank = lax.axis_index("tensor")
    place = lax.axis_index("dp")
    n_dp = lax.axis_size("dp")
    rk = rank.reshape(1).astype(jnp.int32)
    micro, samples, text, wt = text_in.shape
    regions, wv = image_in.shape[2:]
    dt, dv = wt * Z, wv * Z
    nt = -(-samples * text // 64) * 64
    nv = -(-samples * regions // 64) * 64
    rt, rv = micro * nt, micro * nv
    ct, cv = rt // Z, rv // Z
    co_w = co_text_qkv.shape[2]
    st_w = self_text_qkv.shape[2]
    si_w = self_image_qkv.shape[2]
    ft = co_text_up.shape[1]

    def gathered(up, down):
        cut = up.shape[0] // n_dp
        mine = lax.dynamic_slice_in_dim(up, place * cut, cut, 0)
        other = lax.dynamic_slice_in_dim(down, place * cut, cut, 1).T
        return lax.all_gather(jnp.stack([mine, other]), ("tensor", "dp"), axis=1, tiled=True)

    tin = spread(pad_rows(text_in, nt))
    vin = spread(pad_rows(image_in, nv))
    w_mid = gathered(co_image_up, co_image_down)
    w_end = gathered(image_up, image_down)
    tcot = swap(row_chunks(pad_rows(text_cot, nt), rank))
    vcot = swap(row_chunks(pad_rows(image_cot, nv), rank))
    kt = key_ids(caption_len, text, nt)
    kv = key_ids(region_count, regions, nv)

    co_dims = (samples, text, regions, nt, nv)
    text_dims = (samples, text, nt, TEXT_HEAD)
    image_dims = (samples, regions, nv, IMAGE_HEAD)

    xt0, xv0, bt, bv, qt0, qv0, ot0, ov0, st, sv = run(
        "co_fwd", functools.partial(co_fwd, co_dims),
        [((rt, dt), BF, 0), ((rv, dv), BF, 0), ((ct, dt), BF, 0), ((cv, dv), BF, 0),
         ((3, rt, co_w), BF, 0), ((3, rv, co_w), BF, 0), ((rt, co_w), BF, 0), ((rv, co_w), BF, 0),
         ((ct, dt), BF, Z), ((cv, dv), BF, Z)],
        [rk, tin, vin, kt, kv, co_text_qkv, co_image_qkv, co_text_out, co_image_out],
    )
    norm_t = [((ct, dt), F32, 0), ((ct, dt), F32, 0), ((ct, dt), BF, 0)]
    zt0, at, atb = run(
        "text_norm0", functools.partial(text_norm, 0), norm_t,
        [rk, swap(st), bt, text_gains, text_shifts],
    )
    ffn_t = [((rt, dt), BF, 0), ((rt, ft), F32, 0), ((rt, ft), BF, 0), ((ct, dt), BF, Z)]
    xt1, ut1, gt1, st = run(
        "text_ffn1", text_ffn, ffn_t, [rk, spread(atb), co_text_up, co_text_down]
    )
    zv0, av, uv1, gv1, zv1, bv, bvb = run(
        "image_mid", functools.partial(image_mid, 0),
        [((cv, dv), F32, 0), ((cv, dv), BF, 0), ((cv, dv), F32, 0), ((cv, dv), BF, 0),
         ((cv, dv), F32, 0), ((cv, dv), F32, 0), ((cv, dv), BF, 0)],
        [rk, swap(sv), bv, w_mid, image_gains, image_shifts],
        [((cv, dv), F32)],
    )
    zt1, bt, btb = run(
        "text_norm1", functools.partial(text_norm, 1), norm_t,
        [rk, swap(st), at, text_gains, text_shifts],
    )
    xv2, qv2, ov2, sv = run(
        "image_self", functools.partial(self_fwd, image_dims),
        [((rv, dv), BF, 0), ((3, rv, si_w), BF, 0), ((rv, si_w), BF, 0), ((cv, dv), BF, Z)],
        [rk, spread(bvb), kv, self_image_qkv, self_image_out],
    )
    xt2, qt2, ot2, st = run(
        "text_self", functools.partial(self_fwd, text_dims),
        [((rt, dt), BF, 0), ((3, rt, st_w), BF, 0), ((rt, st_w), BF, 0), ((ct, dt), BF, Z)],
        [rk, spread(btb), kt, self_text_qkv, self_text_out],
    )
    out_v, av3, gv3, dv3, duv3, gv, gvb, stat_v1 = run(
        "image_turn", functools.partial(image_turn, 2),
        [((cv, wv), BF, Z), ((cv, dv), BF, 0), ((cv, dv), BF, 0), ((cv, dv), BF, 0),
         ((cv, dv), BF, 0), ((cv, dv), F32, 0), ((cv, dv), BF, 0), ((4, dv), F32, 0)],
        [rk, swap(sv), bv, vcot, w_end, image_gains, image_shifts],
        [((cv, dv), F32)] * 8,
    )
    zt2, ctf, ctb = run(
        "text_norm2", functools.partial(text_norm, 2), norm_t,
        [rk, swap(st), bt, text_gains, text_shifts],
    )
    xt3, ut3, gt3, st = run("text_ffn3", text_ffn, ffn_t, [rk, spread(ctb), text_up, text_down])
    out_t, gt, gtb, stat_t3 = run(
        "text_turn", functools.partial(text_turn, 3),
        [((ct, wt), BF, Z), ((ct, dt), F32, 0), ((ct, dt), BF, 0), ((2, dt), F32, 0)],
        [rk, swap(st), ctf, tcot, text_gains, text_shifts],
    )
    text_out = from_row_chunks(swap(out_t), rank, text_in.shape, nt)
    image_out = from_row_chunks(swap(out_v), rank, image_in.shape, nv)

    back_ffn = [((rt, dt), BF, 0), ((rt, ft), BF, 0), ((ct, dt), BF, Z)]
    back_norm = [((ct, dt), F32, 0), ((ct, dt), BF, 0), ((2, dt), F32, 0)]
    dt3, dut3, st = run(
        "text_ffn3_back", text_ffn_back, back_ffn, [rk, spread(gtb), text_up, text_down, ut3]
    )
    dv2, dqv2, sv = run(
        "image_self_back", functools.partial(self_bwd, image_dims),
        [((rv, dv), BF, 0), ((3, rv, si_w), BF, 0), ((cv, dv), BF, Z)],
        [rk, spread(gvb), kv, qv2, self_image_qkv, self_image_out],
        [((rv, si_w), BF)],
    )
    gt, gtb, stat_t2 = run(
        "text_norm2_back", functools.partial(text_norm_back, 2), back_norm,
        [rk, swap(st), gt, zt2, text_gains],
    )
    dt2, dqt2, st = run(
        "text_self_back", functools.partial(self_bwd, text_dims),
        [((rt, dt), BF, 0), ((3, rt, st_w), BF, 0), ((ct, dt), BF, Z)],
        [rk, spread(gtb), kt, qt2, self_text_qkv, self_text_out],
        [((rt, st_w), BF)],
    )
    dv1, duv1, gv, gvb, stat_v0 = run(
        "image_mid_back", functools.partial(image_mid_back, 0),
        [((cv, dv), BF, 0), ((cv, dv), BF, 0), ((cv, dv), F32, 0), ((cv, dv), BF, 0),
         ((4, dv), F32, 0)],
        [rk, swap(sv), gv, zv1, zv0, uv1, w_mid, image_gains],
        [((cv, dv), F32)] * 2,
    )
    gt, gtb, stat_t1 = run(
        "text_norm1_back", functools.partial(text_norm_back, 1), back_norm,
        [rk, swap(st), gt, zt1, text_gains],
    )
    dt1, dut1, st = run(
        "text_ffn1_back", text_ffn_back, back_ffn, [rk, spread(gtb), co_text_up, co_text_down, ut1]
    )
    gt, gtb, stat_t0 = run(
        "text_norm0_back", functools.partial(text_norm_back, 0), back_norm,
        [rk, swap(st), gt, zt0, text_gains],
    )
    dt0, dv0, dqt0, dqv0, st, sv = run(
        "co_back", functools.partial(co_bwd, co_dims),
        [((rt, dt), BF, 0), ((rv, dv), BF, 0), ((3, rt, co_w), BF, 0), ((3, rv, co_w), BF, 0),
         ((rt, wt), BF, Z), ((rv, wv), BF, Z)],
        [rk, spread(gtb), spread(gvb), kt, kv, qt0, qv0, co_text_qkv, co_image_qkv,
         co_text_out, co_image_out, gt, gv],
        [((rt, co_w), BF), ((rv, co_w), BF), ((rt, wt), F32), ((rv, wv), F32)],
    )
    text_grad = sum(piece.astype(F32) for piece in swap(st))
    image_grad = sum(piece.astype(F32) for piece in swap(sv))
    text_grad = unpad_rows(text_grad, text_in.shape, nt)
    image_grad = unpad_rows(image_grad, image_in.shape, nv)

    def image_ffn_grad(name, a, du, g, dz):
        (pieces,) = run(name, image_ffn_weights, [((2, dv, wv), BF, Z)], [rk, a, du, g, dz])
        return sum(piece.astype(F32) for piece in swap(pieces)).astype(BF)

    end_ffn = image_ffn_grad("image_ffn3_weights", av3, duv3, gv3, dv3)
    mid_ffn = image_ffn_grad("image_ffn1_weights", av, duv1, gv1, dv1)
    stats = jnp.concatenate(
        [
            jnp.pad(
                jnp.concatenate([stat_t0, stat_t1, stat_t2, stat_t3], axis=0),
                ((0, 0), (0, dv - dt)),
            ),
            stat_v0,
            stat_v1,
        ],
        axis=0,
    )
    stats = sum(spread(stats)).astype(BF)
    parts = [
        weight_grad(xt0, dqt0[0]), weight_grad(xt0, dqt0[1]), weight_grad(xt0, dqt0[2]),
        weight_grad(xv0, dqv0[0]), weight_grad(xv0, dqv0[1]), weight_grad(xv0, dqv0[2]),
        weight_grad(ot0, dt0), weight_grad(ov0, dv0),
        weight_grad(xt1, dut1), weight_grad(gt1, dt1),
        mid_ffn,
        weight_grad(xt2, dqt2[0]), weight_grad(xt2, dqt2[1]), weight_grad(xt2, dqt2[2]),
        weight_grad(xv2, dqv2[0]), weight_grad(xv2, dqv2[1]), weight_grad(xv2, dqv2[2]),
        weight_grad(ot2, dt2), weight_grad(ov2, dv2),
        weight_grad(xt3, dut3), weight_grad(gt3, dt3),
        end_ffn,
        stats,
    ]
    parts = [member.astype(F32) for member in lax.psum(tuple(parts), "dp")]
    mid_ffn, end_ffn, stats = parts[10], parts[21], parts[22]
    text_stats = stats[:8, :dt].reshape(4, 2, dt)
    image_stats = stats[8:16].reshape(4, 2, dv)
    return (
        text_out, image_out, text_grad, image_grad,
        jnp.stack(parts[0:3]), jnp.stack(parts[3:6]), parts[6], parts[7],
        parts[8], parts[9], mid_ffn[0], mid_ffn[1].T,
        jnp.stack(parts[11:14]), jnp.stack(parts[14:17]), parts[17], parts[18],
        parts[19], parts[20], end_ffn[0], end_ffn[1].T,
        text_stats[:, 0], text_stats[:, 1], image_stats[:, 0], image_stats[:, 1],
    )


def solution(mesh):
    stream = P(None, "dp", None, "tensor")
    lengths = P(None, "dp")
    stacked = P(None, None, "tensor")
    rows = P("tensor", None)
    cols = P(None, "tensor")
    weights = (
        stacked, stacked, rows, rows, cols, rows, cols, rows,
        stacked, stacked, rows, rows, cols, rows, cols, rows,
        P(), P(), P(), P(),
    )
    in_specs = (stream, stream, lengths, lengths, stream, stream) + weights
    out_specs = (stream,) * 4 + weights
    return jax.shard_map(shards, mesh=mesh, in_specs=in_specs, out_specs=out_specs, check_vma=False)
```

time: 1310 us -> 656 us (0.50)
  waiting for transfers between devices: 642 us -> 159 us
  local copies, waits for them, and re-layouts: 204 us -> 64.2 us
  matrix products: 162 us -> 27.3 us
  starting transfers between devices: 2.53 us -> 133 us
  Pallas kernels: 0 us -> 96.6 us
  other arithmetic: 97.2 us -> 25.2 us
  blocking collectives: 170 us -> 125 us
    psum x8 -> x1, waiting for transfers between devices: 628 us -> 0.01 us  [shards(): parts = [member.astype(F32) for member in lax.psum(tuple(parts), 'dp')]]
    ppermute x0 -> x93, waiting for transfers between devices: none -> 159 us  [shift(): return lax.ppermute(values, 'tensor', [(i, (i + k) % Z) for i in range(Z)])]
    dot_general x144 -> x20, matrix products: 162 us -> 27.3 us  [dot_tn(): lax.dot_general(a, b, (((0,), (0,)), ((), ())), preferred_element_type=F32)]
    ppermute x0 -> x93, starting transfers between devices: none -> 133 us  [shift(): return lax.ppermute(values, 'tensor', [(i, (i + k) % Z) for i in range(Z)])]
    pallas_call x0 -> x22, Pallas kernels: none -> 96.6 us  [run(): pl.pallas_call(body, out_shape=shapes, in_specs=[pl.BlockSpec(memory_spac...]
    reduce_sum x58 -> x0, other arithmetic: 58.1 us -> none  [the longest x18 33.4 us: normed(): return centre * lax.rsqrt(spread + norm_eps) * gain_vec + shift_vec]
    unnamed x1060 -> x393, local copies, waits for them, and re-layouts: 102 us -> 50.4 us
    all_gather x2 -> x0, blocking collectives: 40.5 us -> none  [the longest x1 21.4 us: shards(): lax.all_gather(text_cot, 'tensor', axis=3, tiled=True)]
  transfers between devices with their start and end apart: 14 -> 96, of which waited for: 9 -> 51; matrix products, arithmetic and copies ran while one was open for 10% -> 7% of each run, Pallas kernels for 0% -> 15%
where the time goes in v1:
time: 656 us; the launch traced here: 646 us
  waiting for transfers between devices  159 us (24%)
  starting transfers between devices  133 us (20%)
  blocking collectives  125 us (19%)
  Pallas kernels  96.6 us (15%)
  local copies, waits for them, and re-layouts  64.2 us (10%)
  matrix products  27.3 us (4%)
  other arithmetic  25.2 us (4%)
  between operations  15.5 us (2%)
    ppermute x93, waiting for transfers between devices, shift(): return lax.ppermute(values, 'tensor', [(i, (i + k) % Z) for i in range(Z)])  159 us
    ppermute x93, starting transfers between devices, shift(): return lax.ppermute(values, 'tensor', [(i, (i + k) % Z) for i in range(Z)])  133 us
    psum x1, blocking collectives, shards(): parts = [member.astype(F32) for member in lax.psum(tuple(parts), 'dp')]  125 us
    pallas_call x22, Pallas kernels, run(): pl.pallas_call(body, out_shape=shapes, in_specs=[pl.BlockSpec(memory_spac...  96.6 us
    unnamed x393, local copies, waits for them, and re-layouts  50.4 us
    dot_general x20, matrix products, dot_tn(): lax.dot_general(a, b, (((0,), (0,)), ((), ())), preferred_element_type=F32)  27.3 us
  transfers between devices with their start and end apart: 96, of which 51 were waited for; matrix products, arithmetic and copies ran while one was open for 7% of the time, Pallas kernels for 15%

profile of v1, /device:TPU:0, one launch (start us, length us, event | category | flops | bytes accessed | tf_op | source)
XLA Modules:
  0.0 646.5 jit_solution(15363348933808915918)
XLA Ops:
  15.3 3.6 collective-permute-start.1
  26.0 13.9 %collective-permute-done.2.refs_4_ = bf16[256,192]{1,0:T(8,128)(2,1)S(1)} collective-permute-done((bf16[256,192]{1,0:T(8,128)(2,1)S(1)}, bf16[256,192]{1,0:T(8,128)(2,1)S(1)}, u32[]{:S(2)}, u32[]{:S(2)}) %collective-permute-start.2) | collective-permute-done | bytes 98336 | tf_op jit(solution)/shard_map/ppermute | solution.py:529
  40.0 9.2 %co_fwd.1 = (bf16[256,768]{1,0:T(8,128)(2,1)S(1)}, bf16[640,1024]{1,0:T(8,128)(2,1)}, bf16[64,768]{1,0:T(8,128)(2,1)S(1)}, bf16[160,1024]{1,0:T(8,128)(2,1)S(1)}...) custom-call(s32[1]{0:T(128)} %bitcast.refs_0_, ...), custom_call_target="tpu_custom_call" | custom-call | tf_op jit(solution)/shard_map/co_fwd/pallas_call | solution.py:516
  53.8 2.8 collective-permute-start.7
  66.7 3.8 collective-permute-done.9.refs_2_
  89.5 2.8 collective-permute-start.16
  99.1 4.8 text_self.1
  105.6 3.1 collective-permute-start.19
  118.3 3.2 collective-permute-start.22
  126.5 3.4 text_ffn3.1
  131.5 3.3 collective-permute-start.25
  137.7 4.8 collective-permute-done.27.refs_7_
  147.6 4.5 collective-permute-start.49
  153.4 2.9 collective-permute-done.49.refs_3_
  157.0 4.2 text_ffn3_back.1
  177.6 5.5 collective-permute-done.54.refs_2_
  184.7 3.1 collective-permute-done.56.refs_4_
  187.8 5.3 text_self_back.1
  203.6 5.6 image_mid.1
  209.4 4.7 collective-permute-start.37
  217.2 3.1 collective-permute-start.59
  221.3 4.2 collective-permute-done.58.refs_3_
  229.0 6.4 image_self.1
  237.7 3.0 collective-permute-start.40
  247.6 2.9 collective-permute-done.61.refs_3_
  252.0 4.6 collective-permute-start.44
  257.7 4.0 text_ffn1_back.1
  273.3 9.2 %image_turn.1 = (bf16[160,256]{1,0:T(8,128)(2,1)S(1)}, bf16[160,256]{1,0:T(8,128)(2,1)S(1)}, bf16[160,256]{1,0:T(8,128)(2,1)S(1)}, bf16[160,256]{1,0:T(8,128)(2,...) custom-call(s32[1]{0:T(128)} %bitcast.refs_0_, ...), custom_call_target="tpu_custom_call" | custom-call | tf_op jit(solution)/shard_map/image_turn/pallas_call | solution.py:516
  292.7 4.3 collective-permute-done.65.refs_4_
  306.2 8.7 %image_self_back.1 = (bf16[640,1024]{1,0:T(8,128)(2,1)}, bf16[3,640,256]{2,1,0:T(8,128)(2,1)S(1)}, bf16[160,1024]{1,0:T(8,128)(2,1)S(1)}, bf16[160,1024]{1,0:T(8...) custom-call(s32[1]{0:T(128)} %bitcast.refs_0_, ...), custom_call_target="tpu_custom_call" | custom-call | tf_op jit(solution)/shard_map/image_self_back/pallas_call | solution.py:516
  321.6 12.0 %collective-permute-done.72.refs_2_ = bf16[160,1024]{1,0:T(8,128)(2,1)S(1)} collective-permute-done((bf16[160,1024]{1,0:T(8,128)(2,1)S(1)}, bf16[160,1024]{1,0:T(8,128)(2,1)S(1)}, u32[]{:S(2)}, u32[]{:S(2)}) %collective-permute-start.72) | collective-permute-done | bytes 327712 | tf_op jit(solution)/shard_map/ppermute | solution.py:529
  334.7 6.3 image_mid_back.1
  341.5 3.9 collective-permute-start.76
  353.6 16.3 %collective-permute-done.68.refs_4_ = bf16[64,768]{1,0:T(8,128)(2,1)S(1)} collective-permute-done((bf16[64,768]{1,0:T(8,128)(2,1)S(1)}, bf16[64,768]{1,0:T(8,128)(2,1)S(1)}, u32[]{:S(2)}, u32[]{:S(2)}) %collective-permute-start.68) | collective-permute-done | bytes 98336 | tf_op jit(solution)/shard_map/ppermute | solution.py:529
  371.0 3.6 collective-permute-start.87
  376.7 16.7 %co_back.1 = (bf16[256,768]{1,0:T(8,128)(2,1)S(1)}, bf16[640,1024]{1,0:T(8,128)(2,1)}, bf16[3,256,256]{2,1,0:T(8,128)(2,1)S(1)}, bf16[3,640,256]{2,1,0:T(8,128)(...) custom-call(s32[1]{0:T(128)} %bitcast.refs_0_, ...), custom_call_target="tpu_custom_call" | custom-call | tf_op jit(solution)/shard_map/co_back/pallas_call | solution.py:516
  393.5 3.0 fusion.2
  405.5 8.7 %collective-permute-done.87 = bf16[2,1024,256]{2,1,0:T(8,128)(2,1)} collective-permute-done((bf16[2,1024,256]{2,1,0:T(8,128)(2,1)S(1)}, bf16[2,1024,256]{2,1,0:T(8,128)(2,1)}, u32[]{:S(2)}, u32[]{:S(2)}) %collective-permute-start.87) | collective-permute-done | bytes 1048608 | tf_op jit(solution)/shard_map/ppermute | solution.py:529
  414.3 3.1 add_convert_fusion
  417.4 6.0 collective-permute-done.86
  423.3 2.9 collective-permute-done.85
  426.2 12.9 %collective-permute-done.84 = bf16[2,1024,256]{2,1,0:T(8,128)(2,1)S(1)} collective-permute-done((bf16[2,1024,256]{2,1,0:T(8,128)(2,1)S(1)}, bf16[2,1024,256]{2,1,0:T(8,128)(2,1)S(1)}, u32[]{:S(2)}, u32[]{:S(2)}) %collective-permute-start.84) | collective-permute-done | bytes 1048608 | tf_op jit(solution)/shard_map/ppermute | solution.py:529
  455.4 3.1 collective-permute-done.46
  466.6 125.5 %psum.183 = bf16[16,1024]{1,0:T(8,128)(2,1)S(1)} all-reduce(bf16[16,1024]{1,0:T(8,128)(2,1)S(1)} %add_convert_fusion.2), channel_id=1, replica_groups=mesh['tensor'=4,'dp'=32] {'dp'}, use_global_device_ids=true, to_apply=%region_22.23 | all-reduce | flops 16384 | bytes 65536 | tf_op jit(solution)/shard_map/psum | solution.py:761
  595.7 3.2 collective-permute-start.83
  605.6 4.4 collective-permute-done.83
  610.3 3.4 collective-permute-done.81
  636.5 3.2 maximum_convert_fusion
  (655 shorter events, 247.8 us)
Async XLA Ops:
  7.3 191.4 %all-gather.3.cloned.1.call-start = ((), (), s32[]{:S(2)}) async-start(), calls=%async_computation | async-start | bytes 4227072 | tf_op jit(solution)/shard_map/all_gather | solution.py:606
  9.8 257.9 %all-gather.5.cloned.1.call-start = ((), (), s32[]{:S(2)}) async-start(), calls=%async_computation.1 | async-start | bytes 4227072 | tf_op jit(solution)/shard_map/all_gather | solution.py:606
  12.2 603.0 %all-reduce.10.cloned.1.call-start = ((), (), s32[]{:S(2)}) async-start(), calls=%async_computation.2 | async-start | bytes 27525120 | tf_op jit(solution)/shard_map/psum | solution.py:761
  15.3 10.7 %collective-permute-start.1 = (bf16[256,192]{1,0:T(8,128)(2,1)S(1)}, bf16[256,192]{1,0:T(8,128)(2,1)S(1)}, u32[]{:S(2)}, u32[]{:S(2)}) collective-permute-start(bf16[256,192]{1,0:T(8,128)(2,1)S(1)} %bitcast.140), channel_id=1, source_target_pairs={{0,64},{32,96},{64,0},{96,32},{1,65},{33,97},{65,1},{97,33},{2,66}... | collective-permute-start | bytes 294920 | tf_op jit(solution)/shard_map/ppermute | solution.py:529
  18.9 21.0 %collective-permute-start.3 = (bf16[640,256]{1,0:T(8,128)(2,1)S(1)}, bf16[640,256]{1,0:T(8,128)(2,1)S(1)}, u32[]{:S(2)}, u32[]{:S(2)}) collective-permute-start(bf16[640,256]{1,0:T(8,128)(2,1)S(1)} %bitcast.135), channel_id=1, source_target_pairs={{0,32},{32,64},{64,96},{96,0},{1,33},{33,65},{65,97},{97,1},{2,34}... | collective-permute-start | bytes 983048 | tf_op jit(solution)/shard_map/ppermute | solution.py:529
  19.0 20.9 %collective-permute-start.4 = (bf16[640,256]{1,0:T(8,128)(2,1)S(1)}, bf16[640,256]{1,0:T(8,128)(2,1)S(1)}, u32[]{:S(2)}, u32[]{:S(2)}) collective-permute-start(bf16[640,256]{1,0:T(8,128)(2,1)S(1)} %bitcast.136), channel_id=1, source_target_pairs={{0,64},{32,96},{64,0},{96,32},{1,65},{33,97},{65,1},{97,33},{2,66}... | collective-permute-start | bytes 983048 | tf_op jit(solution)/shard_map/ppermute | solution.py:529
  21.5 18.4 %collective-permute-start.5 = (bf16[640,256]{1,0:T(8,128)(2,1)S(1)}, bf16[640,256]{1,0:T(8,128)(2,1)S(1)}, u32[]{:S(2)}, u32[]{:S(2)}) collective-permute-start(bf16[640,256]{1,0:T(8,128)(2,1)S(1)} %bitcast.137), channel_id=1, source_target_pairs={{0,96},{32,0},{64,32},{96,64},{1,97},{33,1},{65,33},{97,65},{2,98}... | collective-permute-start | bytes 983048 | tf_op jit(solution)/shard_map/ppermute | solution.py:529
  22.9 16.9 %collective-permute-start.2 = (bf16[256,192]{1,0:T(8,128)(2,1)S(1)}, bf16[256,192]{1,0:T(8,128)(2,1)S(1)}, u32[]{:S(2)}, u32[]{:S(2)}) collective-permute-start(bf16[256,192]{1,0:T(8,128)(2,1)S(1)} %bitcast.141), channel_id=1, source_target_pairs={{0,96},{32,0},{64,32},{96,64},{1,97},{33,1},{65,33},{97,65},{2,98}... | collective-permute-start | bytes 294920 | tf_op jit(solution)/shard_map/ppermute | solution.py:529
  131.4 15.5 %collective-permute-start.24 = (bf16[64,768]{1,0:T(8,128)(2,1)S(1)}, bf16[64,768]{1,0:T(8,128)(2,1)S(1)}, u32[]{:S(2)}, u32[]{:S(2)}) collective-permute-start(bf16[64,768]{1,0:T(8,128)(2,1)S(1)} %get-tuple-element.179), channel_id=1, source_target_pairs={{0,32},{32,64},{64,96},{96,0},{1,33},{33,65},{65,97},{97,1},{2,34}... | collective-permute-start | bytes 294920 | tf_op jit(solution)/shard_map/ppermute | solution.py:529
  131.5 15.4 %collective-permute-start.25 = (bf16[64,768]{1,0:T(8,128)(2,1)S(1)}, bf16[64,768]{1,0:T(8,128)(2,1)S(1)}, u32[]{:S(2)}, u32[]{:S(2)}) collective-permute-start(bf16[64,768]{1,0:T(8,128)(2,1)S(1)} %get-tuple-element.180), channel_id=1, source_target_pairs={{0,64},{32,96},{64,0},{96,32},{1,65},{33,97},{65,1},{97,33},{2,66}... | collective-permute-start | bytes 294920 | tf_op jit(solution)/shard_map/ppermute | solution.py:529
  134.8 12.1 %collective-permute-start.26 = (bf16[64,768]{1,0:T(8,128)(2,1)S(1)}, bf16[64,768]{1,0:T(8,128)(2,1)S(1)}, u32[]{:S(2)}, u32[]{:S(2)}) collective-permute-start(bf16[64,768]{1,0:T(8,128)(2,1)S(1)} %get-tuple-element.181), channel_id=1, source_target_pairs={{0,96},{32,0},{64,32},{96,64},{1,97},{33,1},{65,33},{97,65},{2,98}... | collective-permute-start | bytes 294920 | tf_op jit(solution)/shard_map/ppermute | solution.py:529
  169.0 27.6 %collective-permute-start.33 = (bf16[160,1024]{1,0:T(8,128)(2,1)}, bf16[160,1024]{1,0:T(8,128)(2,1)S(1)}, u32[]{:S(2)}, u32[]{:S(2)}) collective-permute-start(bf16[160,1024]{1,0:T(8,128)(2,1)} %copy-done.128), channel_id=1, source_target_pairs={{0,32},{32,64},{64,96},{96,0},{1,33},{33,65},{65,97},{97,1},{2,34}... | collective-permute-start | bytes 983048 | tf_op jit(solution)/shard_map/ppermute | solution.py:529
  169.0 28.2 %collective-permute-start.34 = (bf16[160,1024]{1,0:T(8,128)(2,1)}, bf16[160,1024]{1,0:T(8,128)(2,1)S(1)}, u32[]{:S(2)}, u32[]{:S(2)}) collective-permute-start(bf16[160,1024]{1,0:T(8,128)(2,1)} %copy-done.127), channel_id=1, source_target_pairs={{0,64},{32,96},{64,0},{96,32},{1,65},{33,97},{65,1},{97,33},{2,66}... | collective-permute-start | bytes 983048 | tf_op jit(solution)/shard_map/ppermute | solution.py:529
  172.1 25.9 %collective-permute-start.35 = (bf16[160,1024]{1,0:T(8,128)(2,1)}, bf16[160,1024]{1,0:T(8,128)(2,1)S(1)}, u32[]{:S(2)}, u32[]{:S(2)}) collective-permute-start(bf16[160,1024]{1,0:T(8,128)(2,1)} %copy-done.126), channel_id=1, source_target_pairs={{0,96},{32,0},{64,32},{96,64},{1,97},{33,1},{65,33},{97,65},{2,98}... | collective-permute-start | bytes 983048 | tf_op jit(solution)/shard_map/ppermute | solution.py:529
  196.5 20.6 %collective-permute-start.57 = (bf16[64,768]{1,0:T(8,128)(2,1)}, bf16[64,768]{1,0:T(8,128)(2,1)}, u32[]{:S(2)}, u32[]{:S(2)}) collective-permute-start(bf16[64,768]{1,0:T(8,128)(2,1)} %get-tuple-element.213), channel_id=1, source_target_pairs={{0,32},{32,64},{64,96},{96,0},{1,33},{33,65},{65,97},{97,1},{2,34}... | collective-permute-start | bytes 294920 | tf_op jit(solution)/shard_map/ppermute | solution.py:529
  209.3 19.6 %collective-permute-start.36 = (bf16[160,1024]{1,0:T(8,128)(2,1)S(1)}, bf16[160,1024]{1,0:T(8,128)(2,1)S(1)}, u32[]{:S(2)}, u32[]{:S(2)}) collective-permute-start(bf16[160,1024]{1,0:T(8,128)(2,1)S(1)} %get-tuple-element.192.refs_1_), channel_id=1, source_target_pairs={{0,32},{32,64},{64,96},{96,0},{1,33},{33,65},{65,97},{97,1},{2,34}... | collective-permute-start | bytes 983048 | tf_op jit(solution)/shard_map/ppermute | solution.py:529
  209.4 19.6 %collective-permute-start.37 = (bf16[160,1024]{1,0:T(8,128)(2,1)S(1)}, bf16[160,1024]{1,0:T(8,128)(2,1)S(1)}, u32[]{:S(2)}, u32[]{:S(2)}) collective-permute-start(bf16[160,1024]{1,0:T(8,128)(2,1)S(1)} %get-tuple-element.192.refs_1_), channel_id=1, source_target_pairs={{0,64},{32,96},{64,0},{96,32},{1,65},{33,97},{65,1},{97,33},{2,66}... | collective-permute-start | bytes 983048 | tf_op jit(solution)/shard_map/ppermute | solution.py:529
  214.0 14.9 %collective-permute-start.38 = (bf16[160,1024]{1,0:T(8,128)(2,1)S(1)}, bf16[160,1024]{1,0:T(8,128)(2,1)S(1)}, u32[]{:S(2)}, u32[]{:S(2)}) collective-permute-start(bf16[160,1024]{1,0:T(8,128)(2,1)S(1)} %get-tuple-element.192.refs_1_), channel_id=1, source_target_pairs={{0,96},{32,0},{64,32},{96,64},{1,97},{33,1},{65,33},{97,65},{2,98}... | collective-permute-start | bytes 983048 | tf_op jit(solution)/shard_map/ppermute | solution.py:529
  225.6 18.7 %collective-permute-start.42 = (bf16[160,256]{1,0:T(8,128)(2,1)S(1)}, bf16[160,256]{1,0:T(8,128)(2,1)S(1)}, u32[]{:S(2)}, u32[]{:S(2)}) collective-permute-start(bf16[160,256]{1,0:T(8,128)(2,1)S(1)} %copy-done.181), channel_id=1, source_target_pairs={{0,32},{32,64},{64,96},{96,0},{1,33},{33,65},{65,97},{97,1},{2,34}... | collective-permute-start | bytes 245768 | tf_op jit(solution)/shard_map/ppermute | solution.py:529
  228.3 15.9 %collective-permute-start.60 = (bf16[64,768]{1,0:T(8,128)(2,1)S(1)}, bf16[64,768]{1,0:T(8,128)(2,1)S(1)}, u32[]{:S(2)}, u32[]{:S(2)}) collective-permute-start(bf16[64,768]{1,0:T(8,128)(2,1)S(1)} %get-tuple-element.218.refs_1_), channel_id=1, source_target_pairs={{0,32},{32,64},{64,96},{96,0},{1,33},{33,65},{65,97},{97,1},{2,34}... | collective-permute-start | bytes 294920 | tf_op jit(solution)/shard_map/ppermute | solution.py:529
  236.4 31.3 %collective-permute-start.39 = (bf16[160,1024]{1,0:T(8,128)(2,1)}, bf16[160,1024]{1,0:T(8,128)(2,1)}, u32[]{:S(2)}, u32[]{:S(2)}) collective-permute-start(bf16[160,1024]{1,0:T(8,128)(2,1)} %get-tuple-element.194), channel_id=1, source_target_pairs={{0,32},{32,64},{64,96},{96,0},{1,33},{33,65},{65,97},{97,1},{2,34}... | collective-permute-start | bytes 983048 | tf_op jit(solution)/shard_map/ppermute | solution.py:529
  237.7 30.0 %collective-permute-start.40 = (bf16[160,1024]{1,0:T(8,128)(2,1)}, bf16[160,1024]{1,0:T(8,128)(2,1)}, u32[]{:S(2)}, u32[]{:S(2)}) collective-permute-start(bf16[160,1024]{1,0:T(8,128)(2,1)} %get-tuple-element.195), channel_id=1, source_target_pairs={{0,64},{32,96},{64,0},{96,32},{1,65},{33,97},{65,1},{97,33},{2,66}... | collective-permute-start | bytes 983048 | tf_op jit(solution)/shard_map/ppermute | solution.py:529
  240.7 27.0 %collective-permute-start.41 = (bf16[160,1024]{1,0:T(8,128)(2,1)}, bf16[160,1024]{1,0:T(8,128)(2,1)}, u32[]{:S(2)}, u32[]{:S(2)}) collective-permute-start(bf16[160,1024]{1,0:T(8,128)(2,1)} %get-tuple-element.196), channel_id=1, source_target_pairs={{0,96},{32,0},{64,32},{96,64},{1,97},{33,1},{65,33},{97,65},{2,98}... | collective-permute-start | bytes 983048 | tf_op jit(solution)/shard_map/ppermute | solution.py:529
  250.5 14.0 %collective-permute-start.43 = (bf16[160,256]{1,0:T(8,128)(2,1)S(1)}, bf16[160,256]{1,0:T(8,128)(2,1)S(1)}, u32[]{:S(2)}, u32[]{:S(2)}) collective-permute-start(bf16[160,256]{1,0:T(8,128)(2,1)S(1)} %copy-done.180), channel_id=1, source_target_pairs={{0,64},{32,96},{64,0},{96,32},{1,65},{33,97},{65,1},{97,33},{2,66}... | collective-permute-start | bytes 245768 | tf_op jit(solution)/shard_map/ppermute | solution.py:529
  252.0 13.1 %collective-permute-start.44 = (bf16[160,256]{1,0:T(8,128)(2,1)S(1)}, bf16[160,256]{1,0:T(8,128)(2,1)S(1)}, u32[]{:S(2)}, u32[]{:S(2)}) collective-permute-start(bf16[160,256]{1,0:T(8,128)(2,1)S(1)} %copy-done.179), channel_id=1, source_target_pairs={{0,96},{32,0},{64,32},{96,64},{1,97},{33,1},{65,33},{97,65},{2,98}... | collective-permute-start | bytes 245768 | tf_op jit(solution)/shard_map/ppermute | solution.py:529
  265.1 24.6 %collective-permute-start.63 = (bf16[64,768]{1,0:T(8,128)(2,1)}, bf16[64,768]{1,0:T(8,128)(2,1)}, u32[]{:S(2)}, u32[]{:S(2)}) collective-permute-start(bf16[64,768]{1,0:T(8,128)(2,1)} %get-tuple-element.221), channel_id=1, source_target_pairs={{0,32},{32,64},{64,96},{96,0},{1,33},{33,65},{65,97},{97,1},{2,34}... | collective-permute-start | bytes 294920 | tf_op jit(solution)/shard_map/ppermute | solution.py:529
  265.8 26.9 %collective-permute-start.64 = (bf16[64,768]{1,0:T(8,128)(2,1)}, bf16[64,768]{1,0:T(8,128)(2,1)}, u32[]{:S(2)}, u32[]{:S(2)}) collective-permute-start(bf16[64,768]{1,0:T(8,128)(2,1)} %get-tuple-element.222), channel_id=1, source_target_pairs={{0,64},{32,96},{64,0},{96,32},{1,65},{33,97},{65,1},{97,33},{2,66}... | collective-permute-start | bytes 294920 | tf_op jit(solution)/shard_map/ppermute | solution.py:529
  283.2 23.0 %collective-permute-start.69 = (bf16[160,1024]{1,0:T(8,128)(2,1)S(1)}, bf16[160,1024]{1,0:T(8,128)(2,1)S(1)}, u32[]{:S(2)}, u32[]{:S(2)}) collective-permute-start(bf16[160,1024]{1,0:T(8,128)(2,1)S(1)} %get-tuple-element.227.refs_1_), channel_id=1, source_target_pairs={{0,32},{32,64},{64,96},{96,0},{1,33},{33,65},{65,97},{97,1},{2,34}... | collective-permute-start | bytes 983048 | tf_op jit(solution)/shard_map/ppermute | solution.py:529
  285.4 20.8 %collective-permute-start.70 = (bf16[160,1024]{1,0:T(8,128)(2,1)S(1)}, bf16[160,1024]{1,0:T(8,128)(2,1)S(1)}, u32[]{:S(2)}, u32[]{:S(2)}) collective-permute-start(bf16[160,1024]{1,0:T(8,128)(2,1)S(1)} %get-tuple-element.227.refs_1_), channel_id=1, source_target_pairs={{0,64},{32,96},{64,0},{96,32},{1,65},{33,97},{65,1},{97,33},{2,66}... | collective-permute-start | bytes 983048 | tf_op jit(solution)/shard_map/ppermute | solution.py:529
  286.0 20.2 %collective-permute-start.71 = (bf16[160,1024]{1,0:T(8,128)(2,1)S(1)}, bf16[160,1024]{1,0:T(8,128)(2,1)S(1)}, u32[]{:S(2)}, u32[]{:S(2)}) collective-permute-start(bf16[160,1024]{1,0:T(8,128)(2,1)S(1)} %get-tuple-element.227.refs_1_), channel_id=1, source_target_pairs={{0,96},{32,0},{64,32},{96,64},{1,97},{33,1},{65,33},{97,65},{2,98}... | collective-permute-start | bytes 983048 | tf_op jit(solution)/shard_map/ppermute | solution.py:529
  298.5 48.2 %collective-permute-start.66 = (bf16[64,768]{1,0:T(8,128)(2,1)S(1)}, bf16[64,768]{1,0:T(8,128)(2,1)S(1)}, u32[]{:S(2)}, u32[]{:S(2)}) collective-permute-start(bf16[64,768]{1,0:T(8,128)(2,1)S(1)} %get-tuple-element.226.refs_1_), channel_id=1, source_target_pairs={{0,32},{32,64},{64,96},{96,0},{1,33},{33,65},{65,97},{97,1},{2,34}... | collective-permute-start | bytes 294920 | tf_op jit(solution)/shard_map/ppermute | solution.py:529
  300.2 47.1 %collective-permute-start.67 = (bf16[64,768]{1,0:T(8,128)(2,1)S(1)}, bf16[64,768]{1,0:T(8,128)(2,1)S(1)}, u32[]{:S(2)}, u32[]{:S(2)}) collective-permute-start(bf16[64,768]{1,0:T(8,128)(2,1)S(1)} %get-tuple-element.226.refs_1_), channel_id=1, source_target_pairs={{0,64},{32,96},{64,0},{96,32},{1,65},{33,97},{65,1},{97,33},{2,66}... | collective-permute-start | bytes 294920 | tf_op jit(solution)/shard_map/ppermute | solution.py:529
  315.0 18.6 %collective-permute-start.72 = (bf16[160,1024]{1,0:T(8,128)(2,1)S(1)}, bf16[160,1024]{1,0:T(8,128)(2,1)S(1)}, u32[]{:S(2)}, u32[]{:S(2)}) collective-permute-start(bf16[160,1024]{1,0:T(8,128)(2,1)S(1)} %get-tuple-element.230), channel_id=1, source_target_pairs={{0,32},{32,64},{64,96},{96,0},{1,33},{33,65},{65,97},{97,1},{2,34}... | collective-permute-start | bytes 983048 | tf_op jit(solution)/shard_map/ppermute | solution.py:529
  315.0 18.5 %collective-permute-start.73 = (bf16[160,1024]{1,0:T(8,128)(2,1)S(1)}, bf16[160,1024]{1,0:T(8,128)(2,1)S(1)}, u32[]{:S(2)}, u32[]{:S(2)}) collective-permute-start(bf16[160,1024]{1,0:T(8,128)(2,1)S(1)} %get-tuple-element.231), channel_id=1, source_target_pairs={{0,64},{32,96},{64,0},{96,32},{1,65},{33,97},{65,1},{97,33},{2,66}... | collective-permute-start | bytes 983048 | tf_op jit(solution)/shard_map/ppermute | solution.py:529
  317.3 17.3 %collective-permute-start.74 = (bf16[160,1024]{1,0:T(8,128)(2,1)S(1)}, bf16[160,1024]{1,0:T(8,128)(2,1)S(1)}, u32[]{:S(2)}, u32[]{:S(2)}) collective-permute-start(bf16[160,1024]{1,0:T(8,128)(2,1)S(1)} %get-tuple-element.232), channel_id=1, source_target_pairs={{0,96},{32,0},{64,32},{96,64},{1,97},{33,1},{65,33},{97,65},{2,98}... | collective-permute-start | bytes 983048 | tf_op jit(solution)/shard_map/ppermute | solution.py:529
  341.0 30.1 %collective-permute-start.75 = (bf16[160,1024]{1,0:T(8,128)(2,1)S(1)}, bf16[160,1024]{1,0:T(8,128)(2,1)S(1)}, u32[]{:S(2)}, u32[]{:S(2)}) collective-permute-start(bf16[160,1024]{1,0:T(8,128)(2,1)S(1)} %get-tuple-element.237.refs_5_), channel_id=1, source_target_pairs={{0,32},{32,64},{64,96},{96,0},{1,33},{33,65},{65,97},{97,1},{2,34}... | collective-permute-start | bytes 983048 | tf_op jit(solution)/shard_map/ppermute | solution.py:529
  341.5 33.1 %collective-permute-start.76 = (bf16[160,1024]{1,0:T(8,128)(2,1)S(1)}, bf16[160,1024]{1,0:T(8,128)(2,1)S(1)}, u32[]{:S(2)}, u32[]{:S(2)}) collective-permute-start(bf16[160,1024]{1,0:T(8,128)(2,1)S(1)} %get-tuple-element.237.refs_5_), channel_id=1, source_target_pairs={{0,64},{32,96},{64,0},{96,32},{1,65},{33,97},{65,1},{97,33},{2,66}... | collective-permute-start | bytes 983048 | tf_op jit(solution)/shard_map/ppermute | solution.py:529
  345.3 29.3 %collective-permute-start.77 = (bf16[160,1024]{1,0:T(8,128)(2,1)S(1)}, bf16[160,1024]{1,0:T(8,128)(2,1)S(1)}, u32[]{:S(2)}, u32[]{:S(2)}) collective-permute-start(bf16[160,1024]{1,0:T(8,128)(2,1)S(1)} %get-tuple-element.237.refs_5_), channel_id=1, source_target_pairs={{0,96},{32,0},{64,32},{96,64},{1,97},{33,1},{65,33},{97,65},{2,98}... | collective-permute-start | bytes 983048 | tf_op jit(solution)/shard_map/ppermute | solution.py:529
  346.8 23.1 %collective-permute-start.68 = (bf16[64,768]{1,0:T(8,128)(2,1)S(1)}, bf16[64,768]{1,0:T(8,128)(2,1)S(1)}, u32[]{:S(2)}, u32[]{:S(2)}) collective-permute-start(bf16[64,768]{1,0:T(8,128)(2,1)S(1)} %get-tuple-element.226.refs_1_), channel_id=1, source_target_pairs={{0,96},{32,0},{64,32},{96,64},{1,97},{33,1},{65,33},{97,65},{2,98}... | collective-permute-start | bytes 294920 | tf_op jit(solution)/shard_map/ppermute | solution.py:529
  347.3 53.1 %collective-permute-start.89 = (bf16[2,1024,256]{2,1,0:T(8,128)(2,1)S(1)}, bf16[2,1024,256]{2,1,0:T(8,128)(2,1)}, u32[]{:S(2)}, u32[]{:S(2)}) collective-permute-start(bf16[2,1024,256]{2,1,0:T(8,128)(2,1)S(1)} %copy-done.125), channel_id=1, source_target_pairs={{0,96},{32,0},{64,32},{96,64},{1,97},{33,1},{65,33},{97,65},{2,98}... | collective-permute-start | bytes 3145736 | tf_op jit(solution)/shard_map/ppermute | solution.py:529
  369.9 35.7 %collective-permute-start.88 = (bf16[2,1024,256]{2,1,0:T(8,128)(2,1)S(1)}, bf16[2,1024,256]{2,1,0:T(8,128)(2,1)S(1)}, u32[]{:S(2)}, u32[]{:S(2)}) collective-permute-start(bf16[2,1024,256]{2,1,0:T(8,128)(2,1)S(1)} %copy-done.123), channel_id=1, source_target_pairs={{0,64},{32,96},{64,0},{96,32},{1,65},{33,97},{65,1},{97,33},{2,66}... | collective-permute-start | bytes 3145736 | tf_op jit(solution)/shard_map/ppermute | solution.py:529
  371.0 43.2 %collective-permute-start.87 = (bf16[2,1024,256]{2,1,0:T(8,128)(2,1)S(1)}, bf16[2,1024,256]{2,1,0:T(8,128)(2,1)}, u32[]{:S(2)}, u32[]{:S(2)}) collective-permute-start(bf16[2,1024,256]{2,1,0:T(8,128)(2,1)S(1)} %get-tuple-element.287), channel_id=1, source_target_pairs={{0,32},{32,64},{64,96},{96,0},{1,33},{33,65},{65,97},{97,1},{2,34}... | collective-permute-start | bytes 3145736 | tf_op jit(solution)/shard_map/ppermute | solution.py:529
  374.6 48.7 %collective-permute-start.86 = (bf16[2,1024,256]{2,1,0:T(8,128)(2,1)}, bf16[2,1024,256]{2,1,0:T(8,128)(2,1)S(1)}, u32[]{:S(2)}, u32[]{:S(2)}) collective-permute-start(bf16[2,1024,256]{2,1,0:T(8,128)(2,1)} %get-tuple-element.269), channel_id=1, source_target_pairs={{0,96},{32,0},{64,32},{96,64},{1,97},{33,1},{65,33},{97,65},{2,98}... | collective-permute-start | bytes 3145736 | tf_op jit(solution)/shard_map/ppermute | solution.py:529
  374.6 51.6 %collective-permute-start.85 = (bf16[2,1024,256]{2,1,0:T(8,128)(2,1)}, bf16[2,1024,256]{2,1,0:T(8,128)(2,1)}, u32[]{:S(2)}, u32[]{:S(2)}) collective-permute-start(bf16[2,1024,256]{2,1,0:T(8,128)(2,1)} %get-tuple-element.268), channel_id=1, source_target_pairs={{0,64},{32,96},{64,0},{96,32},{1,65},{33,97},{65,1},{97,33},{2,66}... | collective-permute-start | bytes 3145736 | tf_op jit(solution)/shard_map/ppermute | solution.py:529
  400.4 38.7 %collective-permute-start.84 = (bf16[2,1024,256]{2,1,0:T(8,128)(2,1)S(1)}, bf16[2,1024,256]{2,1,0:T(8,128)(2,1)S(1)}, u32[]{:S(2)}, u32[]{:S(2)}) collective-permute-start(bf16[2,1024,256]{2,1,0:T(8,128)(2,1)S(1)} %get-tuple-element.267), channel_id=1, source_target_pairs={{0,32},{32,64},{64,96},{96,0},{1,33},{33,65},{65,97},{97,1},{2,34}... | collective-permute-start | bytes 3145736 | tf_op jit(solution)/shard_map/ppermute | solution.py:529
  595.7 14.3 %collective-permute-start.83 = (bf16[640,256]{1,0:T(8,128)(2,1)S(1)}, bf16[640,256]{1,0:T(8,128)(2,1)S(1)}, u32[]{:S(2)}, u32[]{:S(2)}) collective-permute-start(bf16[640,256]{1,0:T(8,128)(2,1)S(1)} %copy-done.130), channel_id=1, source_target_pairs={{0,96},{32,0},{64,32},{96,64},{1,97},{33,1},{65,33},{97,65},{2,98}... | collective-permute-start | bytes 983048 | tf_op jit(solution)/shard_map/ppermute | solution.py:529
  599.0 11.3 %collective-permute-start.82 = (bf16[640,256]{1,0:T(8,128)(2,1)S(1)}, bf16[640,256]{1,0:T(8,128)(2,1)S(1)}, u32[]{:S(2)}, u32[]{:S(2)}) collective-permute-start(bf16[640,256]{1,0:T(8,128)(2,1)S(1)} %get-tuple-element.248), channel_id=1, source_target_pairs={{0,64},{32,96},{64,0},{96,32},{1,65},{33,97},{65,1},{97,33},{2,66}... | collective-permute-start | bytes 983048 | tf_op jit(solution)/shard_map/ppermute | solution.py:529
  602.7 11.0 %collective-permute-start.81 = (bf16[640,256]{1,0:T(8,128)(2,1)S(1)}, bf16[640,256]{1,0:T(8,128)(2,1)S(1)}, u32[]{:S(2)}, u32[]{:S(2)}) collective-permute-start(bf16[640,256]{1,0:T(8,128)(2,1)S(1)} %get-tuple-element.247), channel_id=1, source_target_pairs={{0,32},{32,64},{64,96},{96,0},{1,33},{33,65},{65,97},{97,1},{2,34}... | collective-permute-start | bytes 983048 | tf_op jit(solution)/shard_map/ppermute | solution.py:529
  (234 other events, 2247.4 us)
Sparse Core Ops, SparseCore 0:
  11.1 71.5 all-gather.2
  85.7 66.6 all-gather.4
  442.0 145.3 all-reduce.9

commit v2 on v1

v2 whole, which is shorter than its diff:
```python
import functools
import math

import jax
import jax.numpy as jnp
from jax import lax
from jax.experimental import pallas as pl
from jax.experimental.pallas import tpu as pltpu
from jax.sharding import PartitionSpec as P

CO_HEAD = 128
TEXT_HEAD = 64
IMAGE_HEAD = 128
EPS = 1e-05
FILL = -1000000000.0
ROOT_HALF = 0.7071067811865476
INV_ROOT_TWO_PI = 0.3989422804014327
F32 = jnp.float32
BF = jnp.bfloat16
Z = 4
SHORT = pl.CostEstimate(flops=1000, bytes_accessed=1000, transcendentals=0)
LENGTHS = 5


def dot(a, b):
    return lax.dot_general(a, b, (((1,), (0,)), ((), ())), preferred_element_type=F32)


def dot_nt(a, b):
    return lax.dot_general(a, b, (((1,), (1,)), ((), ())), preferred_element_type=F32)


def dot_tn(a, b):
    return lax.dot_general(a, b, (((0,), (0,)), ((), ())), preferred_element_type=F32)


def part(index, size):
    return pl.ds(pl.multiple_of(index * size, size), size)


def row_ids(count, step, samples):
    place = lax.broadcasted_iota(jnp.int32, (count, 1), 0)
    ids = jnp.zeros((count, 1), jnp.int32)
    for s in range(1, samples):
        ids = ids + (place >= s * step).astype(jnp.int32)
    return ids


def key_ids(pos, first, m, step, samples, count):
    place = lax.broadcasted_iota(jnp.int32, (1, count), 1)
    ids = jnp.full((1, count), -1, jnp.int32)
    for s in range(samples):
        live = pos[first + m * samples + s]
        ids = jnp.where((place >= s * step) & (place < s * step + live), s, ids)
    return ids


def probabilities(q, k, same, scale):
    s = jnp.where(same, dot_nt(q, k) * scale, FILL)
    e = jnp.exp(s - jnp.max(s, axis=-1, keepdims=True))
    return e / jnp.sum(e, axis=-1, keepdims=True)


def head_fwd(q, k, v, same, scale):
    return dot(probabilities(q, k, same, scale).astype(BF), v).astype(BF)


def head_bwd(q, k, v, same, scale, do):
    p = probabilities(q, k, same, scale)
    dv = dot_tn(p.astype(BF), do)
    dp = dot_nt(do, v)
    ds = (p * (dp - jnp.sum(dp * p, axis=-1, keepdims=True))).astype(BF)
    dq = dot(ds, k) * scale
    dk = dot_tn(ds, q) * scale
    return dq.astype(BF), dk.astype(BF), dv.astype(BF)


def gelu(u):
    return u * (1.0 + lax.erf(u * ROOT_HALF)) * 0.5


def gelu_slope(u):
    return (1.0 + lax.erf(u * ROOT_HALF)) * 0.5 + u * jnp.exp(u * u * -0.5) * INV_ROOT_TWO_PI


def normalise(z):
    centre = z - jnp.mean(z, axis=-1, keepdims=True)
    rstd = lax.rsqrt(jnp.mean(centre * centre, axis=-1, keepdims=True) + EPS)
    return centre * rstd, rstd


def norm_back(z, gain, dy):
    xhat, rstd = normalise(z)
    dxh = dy * gain
    dz = rstd * (
        dxh
        - jnp.mean(dxh, axis=-1, keepdims=True)
        - xhat * jnp.mean(dxh * xhat, axis=-1, keepdims=True)
    )
    return dz, jnp.sum(dy * xhat, axis=0, keepdims=True), jnp.sum(dy, axis=0, keepdims=True)


class Arriving:
    in_loop = False

    def __init__(self, ref, copy):
        self.ref, self.copy = ref, copy
        self.shape, self.dtype = ref.shape, ref.dtype

    def wait(self):
        if self.copy is not None:
            assert not Arriving.in_loop
            self.copy.wait()
            self.copy = None

    def __getitem__(self, index):
        self.wait()
        return self.ref[index]

    @property
    def at(self):
        self.wait()
        return self.ref.at


class View:
    def __init__(self, array, index, shape):
        self.array, self.index, self.shape, self.dtype = array, index, shape, array.dtype


class Leaving:
    def __init__(self, ref, target, sem):
        self.ref, self.target, self.sem, self.sent = ref, target, sem, False
        self.copy = pltpu.make_async_copy(ref, target, sem)
        self.shape, self.dtype, self.at = ref.shape, ref.dtype, ref.at

    def send(self):
        if not self.sent:
            self.copy.start()
            self.sent = True

    def __getitem__(self, index):
        return self.ref[index]

    def __setitem__(self, index, value):
        assert not self.sent
        self.ref[index] = value


def send(*refs):
    for ref in refs:
        for one in ref if isinstance(ref, list) else [ref]:
            one.send()


def ready(*refs):
    for ref in refs:
        for one in ref if isinstance(ref, list) else [ref]:
            one.wait()


def tiles(count, tile, body):
    def step(i, carry):
        body(part(i, tile))
        return carry

    Arriving.in_loop = True
    lax.fori_loop(0, count // tile, step, 0)
    Arriving.in_loop = False


def total(refs, rows):
    acc = refs[0][rows, :].astype(F32)
    for ref in refs[1:]:
        acc = acc + ref[rows, :].astype(F32)
    return acc


def lanes_in_order(values, r, width):
    near = [values[0], values[3], values[2], values[1]]
    joined = jnp.concatenate([value.astype(F32) for value in near], axis=1)
    return pltpu.roll(joined, r * width, 1)


def lanes_from_own(values, r, width):
    return pltpu.roll(values, ((Z - r) & 3) * width, 1)


def rows_in_order(full, refs, r):
    size = refs[0].shape[0]
    for k, ref in enumerate(refs):
        full[part((r - k) & 3, size), :] = ref[...]


def packed_rows(rows, width, wide):
    return rows * width // wide if width < wide else rows


def put_text(ref, at, value):
    rows, width = value.shape
    wide = ref.shape[1]
    main = packed_rows(rows, width, wide)
    rest = rows - main
    ref[at : at + main, 0:width] = value[0:main]
    for j in range(width // (wide - width)):
        cols = slice(j * (wide - width), (j + 1) * (wide - width))
        ref[at + j * rest : at + (j + 1) * rest, width:wide] = value[main:rows, cols]


def get_text(ref, at, rows, width):
    wide = ref.shape[1]
    if width == wide:
        return ref[at : at + rows, :]
    main = packed_rows(rows, width, wide)
    rest = rows - main
    tail = [
        ref[at + j * rest : at + (j + 1) * rest, width:wide]
        for j in range(width // (wide - width))
    ]
    return jnp.concatenate([ref[at : at + main, 0:width], jnp.concatenate(tail, axis=1)], axis=0)


def both_in_order(xt, xv, both, r):
    ct, cv = xt.shape[0] // Z, xv.shape[0] // Z
    for k, ref in enumerate(both):
        src = (r - k) & 3
        xv[part(src, cv), :] = ref[0:cv, :]
        xt[part(src, ct), :] = get_text(ref, cv, ct, xt.shape[1])


def split(refs, *counts):
    found, at = [], 0
    for count in counts:
        found.append(refs[at] if count == 0 else list(refs[at : at + count]))
        at += max(count, 1)
    assert at == len(refs)
    return found


def co_fwd(dims, *refs):
    rank, both, wt, wv, pt, pv, xt, xv, bt, bv, qt, qv, ot, ov, s = split(
        refs, 0, 4, 0, 0, 0, 0, 0, 0, 0, 0, 0, 0, 0, 0, 4
    )
    samples, text, regions, nt, nv = dims
    r = rank[0]
    rows_t, rows_v = xt.shape[0], xv.shape[0]
    width_t, width_v = xt.shape[1] // Z, xv.shape[1] // Z
    ct, cv = bt.shape[0], bv.shape[0]
    tin = [get_text(ref, rows_v, rows_t, width_t) for ref in both]
    xt[...] = lanes_in_order(tin, r, width_t).astype(BF)
    for k, ref in enumerate(both):
        xv[:, part((r - k) & 3, width_v)] = ref[0:rows_v, :]
    bt[...] = xt[part(r, ct), :]
    bv[...] = xv[part(r, cv), :]
    send(xt, xv, bt, bv)
    for i in range(3):
        qt[i] = dot(xt[...], wt[i]).astype(BF)

    def project(rows):
        for i in range(3):
            qv[i, rows, :] = dot(xv[rows, :], wv[i]).astype(BF)

    ready(wv)
    tiles(xv.shape[0], cv, project)
    send(qt, qv)
    scale = CO_HEAD ** (-0.5)
    rid_t, rid_v = row_ids(nt, text, samples), row_ids(nv, regions, samples)
    for m in range(2):
        rt, rv = slice(m * nt, (m + 1) * nt), slice(m * nv, (m + 1) * nv)
        same_tv = rid_t == key_ids(rank, LENGTHS + 2 * samples, m, regions, samples, nv)
        same_vt = rid_v == key_ids(rank, LENGTHS, m, text, samples, nt)
        for h in range(qt.shape[2] // CO_HEAD):
            c = slice(h * CO_HEAD, (h + 1) * CO_HEAD)
            ot[rt, c] = head_fwd(qt[0, rt, c], qv[1, rv, c], qv[2, rv, c], same_tv, scale)
            ov[rv, c] = head_fwd(qv[0, rv, c], qt[1, rt, c], qt[2, rt, c], same_vt, scale)
    for k in range(Z):
        c = (r + k) & 3
        s[k][0:cv, :] = dot(ov[part(c, cv), :], pv[...]).astype(BF)
        put_text(s[k], cv, dot(ot[part(c, ct), :], pt[...]).astype(BF))
        send(s[k])


def co_bwd(dims, *refs):
    (rank, both, qt, qv, pt, pv, xt, xv, ot, ov,
     dqt, dqv, tq, vq, to, vo, zt, zv, dot_s, dov_s) = split(
        refs, 0, 4, *([0] * 18)
    )
    samples, text, regions, nt, nv = dims
    r = rank[0]
    cv = zv.shape[0] // Z
    both_in_order(zt, zv, both, r)
    dot_s[...] = dot_nt(zt[...], pt[...]).astype(BF)

    def back_out(rows):
        dov_s[rows, :] = dot_nt(zv[rows, :], pv[...]).astype(BF)

    ready(pv)
    tiles(zv.shape[0], cv, back_out)
    scale = CO_HEAD ** (-0.5)
    rid_t, rid_v = row_ids(nt, text, samples), row_ids(nv, regions, samples)
    for m in range(2):
        rt, rv = slice(m * nt, (m + 1) * nt), slice(m * nv, (m + 1) * nv)
        same_tv = rid_t == key_ids(rank, LENGTHS + 2 * samples, m, regions, samples, nv)
        same_vt = rid_v == key_ids(rank, LENGTHS, m, text, samples, nt)
        for h in range(qt.shape[2] // CO_HEAD):
            c = slice(h * CO_HEAD, (h + 1) * CO_HEAD)
            a, b, d = head_bwd(
                qt[0, rt, c], qv[1, rv, c], qv[2, rv, c], same_tv, scale, dot_s[rt, c]
            )
            dqt[0, rt, c], dqv[1, rv, c], dqv[2, rv, c] = a, b, d
            a, b, d = head_bwd(
                qv[0, rv, c], qt[1, rt, c], qt[2, rt, c], same_vt, scale, dov_s[rv, c]
            )
            dqv[0, rv, c], dqt[1, rt, c], dqt[2, rt, c] = a, b, d
    send(dqt, dqv)
    for i in range(3):
        matrix_whole(tq.at[i], xt, dqt.at[i])
        matrix_whole(vq.at[i], xv, dqv.at[i])
    send(tq, vq)
    matrix_whole(to, ot, zt)
    matrix_whole(vo, ov, zv)


def co_bwd_in(*refs):
    rank, dqt, dqv, wt, wv, gt, gv, s, acc_t, acc_v = split(
        refs, 0, 0, 0, 0, 0, 0, 0, 4, 0, 0
    )
    r = rank[0]
    rows_v = acc_v.shape[0]
    ct, cv = gt.shape[0], gv.shape[0]
    width_t, width_v = acc_t.shape[1], acc_v.shape[1]
    own_t = lanes_from_own(gt[...], r, width_t)
    for k in range(Z):
        c = (r + k) & 3
        acc_t[...] = sum(dot_nt(dqt[i], wt[i, part(c, width_t), :]) for i in range(3))
        acc_t[part(r, ct), :] += own_t[:, k * width_t : (k + 1) * width_t]
        put_text(s[k], rows_v, acc_t[...].astype(BF))

        ready(wv, dqv)

        def back_in(rows):
            acc_v[rows, :] = sum(
                dot_nt(dqv[i, rows, :], wv[i, part(c, width_v), :]) for i in range(3)
            )

        tiles(acc_v.shape[0], cv, back_in)
        acc_v[part(r, cv), :] += gv[:, part(c, width_v)]
        s[k][0:rows_v, :] = acc_v[...].astype(BF)
        send(s[k])


def self_fwd(dims_t, dims_v, *refs):
    rank, both, wt, wv, pt, pv, xt, xv, qt, qv, ot, ov, s = split(
        refs, 0, 4, 0, 0, 0, 0, 0, 0, 0, 0, 0, 0, 4
    )
    r = rank[0]
    ct, cv = xt.shape[0] // Z, xv.shape[0] // Z
    both_in_order(xt, xv, both, r)
    send(xt, xv)
    for dims, x, w, q, o in ((dims_v, xv, wv, qv, ov), (dims_t, xt, wt, qt, ot)):
        samples, step, n, head, first = dims

        def project(rows, x=x, w=w, q=q):
            for i in range(3):
                q[i, rows, :] = dot(x[rows, :], w[i]).astype(BF)

        ready(w)
        tiles(x.shape[0], x.shape[0] // Z, project)
        send(q)
        rid = row_ids(n, step, samples)
        for m in range(2):
            rm = slice(m * n, (m + 1) * n)
            same = rid == key_ids(rank, first, m, step, samples, n)
            for h in range(q.shape[2] // head):
                c = slice(h * head, (h + 1) * head)
                o[rm, c] = head_fwd(q[0, rm, c], q[1, rm, c], q[2, rm, c], same, head ** (-0.5))
    for k in range(Z):
        c = (r + k) & 3
        s[k][0:cv, :] = dot(ov[part(c, cv), :], pv[...]).astype(BF)
        put_text(s[k], cv, dot(ot[part(c, ct), :], pt[...]).astype(BF))
        send(s[k])


def self_bwd(dims_t, dims_v, *refs):
    (rank, both, qt, qv, wt, wv, pt, pv,
     zt, zv, dqt, dqv, s, dot_s, dov_s) = split(
        refs, 0, 4, 0, 0, 0, 0, 0, 0, 0, 0, 0, 0, 4, 0, 0
    )
    r = rank[0]
    ct, cv = zt.shape[0] // Z, zv.shape[0] // Z
    both_in_order(zt, zv, both, r)
    send(zt, zv)
    for dims, z, po, q, do, dq in (
        (dims_v, zv, pv, qv, dov_s, dqv),
        (dims_t, zt, pt, qt, dot_s, dqt),
    ):
        samples, step, n, head, first = dims

        def back_out(rows, z=z, po=po, do=do):
            do[rows, :] = dot_nt(z[rows, :], po[...]).astype(BF)

        ready(po)
        tiles(z.shape[0], z.shape[0] // Z, back_out)
        rid = row_ids(n, step, samples)
        for m in range(2):
            rm = slice(m * n, (m + 1) * n)
            same = rid == key_ids(rank, first, m, step, samples, n)
            for h in range(q.shape[2] // head):
                c = slice(h * head, (h + 1) * head)
                a, b, d = head_bwd(
                    q[0, rm, c], q[1, rm, c], q[2, rm, c], same, head ** (-0.5), do[rm, c]
                )
                dq[0, rm, c], dq[1, rm, c], dq[2, rm, c] = a, b, d
    for k in range(Z):
        c = (r + k) & 3
        rows = part(c, cv)
        s[k][0:cv, :] = sum(dot_nt(dqv[i, rows, :], wv[i]) for i in range(3)).astype(BF)
        rows = part(c, ct)
        put_text(s[k], cv, sum(dot_nt(dqt[i, rows, :], wt[i]) for i in range(3)).astype(BF))


def text_total(base, s):
    rows, width = base.shape
    at = s[0].shape[0] - packed_rows(rows, width, s[0].shape[1])
    acc = base[...].astype(F32)
    for ref in s:
        acc = acc + get_text(ref, at, rows, width).astype(F32)
    return acc


def send_text(out, value, image):
    if image is not None:
        out[0 : image.shape[0], :] = image[...]
        put_text(out, image.shape[0], value)
    else:
        out[...] = value


def cut(*refs):
    pos, whole, out = split(refs, 0, 0, 4)
    for k in range(Z):
        out[k][...] = whole[(pos[0] + k) & 3]


def text_norm(position, joint, *refs):
    rank, s, base, gains, shifts, image, z, y, out = split(
        refs if joint else list(refs[:8]) + [None] + list(refs[8:]), 0, 4, 0, 0, 0, 0, 0, 0, 0
    )
    zz = text_total(base, s)
    z[...] = zz
    yy = normalise(zz)[0] * gains[position : position + 1, :] + shifts[position : position + 1, :]
    y[...] = yy
    send_text(out, yy.astype(BF), image)


def text_norm_back(position, joint, *refs):
    rank, s, base, z, gains, image, dz, out, stat = split(
        refs if joint else list(refs[:8]) + [None] + list(refs[8:]), 0, 4, 0, 0, 0, 0, 0, 0, 0
    )
    d, dg, ds = norm_back(z[...], gains[position : position + 1, :], text_total(base, s))
    dz[...] = d
    send_text(out, d.astype(BF), image)
    stat[0:1, :] = dg
    stat[1:2, :] = ds


def text_norm_back_stats(position, *refs):
    rank, s, base, z, gains, image, stats_t, stats_v, dz, out = split(
        refs, 0, 4, 0, 0, 0, 0, 2, 2, 0, 0
    )
    d, dg, ds = norm_back(z[...], gains[position : position + 1, :], text_total(base, s))
    dz[...] = d
    send_text(out, d.astype(BF), image)
    wide = out.shape[1]
    short = [dg, ds] + [ref[...] for ref in stats_t]
    short = jnp.concatenate(short, axis=0)
    short = jnp.concatenate(
        [short, jnp.zeros((short.shape[0], wide - short.shape[1]), F32)], axis=1
    )
    every = jnp.concatenate([short] + [ref[...] for ref in stats_v], axis=0)
    out[out.shape[0] - every.shape[0] : out.shape[0], :] = every.astype(BF)


def text_turn(position, *refs):
    (rank, s, base, cot, image, image_back, w, gains, shifts, out, a, g, d1b, du, dz, send_on, stat,
     u, x, d1) = split(refs, 0, 4, 0, 4, 4, 0, 0, 0, 0, 4, 0, 0, 0, 0, 0, 0, 0, 0, 0, 0)
    r = rank[0]
    g0, b0 = gains[position : position + 1, :], shifts[position : position + 1, :]
    g1, b1 = gains[position + 1 : position + 2, :], shifts[position + 1 : position + 2, :]
    rows, width = base.shape[0], base.shape[1] // Z
    at = image[0].shape[0]
    wide, deep = w.shape[2], base.shape[1]
    blocks = deep // wide
    z0 = text_total(base, s)
    x[...] = normalise(z0)[0] * g0 + b0
    a[...] = x[...].astype(BF)
    send(a)
    down = blocks * deep
    for c in range(Z):
        for j in range(blocks):
            cols = slice((c * blocks + j) * wide, (c * blocks + j + 1) * wide)
            uu = dot(a[...], w[c, j * deep : (j + 1) * deep, :])
            u[:, cols] = uu
            g[:, cols] = gelu(uu).astype(BF)
    send(g)
    for j in range(blocks):
        cols = slice(j * wide, (j + 1) * wide)
        acc = x[:, cols]
        for c in range(Z):
            own = slice(c * deep, (c + 1) * deep)
            acc = acc + dot(g[:, own], w[c, down + j * deep : down + (j + 1) * deep, :])
        x[:, cols] = acc
    z1 = x[...]
    y = lanes_from_own(normalise(z1)[0] * g1 + b1, r, width)
    for k in range(Z):
        send_text(out[k], y[:, k * width : (k + 1) * width].astype(BF), image[k])
        send(out[k])
    dy = lanes_in_order([get_text(ref, at, rows, width) for ref in cot], r, width)
    d, dg, ds = norm_back(z1, g1, dy)
    d1[...] = d
    d1b[...] = d.astype(BF)
    send(d1b)
    stat[2:3, :] = dg
    stat[3:4, :] = ds
    for c in range(Z):
        own = slice(c * deep, (c + 1) * deep)
        back = sum(
            dot_nt(
                d1b[:, j * wide : (j + 1) * wide],
                w[c, down + j * deep : down + (j + 1) * deep, :],
            )
            for j in range(blocks)
        )
        du[:, own] = (back * gelu_slope(u[:, own])).astype(BF)
    send(du)
    back = d1[...]
    for c in range(Z):
        for j in range(blocks):
            cols = slice((c * blocks + j) * wide, (c * blocks + j + 1) * wide)
            back = back + dot_nt(du[:, cols], w[c, j * deep : (j + 1) * deep, :])
    d, dg, ds = norm_back(z0, g0, back)
    dz[...] = d
    send_text(send_on, d.astype(BF), image_back)
    stat[0:1, :] = dg
    stat[1:2, :] = ds


def text_ffn(*refs):
    rank, xin, up, down, x, u, g, s = split(refs, 0, 4, 0, 0, 0, 0, 0, 4)
    r = rank[0]
    size = xin[0].shape[0]
    rows_in_order(x, xin, r)

    def hidden(rows):
        uu = dot(x[rows, :], up[...])
        u[rows, :] = uu
        g[rows, :] = gelu(uu).astype(BF)

    ready(up)
    tiles(x.shape[0], size, hidden)
    send(x, u, g)
    for k in range(Z):
        s[k][...] = dot(g[part((r + k) & 3, size), :], down[...]).astype(BF)
        send(s[k])


def text_ffn_back(*refs):
    rank, din, up, down, u, z, du, s = split(refs, 0, 4, 0, 0, 0, 0, 0, 4)
    r = rank[0]
    size = din[0].shape[0]
    rows_in_order(z, din, r)

    def hidden(rows):
        du[rows, :] = (dot_nt(z[rows, :], down[...]) * gelu_slope(u[rows, :])).astype(BF)

    ready(down, u)
    tiles(z.shape[0], size, hidden)
    send(z, du)
    for k in range(Z):
        s[k][...] = dot_nt(du[part((r + k) & 3, size), :], up[...]).astype(BF)


def image_hidden(a, w, u, g):
    width = w.shape[2]
    depth = w.shape[1] // 2
    for c in range(Z):
        cols = slice(c * width, (c + 1) * width)
        uu = dot(a[...], w[c, 0:depth, :])
        u[:, cols] = uu
        g[:, cols] = gelu(uu).astype(BF)


def image_down(af, g, w, z):
    width = w.shape[2]
    depth = w.shape[1] // 2
    for n in range(Z):
        out = slice(n * width, (n + 1) * width)
        acc = af[:, out]
        rows = slice(depth + n * width, depth + (n + 1) * width)
        for c in range(Z):
            cols = slice(c * width, (c + 1) * width)
            acc = acc + dot(g[:, cols], w[c, rows, :])
        z[:, out] = acc


def image_hidden_back(dzb, w, u, du):
    width = w.shape[2]
    depth = w.shape[1] // 2
    for c in range(Z):
        cols = slice(c * width, (c + 1) * width)
        dg = sum(
            dot_nt(
                dzb[:, n * width : (n + 1) * width],
                w[c, depth + n * width : depth + (n + 1) * width, :],
            )
            for n in range(Z)
        )
        du[:, cols] = (dg * gelu_slope(u[:, cols])).astype(BF)


def image_up_back(dz, du, w, da):
    width = w.shape[2]
    width = w.shape[2]
    for n in range(Z):
        out = slice(n * width, (n + 1) * width)
        acc = dz[:, out]
        for c in range(Z):
            cols = slice(c * width, (c + 1) * width)
            acc = acc + dot_nt(du[:, cols], w[c, n * width : (n + 1) * width, :])
        da[:, out] = acc


def image_mid(position, *refs):
    rank, s, base, w, gains, shifts, z0, a, u, g, z1, y, yb, af = split(
        refs, 0, 4, 0, 0, 0, 0, 0, 0, 0, 0, 0, 0, 0, 0
    )
    g0, b0 = gains[position : position + 1, :], shifts[position : position + 1, :]
    g1, b1 = gains[position + 1 : position + 2, :], shifts[position + 1 : position + 2, :]

    def first(rows):
        zz = base[rows, :].astype(F32) + total(s, rows)
        z0[rows, :] = zz
        aa = normalise(zz)[0] * g0 + b0
        af[rows, :] = aa
        a[rows, :] = aa.astype(BF)

    ready(base, s, gains, shifts)
    tiles(z0.shape[0], 32, first)
    send(z0, a)
    image_hidden(a, w, u, g)
    send(u, g)
    image_down(af, g, w, z1)
    send(z1)

    def second(rows):
        yy = normalise(z1[rows, :])[0] * g1 + b1
        y[rows, :] = yy
        yb[rows, :] = yy.astype(BF)

    tiles(z0.shape[0], 32, second)


def image_mid_back(position, *refs):
    rank, s, base, z1, z0, u, w, gains, d1b, du, d0, d0b, stat, d1, da = split(
        refs, 0, 4, 0, 0, 0, 0, 0, 0, 0, 0, 0, 0, 0, 0, 0
    )
    g0 = gains[position : position + 1, :]
    g1 = gains[position + 1 : position + 2, :]
    stat[...] = jnp.zeros_like(stat)

    def first(rows):
        d, dg, ds = norm_back(z1[rows, :], g1, base[rows, :] + total(s, rows))
        d1[rows, :] = d
        d1b[rows, :] = d.astype(BF)
        stat[2:3, :] += dg
        stat[3:4, :] += ds

    ready(z1, base, s)
    tiles(z0.shape[0], 32, first)
    image_hidden_back(d1b, w, u, du)
    image_up_back(d1, du, w, da)
    ready(z0)

    def second(rows):
        d, dg, ds = norm_back(z0[rows, :], g0, da[rows, :])
        d0[rows, :] = d
        d0b[rows, :] = d.astype(BF)
        stat[0:1, :] += dg
        stat[1:2, :] += ds

    tiles(z0.shape[0], 32, second)


def image_turn(position, *refs):
    (rank, s, base, cot, w, gains, shifts, out, a, g, d1b, du, d0, d0b, stat,
     z0, af, u, z1, y, dy, d1, da) = split(
        refs, 0, 4, 0, 4, 0, 0, 0, 4, 0, 0, 0, 0, 0, 0, 0, 0, 0, 0, 0, 0, 0, 0, 0
    )
    r = rank[0]
    g0, b0 = gains[position : position + 1, :], shifts[position : position + 1, :]
    g1, b1 = gains[position + 1 : position + 2, :], shifts[position + 1 : position + 2, :]
    width = dy.shape[1] // Z
    stat[...] = jnp.zeros_like(stat)
    for k, ref in enumerate(cot):
        dy[:, part((r - k) & 3, width)] = ref[0 : dy.shape[0], :].astype(F32)

    def first(rows):
        zz = base[rows, :] + total(s, rows)
        z0[rows, :] = zz
        aa = normalise(zz)[0] * g0 + b0
        af[rows, :] = aa
        a[rows, :] = aa.astype(BF)

    ready(base, s, gains, shifts)
    tiles(z0.shape[0], 32, first)
    image_hidden(a, w, u, g)
    image_down(af, g, w, z1)

    def second(rows):
        zz = z1[rows, :]
        y[rows, :] = normalise(zz)[0] * g1 + b1
        d, dg, ds = norm_back(zz, g1, dy[rows, :])
        d1[rows, :] = d
        d1b[rows, :] = d.astype(BF)
        stat[2:3, :] += dg
        stat[3:4, :] += ds

    tiles(z0.shape[0], 32, second)
    for k in range(Z):
        out[k][...] = y[:, part((r + k) & 3, width)].astype(BF)
    image_hidden_back(d1b, w, u, du)
    image_up_back(d1, du, w, da)

    def third(rows):
        d, dg, ds = norm_back(z0[rows, :], g0, da[rows, :])
        d0[rows, :] = d
        d0b[rows, :] = d.astype(BF)
        stat[0:1, :] += dg
        stat[1:2, :] += ds

    tiles(z0.shape[0], 32, third)


def ffn_pieces(core, keep, give, a, du, g, dz):
    width = a.shape[1] // Z
    half = a.shape[1] // 2
    for out, which in ((keep, core), (give, 1 - core)):
        cols = part(which, half)
        left_up, right_down = a[:, cols], dz[:, cols]
        for c in range(Z):
            block = slice(c * width, (c + 1) * width)
            row = c * 2 * half
            out[row : row + half, :] = dot_tn(left_up, du[:, block]).astype(BF)
            down = dot_tn(g[:, block], right_down).astype(BF)
            for j in range(half // width):
                at = row + half + j * width
                out[at : at + width, :] = down[:, j * width : (j + 1) * width]


def matrix_whole(out, left, right):
    step = 256 if left.shape[1] % 256 == 0 else left.shape[1]
    for j in range(left.shape[1] // step):
        rows = slice(j * step, (j + 1) * step)
        out[rows, :] = dot_tn(left[:, rows], right[...]).astype(BF)
    if isinstance(out, Leaving):
        send(out)


def grads_image_ffn(*refs):
    pos, a, du, g, dz, keep, give = refs
    ffn_pieces(pos[3], keep, give, a, du, g, dz)


def grads_end(*refs):
    pos, x, du, g, dz, xv, duv, gv, dzv, out = refs
    count, size, wide = out.shape[0], out.shape[2], out.shape[3]
    deep, tall = x.shape[1], xv.shape[1]
    blocks = deep // wide
    ready(x, du, g, dz, xv, duv, gv, dzv)

    def write(c, row, value):
        value = value.astype(BF)
        for d in range(row // size, (row + value.shape[0] - 1) // size + 1):
            lo, hi = max(row, d * size), min(row + value.shape[0], (d + 1) * size)
            out[d, c, lo - d * size : hi - d * size, :] = value[lo - row : hi - row]

    for c in range(Z):
        for j in range(blocks):
            cols = slice((c * blocks + j) * wide, (c * blocks + j + 1) * wide)
            write(c, j * deep, dot_tn(x[...], du[:, cols]))
            own, cols = slice(c * deep, (c + 1) * deep), slice(j * wide, (j + 1) * wide)
            write(c, (blocks + j) * deep, dot_tn(g[:, own], dz[:, cols]))
        row = 2 * blocks * deep
        cols = slice(c * wide, (c + 1) * wide)
        for n in range(tall // wide):
            rows = slice(n * wide, (n + 1) * wide)
            write(c, row + n * wide, dot_tn(xv[:, rows], duv[:, cols]))
            write(c, row + tall + n * wide, dot_tn(gv[:, cols], dzv[:, rows]))


def cut_static(*refs):
    pos, whole, out = split(refs, 0, 0, 4)
    for k in range(Z):
        out[k][...] = whole[-k % Z]


def place_rows(*refs):
    pos, s, out = split(refs, 0, 4, 0)
    out[...] = jnp.zeros(out.shape, BF)
    out[part(pos[4], s[0].shape[0]), :] = total(s, slice(None)).astype(BF)


def grads_text_ffn(*refs):
    pos, x, du, g, dz, up, down = refs
    matrix_whole(up, x, du)
    matrix_whole(down, g, dz)


def grads_attention(*refs):
    pos, xt, dqt, xv, dqv, ot, dzt, ov, dzv, tq, vq, to, vo = refs
    for i in range(3):
        matrix_whole(tq.at[i], xt, dqt.at[i])
        matrix_whole(vq.at[i], xv, dqv.at[i])
    matrix_whole(to, ot, dzt)
    matrix_whole(vo, ov, dzv)


def core_sum(*refs):
    pos, keep, recv, out = split(refs, 0, 0, 0, 4)
    size = out[0].shape[0]
    for k in range(Z):
        rows = slice(-k % Z * size, (-k % Z + 1) * size)
        out[k][...] = (keep[rows, :].astype(F32) + recv[rows, :].astype(F32)).astype(BF)


def tensor_sum_stats(*refs):
    pos, s, both, out = split(refs, 0, 4, 4, 0)
    size, rows = s[0].shape[0], 16
    out[pos[3], 0:size, :] = total(s, slice(None)).astype(BF)
    out[1 - pos[3], 0:size, :] = jnp.zeros(s[0].shape, BF)
    stats = total(both, slice(both[0].shape[0] - rows, both[0].shape[0])).astype(BF)
    wide = out.shape[2]
    for j in range(Z):
        at = size + (j % 2) * rows
        out[j // 2, at : at + rows, :] = stats[:, j * wide : (j + 1) * wide]


def finish(*refs):
    count = 10
    stq, ins, both, end = refs[1], refs[2 : 1 + count], refs[1 + count], refs[2 + count]
    stqo, outs = refs[3 + count], refs[4 + count : 3 + 2 * count]
    up, down, tg, ts, vg, vs = refs[3 + 2 * count : 9 + 2 * count]
    end_refs = refs[9 + 2 * count :]
    for source, out in zip(ins, outs):
        out[...] = source[...].astype(F32)
        send(out)
    for j in range(3):
        stqo[j] = stq[j].astype(F32).T
    send(stqo)
    half, wide = up.shape[0] // 2, up.shape[1]
    for h in range(2):
        up[h * half : (h + 1) * half, :] = both[h, 0:half, :].astype(F32)
        for j in range(half // wide):
            at, to = half + j * wide, h * half + j * wide
            down[:, to : to + wide] = both[h, at : at + wide, :].astype(F32)
    send(up, down)
    blocks = [both[j // 2, 2 * half + j % 2 * 16 : 2 * half + j % 2 * 16 + 16, :] for j in range(Z)]
    stats = jnp.concatenate(blocks, axis=1).astype(F32)
    for i in range(4):
        tg[i : i + 1, :] = stats[2 * i : 2 * i + 1, 0 : tg.shape[1]]
        ts[i : i + 1, :] = stats[2 * i + 1 : 2 * i + 2, 0 : tg.shape[1]]
        vg[i : i + 1, :] = stats[8 + 2 * i : 9 + 2 * i, :]
        vs[i : i + 1, :] = stats[9 + 2 * i : 10 + 2 * i, :]
    up, down, image_up, image_down = end_refs
    deep, tall = up.shape[0], image_up.shape[0]
    blocks = deep // wide
    for j in range(blocks):
        cols = slice(j * wide, (j + 1) * wide)
        up[:, cols] = end[j * deep : (j + 1) * deep, :].astype(F32)
        down[:, cols] = end[(blocks + j) * deep : (blocks + j + 1) * deep, :].astype(F32)
    send(up, down)
    at = 2 * blocks * deep
    image_up[...] = end[at : at + tall, :].astype(F32)
    for j in range(tall // wide):
        row = at + tall + j * wide
        image_down[:, j * wide : (j + 1) * wide] = end[row : row + wide, :].astype(F32)


def placed(array):
    if any(array is one for one in arrived):
        return array
    return pltpu.with_memory_space_constraint(array, pltpu.HBM)


def run(name, body, outs, args, scratch=(), after=()):
    flat = []
    for arg in args:
        flat.extend(arg if isinstance(arg, (list, tuple)) else [arg])
    shapes, groups = [], []
    for shape, dtype, count in outs:
        groups.append(count)
        shapes.extend([pltpu.HBM(shape, dtype)] * max(count, 1))
    scratch = [jax.ShapeDtypeStruct(shape, dtype) for shape, dtype in scratch]
    held = sum(
        math.prod(x.shape) * jnp.dtype(x.dtype).itemsize for x in flat + shapes + scratch
    )
    n_in, n_out = len(flat) - 1, len(shapes)
    first = 1 + n_in + len(after)
    stage = first + n_out
    indices = [x.index if isinstance(x, View) else None for x in flat[1:]]

    def staged_body(*refs):
        sems = refs[-1]
        moves = [
            pltpu.make_async_copy(ref if index is None else ref.at[index], place, sems.at[i])
            for i, (ref, index, place) in enumerate(zip(refs[1 : 1 + n_in], indices, refs[stage:]))
        ]
        for move in moves:
            move.start()
        operands = [Arriving(ref, move) for ref, move in zip(refs[stage:], moves)]
        results = [
            Leaving(ref, target, sems.at[n_in + i])
            for i, (ref, target) in enumerate(zip(refs[stage + n_in :], refs[first:stage]))
        ]
        body(refs[0], *operands, *results, *refs[stage + n_in + n_out : -1])
        for operand in operands:
            operand.wait()
        for result in results:
            result.send()
        for result in results:
            result.copy.wait()

    hbm, free = pl.BlockSpec(memory_space=pltpu.HBM), pl.BlockSpec(memory_space=pl.ANY)
    arrays = [x.array if isinstance(x, View) else x for x in flat[1:]]
    results = pl.pallas_call(
        staged_body,
        out_shape=shapes,
        in_specs=[pl.BlockSpec(memory_space=pltpu.SMEM)] + [free] * (first - 1),
        out_specs=[hbm] * n_out,
        scratch_shapes=[pltpu.VMEM(x.shape, x.dtype) for x in flat[1:] + shapes + scratch]
        + [pltpu.SemaphoreType.DMA((n_in + n_out,))],
        compiler_params=pltpu.CompilerParams(
            vmem_limit_bytes=min(60 << 20, max(16 << 20, held + (8 << 20)))
        ),
        cost_estimate=SHORT,
        name=name,
    )(
        flat[0], *[placed(x) for x in arrays + list(after)])
    return split(list(results), *groups)


def cut_weights(pos, groups, n_dp, wide, after):
    flat = [matrix for group in groups for matrix in group]
    sizes = [sum(math.prod(m.shape) for m in group) // wide // n_dp for group in groups]
    step = 16

    def body(pos_ref, *refs):
        out, sem = refs[-2:]
        sources, base = list(refs[: len(flat)]), 0
        for group, size in zip(groups, sizes):
            steps, offset = size // step, 0
            begin = pos_ref[4] * steps
            for matrix in group:
                source = sources.pop(0)
                rows, width = matrix.shape
                for j in range(width // wide):
                    first = jnp.clip(offset // step - begin, 0, steps)
                    last = jnp.clip((offset + rows) // step - begin, 0, steps)

                    def move(i, carry, source=source, offset=offset, j=j, base=base, begin=begin):
                        row = pl.multiple_of((begin + i) * step - offset, step)
                        to = pl.multiple_of(base + i * step, step)
                        pltpu.make_async_copy(
                            source.at[pl.ds(row, step), pl.ds(j * wide, wide)],
                            out.at[pl.ds(to, step), :],
                            sem,
                        ).start()
                        return carry

                    lax.fori_loop(first, last, move, 0)
                    offset += rows
            base += size
        pltpu.make_async_copy(out, out, sem).wait()

    hbm, free = pl.BlockSpec(memory_space=pltpu.HBM), pl.BlockSpec(memory_space=pl.ANY)
    return pl.pallas_call(
        body,
        out_shape=pltpu.HBM((sum(sizes), wide), BF),
        in_specs=[pl.BlockSpec(memory_space=pltpu.SMEM)] + [free] * (len(flat) + len(after)),
        out_specs=hbm,
        scratch_shapes=[pltpu.SemaphoreType.DMA(())],
        cost_estimate=SHORT,
        name="cut_weights",
    )(pos, *[placed(x) for x in flat + list(after)])


arrived = []


def shift(values, k):
    arrived.append(lax.ppermute(values, "tensor", [(i, (i + k) % Z) for i in range(Z)]))
    return arrived[-1]


def spread(own):
    return [own] + [shift(own, k) for k in (1, 2, 3)]


def swap(chunks):
    return [chunks[0]] + [shift(chunks[k], k) for k in (1, 2, 3)]


def along(values, dy, dx, dc):
    pairs = []
    for y in range(4):
        for x in range(4):
            for c in range(2):
                to = (((y + dy) % 4) * 4 + (x + dx) % 4) * 2 + (c + dc) % 2
                pairs.append(((y * 4 + x) * 2 + c, to))
    arrived.append(lax.ppermute(values, "dp", pairs))
    return arrived[-1]


def pad_rows(values, n):
    micro, samples, rows, width = values.shape
    flat = values.reshape(micro, samples * rows, width)
    flat = jnp.pad(flat, ((0, 0), (0, n - samples * rows), (0, 0)))
    return flat.reshape(micro * n, width)


def unpad_rows(values, shape, n):
    micro, samples, rows, width = shape
    return values.reshape(micro, n, width)[:, : samples * rows].reshape(shape)


def joined(text, image, chunks):
    wide, width = image.shape[1], text.shape[1]
    t = text.reshape(chunks, text.shape[0] // chunks, width)
    main = packed_rows(t.shape[1], width, wide)
    rest = t[:, main:].reshape(chunks, t.shape[1] - main, width // (wide - width), wide - width)
    rest = rest.transpose(0, 2, 1, 3).reshape(chunks, main, wide - width)
    t = jnp.concatenate([t[:, :main], rest], axis=2)
    v = image.reshape(chunks, image.shape[0] // chunks, wide)
    return jnp.concatenate([v, t], axis=1)


def parted(both, text_rows, width):
    wide = both.shape[2]
    main = packed_rows(text_rows, width, wide)
    image, t = both[:, : both.shape[1] - main], both[:, both.shape[1] - main :]
    parts = width // (wide - width)
    rest = t[:, :, width:].reshape(t.shape[0], parts, main // parts, wide - width)
    rest = rest.transpose(0, 2, 1, 3).reshape(t.shape[0], main // parts, width)
    text = jnp.concatenate([t[:, :, :width], rest], axis=1)
    return text.reshape(-1, width), image.reshape(-1, wide)


def in_order(chunks, rank):
    ring = jnp.stack([chunks[0], chunks[3], chunks[2], chunks[1]] * 2)
    return lax.dynamic_slice_in_dim(ring, (Z - rank) & 3, Z, 0)


def shards(
    text_in, image_in, caption_len, region_count, text_cot, image_cot,
    co_text_qkv, co_image_qkv, co_text_out, co_image_out,
    co_text_up, co_text_down, co_image_up, co_image_down,
    self_text_qkv, self_image_qkv, self_text_out, self_image_out,
    text_up, text_down, image_up, image_down,
    text_gains, text_shifts, image_gains, image_shifts,
):
    arrived.clear()
    rank = lax.axis_index("tensor")
    place = lax.axis_index("dp")
    n_dp = lax.axis_size("dp")
    pos = jnp.stack([rank, (place // 2) % 4, place // 8, place % 2, place]).astype(jnp.int32)
    pos = jnp.concatenate([pos, caption_len.reshape(-1), region_count.reshape(-1)])
    micro, samples, text, wt = text_in.shape
    regions, wv = image_in.shape[2:]
    dt, dv = wt * Z, wv * Z
    nt = -(-samples * text // 64) * 64
    nv = -(-samples * regions // 64) * 64
    rt, rv = micro * nt, micro * nv
    ct, cv = rt // Z, rv // Z
    co_w = co_text_qkv.shape[2]
    st_w = self_text_qkv.shape[2]
    si_w = self_image_qkv.shape[2]
    ft = co_text_up.shape[1]
    chunk = ((cv + packed_rows(ct, dt, dv), dv), BF)
    shard = ((cv + packed_rows(ct, wt, wv), wv), BF)
    whole = ((rv + packed_rows(rt, wt, wv), wv), BF)

    both = spread(joined(pad_rows(text_in, nt), pad_rows(image_in, nv), 1)[0])
    groups = [(co_image_up, co_image_down), (text_up, text_down, image_up, image_down)]
    cuts = cut_weights(pos, groups, n_dp, wv, [])
    n_cut = 2 * dv // n_dp
    pieces = spread(cuts)
    w_mid = lax.all_gather(
        jnp.stack([piece[:n_cut] for piece in pieces]), "dp", axis=1, tiled=True
    )
    w_end = lax.all_gather(
        jnp.stack([piece[n_cut:] for piece in pieces]), "dp", axis=1, tiled=True
    )
    n_text = 2 * dt * (ft // wv)
    w_text = View(w_end, (slice(None), pl.ds(0, n_text)), (Z, n_text, wv))
    w_image = View(w_end, (slice(None), pl.ds(n_text, 2 * dv)), (Z, 2 * dv, wv))

    co_dims = (samples, text, regions, nt, nv)
    text_dims = (samples, text, nt, TEXT_HEAD, LENGTHS)
    image_dims = (samples, regions, nv, IMAGE_HEAD, LENGTHS + micro * samples)

    xt0, xv0, bt, bv, qt0, qv0, ot0, ov0, s = run(
        "co_fwd", functools.partial(co_fwd, co_dims),
        [((rt, dt), BF, 0), ((rv, dv), BF, 0), ((ct, dt), BF, 0), ((cv, dv), BF, 0),
         ((3, rt, co_w), BF, 0), ((3, rv, co_w), BF, 0), ((rt, co_w), BF, 0),
         ((rv, co_w), BF, 0), (*chunk, Z)],
        [pos, both, co_text_qkv, co_image_qkv, co_text_out, co_image_out],
    )
    s = swap(s)
    norm_t = [((ct, dt), F32, 0), ((ct, dt), F32, 0)]
    zt0, at, atb = run(
        "text_norm0", functools.partial(text_norm, 0, False), norm_t + [((ct, dt), BF, 0)],
        [pos, s, bt, text_gains, text_shifts],
    )
    cot = joined(pad_rows(text_cot, nt), pad_rows(image_cot, nv), Z)
    (cot,) = run("cut", cut, [(*shard, Z)], [pos, cot], after=[atb])
    cot = swap(cot)
    ffn_t = [((rt, dt), BF, 0), ((rt, ft), F32, 0), ((rt, ft), BF, 0), ((ct, dt), BF, Z)]
    xt1, ut1, gt1, st = run(
        "text_ffn1", text_ffn, ffn_t, [pos, spread(atb), co_text_up, co_text_down]
    )
    zv0, av, uv1, gv1, zv1, bv, bvb = run(
        "image_mid", functools.partial(image_mid, 0),
        [((cv, dv), F32, 0), ((cv, dv), BF, 0), ((cv, dv), F32, 0), ((cv, dv), BF, 0),
         ((cv, dv), F32, 0), ((cv, dv), F32, 0), ((cv, dv), BF, 0)],
        [pos, s, bv, w_mid, image_gains, image_shifts],
        [((cv, dv), F32)],
        after=[st[0]],
    )
    zt1, bt, both = run(
        "text_norm1", functools.partial(text_norm, 1, True), norm_t + [(*chunk, 0)],
        [pos, swap(st), at, text_gains, text_shifts, bvb],
        after=cot[1:],
    )
    both = spread(both)
    xt2, xv2, qt2, qv2, ot2, ov2, s = run(
        "self_fwd", functools.partial(self_fwd, text_dims, image_dims),
        [((rt, dt), BF, 0), ((rv, dv), BF, 0), ((3, rt, st_w), BF, 0),
         ((3, rv, si_w), BF, 0), ((rt, st_w), BF, 0), ((rv, si_w), BF, 0), (*chunk, Z)],
        [pos, both, self_text_qkv, self_image_qkv, self_text_out, self_image_out],
    )
    s = swap(s)
    out_v, av3, gv3, dv3, duv3, gv, gvb, stat_v1 = run(
        "image_turn", functools.partial(image_turn, 2),
        [((cv, wv), BF, Z), ((cv, dv), BF, 0), ((cv, dv), BF, 0), ((cv, dv), BF, 0),
         ((cv, dv), BF, 0), ((cv, dv), F32, 0), ((cv, dv), BF, 0), ((4, dv), F32, 0)],
        [pos, s, bv, cot, w_image, image_gains, image_shifts],
        [((cv, dv), F32)] * 8,
    )
    hidden = Z * ft
    outs, at3, gt3, dt3, dut3, gt, both, stat_t1 = run(
        "text_turn", functools.partial(text_turn, 2),
        [(*shard, Z), ((ct, dt), BF, 0), ((ct, hidden), BF, 0), ((ct, dt), BF, 0),
         ((ct, hidden), BF, 0), ((ct, dt), F32, 0), (*chunk, 0), ((4, dt), F32, 0)],
        [pos, s, bt, cot, out_v, gvb, w_text, text_gains, text_shifts],
        [((ct, hidden), F32), ((ct, dt), F32), ((ct, dt), F32)],
    )

    back_ffn = [((rt, dt), BF, 0), ((rt, ft), BF, 0), ((ct, dt), BF, Z)]
    stat_shape = ((2, dt), F32, 0)

    def image_ffn_grads(name, *saved, after):
        keep, give = run(
            "grads_" + name, grads_image_ffn, [((Z * dv, wv), BF, 0)] * 2, [pos, *saved],
            after=after,
        )
        return keep, along(give, 0, 0, 1)

    def core_summed(name, halves, after):
        (chunks,) = run(
            "core_sum_" + name, core_sum, [((dv, wv), BF, Z)], [pos, *halves], after=after
        )
        return chunks

    both = spread(both)
    (end,) = run(
        "grads_end", grads_end, [((n_dp, Z, (n_text + 2 * dv) // n_dp, wv), BF, 0)],
        [pos, at3, dut3, gt3, dt3, av3, duv3, gv3, dv3],
    )
    end_cut = lax.psum_scatter(end, "dp", scatter_dimension=0, tiled=False)
    dt2, dv2, dqt2, dqv2, s = run(
        "self_back", functools.partial(self_bwd, text_dims, image_dims),
        [((rt, dt), BF, 0), ((rv, dv), BF, 0), ((3, rt, st_w), BF, 0), ((3, rv, si_w), BF, 0),
         (*chunk, Z)],
        [pos, both, qt2, qv2, self_text_qkv, self_image_qkv,
         self_text_out, self_image_out],
        [((rt, st_w), BF), ((rv, si_w), BF)],
        after=[end],
    )
    s = swap(s)
    st_q, sv_q, st_o, sv_o = run(
        "grads_self", grads_attention,
        [((3, dt, st_w), BF, 0), ((3, dv, si_w), BF, 0), ((st_w, dt), BF, 0), ((si_w, dv), BF, 0)],
        [pos, xt2, dqt2, xv2, dqv2, ot2, dt2, ov2, dv2],
    )
    gt, gtb, stat_t2 = run(
        "text_norm1_back", functools.partial(text_norm_back, 1, False),
        [((ct, dt), F32, 0), ((ct, dt), BF, 0), stat_shape],
        [pos, s, gt, zt1, text_gains],
        after=[st_o],
    )
    g = spread(gtb)
    dv1, duv1, gv, gvb, stat_v0 = run(
        "image_mid_back", functools.partial(image_mid_back, 0),
        [((cv, dv), BF, 0), ((cv, dv), BF, 0), ((cv, dv), F32, 0), ((cv, dv), BF, 0),
         ((4, dv), F32, 0)],
        [pos, s, gv, zv1, zv0, uv1, w_mid, image_gains],
        [((cv, dv), F32)] * 2,
        after=[stat_t2],
    )
    dt1, dut1, st = run(
        "text_ffn1_back", text_ffn_back, back_ffn,
        [pos, g, co_text_up, co_text_down, ut1],
        after=[stat_v0],
    )
    st = swap(st)
    mid_f = image_ffn_grads("mid", av, duv1, gv1, dv1, after=[dt1])
    gt, both = run(
        "text_norm0_back", functools.partial(text_norm_back_stats, 0),
        [((ct, dt), F32, 0), ((chunk[0][0] + 16, dv), BF, 0)],
        [pos, st, gt, zt0, text_gains, gvb, stat_t2, stat_t1, stat_v0, stat_v1],
        after=[mid_f[0]],
    )
    both = spread(both)
    (end_cut,) = run(
        "cut_end", cut_static, [(end_cut.shape[1:], BF, Z)], [pos, end_cut], after=[gt]
    )
    end_cut = swap(end_cut)
    t1_up, t1_down = run(
        "grads_ffn1", grads_text_ffn, [((dt, ft), BF, 0), ((ft, dt), BF, 0)],
        [pos, xt1, dut1, gt1, dt1], after=[gt],
    )
    mid_f = core_summed("mid", mid_f, [t1_up, end_cut[0]])
    dqt0, dqv0, tq, vq, to, vo = run(
        "co_back", functools.partial(co_bwd, co_dims),
        [((3, rt, co_w), BF, 0), ((3, rv, co_w), BF, 0),
         ((3, dt, co_w), BF, 0), ((3, dv, co_w), BF, 0), ((co_w, dt), BF, 0), ((co_w, dv), BF, 0)],
        [pos, both, qt0, qv0, co_text_out, co_image_out, xt0, xv0, ot0, ov0],
        [((rt, dt), BF), ((rv, dv), BF), ((rt, co_w), BF), ((rv, co_w), BF)],
        after=[mid_f[0]],
    )
    (end,) = run(
        "place_end", place_rows, [((n_text + 2 * dv, wv), BF, 0)], [pos, end_cut], after=[to]
    )
    (s,) = run(
        "co_back_in", co_bwd_in, [(*whole, Z)],
        [pos, dqt0, dqv0, co_text_qkv, co_image_qkv, gt, gv],
        [((rt, wt), F32), ((rv, wv), F32)],
        after=[end],
    )
    (mid_f,) = run(
        "tensor_sum_mid", tensor_sum_stats, [((2, dv + 32, wv), BF, 0)],
        [pos, swap(mid_f), both], after=[end, s[0]],
    )
    late = lax.psum((st_q, t1_up, t1_down, sv_q, st_o, sv_o, tq, vq, to, vo, mid_f, end), "dp")
    s = swap(s)
    outs = swap(outs)
    ffn_out = [((dt, ft), F32, 0), ((ft, dt), F32, 0)]
    image_out_shapes = [((dv, wv), F32, 0), ((wv, dv), F32, 0)]
    (st_q, t1_up, t1_down, sv_q, st_o, sv_o, tq, vq, to, vo, mid_up, mid_down, tg, ts, vg, vs,
     t_up, t_down, end_up, end_down) = run(
        "finish", finish,
        [((3, st_w, dt), F32, 0)] + ffn_out
        + [((3, dv, si_w), F32, 0), ((st_w, dt), F32, 0), ((si_w, dv), F32, 0),
           ((3, dt, co_w), F32, 0), ((3, dv, co_w), F32, 0),
           ((co_w, dt), F32, 0), ((co_w, dv), F32, 0)] + image_out_shapes
        + [((4, dt), F32, 0)] * 2 + [((4, dv), F32, 0)] * 2 + ffn_out + image_out_shapes,
        [pos, *late],
    )
    st_q = st_q.transpose(0, 2, 1)

    text_out, image_out = parted(in_order(outs, rank), ct, wt)
    text_grad, image_grad = parted(sum(member.astype(F32) for member in s)[None], rt, wt)
    return (
        unpad_rows(text_out, text_in.shape, nt).astype(F32),
        unpad_rows(image_out, image_in.shape, nv).astype(F32),
        unpad_rows(text_grad, text_in.shape, nt),
        unpad_rows(image_grad, image_in.shape, nv),
        tq, vq, to, vo, t1_up, t1_down, mid_up, mid_down,
        st_q, sv_q, st_o, sv_o, t_up, t_down, end_up, end_down,
        tg, ts, vg, vs,
    )


def solution(mesh):
    stream = P(None, "dp", None, "tensor")
    lengths = P(None, "dp")
    stacked = P(None, None, "tensor")
    rows = P("tensor", None)
    cols = P(None, "tensor")
    weights = (
        stacked, stacked, rows, rows, cols, rows, cols, rows,
        stacked, stacked, rows, rows, cols, rows, cols, rows,
        P(), P(), P(), P(),
    )
    in_specs = (stream, stream, lengths, lengths, stream, stream) + weights
    out_specs = (stream,) * 4 + weights
    return jax.shard_map(shards, mesh=mesh, in_specs=in_specs, out_specs=out_specs, check_vma=False)
```

time: 656 us -> 587 us (0.89)
  blocking collectives: 125 us -> 0 us
  waiting for transfers between devices: 159 us -> 280 us
  Pallas kernels: 96.6 us -> 195 us
  starting transfers between devices: 133 us -> 72.1 us
  local copies, waits for them, and re-layouts: 64.2 us -> 12.8 us
  matrix products: 27.3 us -> 0 us
  other arithmetic: 25.2 us -> 2.7 us
    psum x1 -> x0, blocking collectives: 125 us -> none  [shards(): parts = [member.astype(F32) for member in lax.psum(tuple(parts), 'dp')]]
    psum x1, waiting for transfers between devices: 0.01 us -> 108 us  [shards(): lax.psum((st_q, t1_up, t1_down, sv_q, st_o, sv_o, tq, vq, to, vo, mid_f,...]
    pallas_call x22 -> x26, Pallas kernels: 96.6 us -> 195 us  [the longest x25 189 us: run(): pl.pallas_call(staged_body, out_shape=shapes, in_specs=[pl.BlockSpec(memo...]
    ppermute x93 -> x52, starting transfers between devices: 133 us -> 71.9 us  [the longest x51 71.8 us: shift(): lax.ppermute(values, 'tensor', [(i, (i + k) % Z) for i in range(Z)])]
    unnamed x393 -> x51, local copies, waits for them, and re-layouts: 50.4 us -> 3.45 us
    dot_general x20 -> x0, matrix products: 27.3 us -> none  [dot_tn(): lax.dot_general(a, b, (((0,), (0,)), ((), ())), preferred_element_type=F32)]
    convert_element_type x14 -> x1, other arithmetic: 17.6 us -> 0.04 us  [shards(): unpad_rows(image_out, image_in.shape, nv).astype(F32)]
    ppermute x93 -> x52, waiting for transfers between devices: 159 us -> 172 us  [the longest x51 172 us: shift(): lax.ppermute(values, 'tensor', [(i, (i + k) % Z) for i in range(Z)])]
  transfers between devices with their start and end apart: 96 -> 56, of which waited for: 51 -> 30; matrix products, arithmetic and copies ran while one was open for 7% -> 2% of each run, Pallas kernels for 15% -> 23%
where the time goes in v2:
time: 587 us; the launch traced here: 578 us
  waiting for transfers between devices  280 us (48%)
  Pallas kernels  195 us (33%)
  starting transfers between devices  72.1 us (12%)
  between operations  14.9 us (3%)
  local copies, waits for them, and re-layouts  12.8 us (2%)
    pallas_call x25, Pallas kernels, run(): pl.pallas_call(staged_body, out_shape=shapes, in_specs=[pl.BlockSpec(memo...  189 us
    ppermute x51, waiting for transfers between devices, shift(): lax.ppermute(values, 'tensor', [(i, (i + k) % Z) for i in range(Z)])  172 us
    psum x1, waiting for transfers between devices, shards(): lax.psum((st_q, t1_up, t1_down, sv_q, st_o, sv_o, tq, vq, to, vo, mid_f,...  108 us
    ppermute x51, starting transfers between devices, shift(): lax.ppermute(values, 'tensor', [(i, (i + k) % Z) for i in range(Z)])  71.8 us
  transfers between devices with their start and end apart: 56, of which 30 were waited for; matrix products, arithmetic and copies ran while one was open for 2% of the time, Pallas kernels for 23%

profile of v2, /device:TPU:0, one launch (start us, length us, event | category | flops | bytes accessed | tf_op | source)
XLA Modules:
  0.0 577.8 jit_solution(5461568930709770431)
XLA Ops:
  9.4 6.0 %cut_weights.1 = bf16[272,256]{1,0:T(8,128)(2,1)} custom-call(s32[17]{0:T(128)} %concatenate.21.refs_0_.pos_ref, bf16[1024,256]{1,0:T(8,128)(2,1)} %refs_0_.1, bf16[256,1024]{1,0:T(8,128)(2,1)} %refs_1_.1, bf16[768,768]{1,0:T(8,128)(2,1)} %refs_2_.1, bf16[768,768]{1,0:T(8,128)(2,1)} %refs_3_.2, bf16[1024,256]{1,0:T(8,128)(2,1)} %refs_4_.2, ...), custom_call_target="tpu_custom_call" | custom-call | flops 1000 | bytes 1000 | tf_op jit(solution)/shard_map/cut_weights/pallas_call | solution.py:986
  15.4 4.2 collective-permute-start.14
  21.7 4.2 collective-permute-done.14
  34.4 10.7 %collective-permute-done.2.refs_4_ = bf16[832,256]{1,0:T(8,128)(2,1)S(1)} collective-permute-done((bf16[832,256]{1,0:T(8,128)(2,1)S(1)}, bf16[832,256]{1,0:T(8,128)(2,1)S(1)}, u32[]{:S(2)}, u32[]{:S(2)}) %collective-permute-start.2) | collective-permute-done | bytes 426016 | tf_op jit(solution)/shard_map/ppermute | solution.py:1001
  47.6 6.9 %collective-permute-done.refs_2_ = bf16[832,256]{1,0:T(8,128)(2,1)S(1)} collective-permute-done((bf16[832,256]{1,0:T(8,128)(2,1)S(1)}, bf16[832,256]{1,0:T(8,128)(2,1)S(1)}, u32[]{:S(2)}, u32[]{:S(2)}) %collective-permute-start) | collective-permute-done | bytes 426016 | tf_op jit(solution)/shard_map/ppermute | solution.py:1001
  54.5 9.8 %co_fwd.1 = (bf16[256,768]{1,0:T(8,128)(2,1)}, bf16[640,1024]{1,0:T(8,128)(2,1)}, bf16[64,768]{1,0:T(8,128)(2,1)}, bf16[160,1024]{1,0:T(8,128)(2,1)}, bf16[3,256...) custom-call(s32[17]{0:T(128)S(1)} %copy-done, ...), custom_call_target="tpu_custom_call" | custom-call | flops 1000 | bytes 1000 | tf_op jit(solution)/shard_map/co_fwd/pallas_call | solution.py:935
  68.8 17.9 %collective-permute-done.3.refs_2_ = bf16[208,1024]{1,0:T(8,128)(2,1)S(1)} collective-permute-done((bf16[208,1024]{1,0:T(8,128)(2,1)}, bf16[208,1024]{1,0:T(8,128)(2,1)S(1)}, u32[]{:S(2)}, u32[]{:S(2)}) %collective-permute-start.3) | collective-permute-done | bytes 426016 | tf_op jit(solution)/shard_map/ppermute | solution.py:1001
  87.3 3.3 text_norm0.1
  96.9 2.6 collective-permute-start.6
  103.0 4.7 collective-permute-done.6.refs_2_
  107.7 5.3 text_ffn1.1
  116.7 7.7 %image_mid.1 = (f32[160,1024]{1,0:T(8,128)}, bf16[160,1024]{1,0:T(8,128)(2,1)}, f32[160,1024]{1,0:T(8,128)}, bf16[160,1024]{1,0:T(8,128)(2,1)}, f32[160,1024]{1,...) custom-call(s32[17]{0:T(128)S(1)} %copy-done, bf16[208,1024]{1,0:T(8,128)(2,1)} %get-tuple-element.162.refs_1_, ...), custom_call_target="tpu_custom_call" | custom-call | flops 1000 | bytes 1000 | tf_op jit(solution)/shard_map/image_mid/pallas_call | solution.py:935
  124.4 3.1 text_norm1.1
  133.3 7.4 %collective-permute-done.20.refs_4_ = bf16[208,1024]{1,0:T(8,128)(2,1)S(1)} collective-permute-done((bf16[208,1024]{1,0:T(8,128)(2,1)}, bf16[208,1024]{1,0:T(8,128)(2,1)S(1)}, u32[]{:S(2)}, u32[]{:S(2)}) %collective-permute-start.20) | collective-permute-done | bytes 426016 | tf_op jit(solution)/shard_map/ppermute | solution.py:1001
  140.6 2.5 collective-permute-done.19.refs_3_
  143.2 6.0 %collective-permute-done.18.refs_2_ = bf16[208,1024]{1,0:T(8,128)(2,1)S(1)} collective-permute-done((bf16[208,1024]{1,0:T(8,128)(2,1)}, bf16[208,1024]{1,0:T(8,128)(2,1)S(1)}, u32[]{:S(2)}, u32[]{:S(2)}) %collective-permute-start.18) | collective-permute-done | bytes 426016 | tf_op jit(solution)/shard_map/ppermute | solution.py:1001
  149.2 12.8 %self_fwd.1 = (bf16[256,768]{1,0:T(8,128)(2,1)}, bf16[640,1024]{1,0:T(8,128)(2,1)}, bf16[3,256,192]{2,1,0:T(8,128)(2,1)}, bf16[3,640,256]{2,1,0:T(8,128)(2,1)}, ...) custom-call(s32[17]{0:T(128)S(1)} %copy-done, ...), custom_call_target="tpu_custom_call" | custom-call | flops 1000 | bytes 1000 | tf_op jit(solution)/shard_map/self_fwd/pallas_call | solution.py:935
  164.1 3.0 collective-permute-start.23
  167.1 17.2 %collective-permute-done.21.refs_2_ = bf16[208,1024]{1,0:T(8,128)(2,1)S(1)} collective-permute-done((bf16[208,1024]{1,0:T(8,128)(2,1)}, bf16[208,1024]{1,0:T(8,128)(2,1)S(1)}, u32[]{:S(2)}, u32[]{:S(2)}) %collective-permute-start.21) | collective-permute-done | bytes 426016 | tf_op jit(solution)/shard_map/ppermute | solution.py:1001
  184.9 11.9 %image_turn.1 = (bf16[160,256]{1,0:T(8,128)(2,1)}, bf16[160,256]{1,0:T(8,128)(2,1)}, bf16[160,256]{1,0:T(8,128)(2,1)}, bf16[160,256]{1,0:T(8,128)(2,1)}, bf16[16...) custom-call(s32[17]{0:T(128)S(1)} %copy-done, ...), custom_call_target="tpu_custom_call" | custom-call | flops 1000 | bytes 1000 | tf_op jit(solution)/shard_map/image_turn/pallas_call | solution.py:935
  196.8 13.2 %text_turn.1 = (bf16[208,256]{1,0:T(8,128)(2,1)}, bf16[208,256]{1,0:T(8,128)(2,1)}, bf16[208,256]{1,0:T(8,128)(2,1)}, bf16[208,256]{1,0:T(8,128)(2,1)}, bf16[64,...) custom-call(s32[17]{0:T(128)S(1)} %copy-done, ...), custom_call_target="tpu_custom_call" | custom-call | flops 1000 | bytes 1000 | tf_op jit(solution)/shard_map/text_turn/pallas_call | solution.py:935
  210.0 10.9 %grads_end.1.refs_11_ = bf16[32,4,208,256]{3,2,1,0:T(8,128)(2,1)} custom-call(s32[17]{0:T(128)S(1)} %copy-done, bf16[64,768]{1,0:T(8,128)(2,1)} %get-tuple-element.198.refs_1_, bf16[64,3072]{1,0:T(8,128)(2,1)} %get-tuple-element.199.refs_2_, bf16[64,3072]{1,0:T(8,128)(2,1)} %get-tuple-element.200.refs_3_, bf16[64,768]{1,0:T(8,128)(2,1)} %get-tuple-element.201.refs_4_, ...), custom_call_target="tpu_custom_call" | custom-call | flops 1000 | bytes 1000 | tf_op jit(solution)/shard_map/grads_end/pallas_call | solution.py:935
  221.9 2.6 collective-permute-start.29
  225.6 17.4 %collective-permute-done.29.refs_4_ = bf16[208,1024]{1,0:T(8,128)(2,1)S(1)} collective-permute-done((bf16[208,1024]{1,0:T(8,128)(2,1)S(1)}, bf16[208,1024]{1,0:T(8,128)(2,1)S(1)}, u32[]{:S(2)}, u32[]{:S(2)}) %collective-permute-start.29) | collective-permute-done | bytes 426016 | tf_op jit(solution)/shard_map/ppermute | solution.py:1001
  242.9 3.6 collective-permute-done.27.refs_2_
  246.5 18.4 %self_back.1 = (bf16[256,768]{1,0:T(8,128)(2,1)}, bf16[640,1024]{1,0:T(8,128)(2,1)}, bf16[3,256,192]{2,1,0:T(8,128)(2,1)}, bf16[3,640,256]{2,1,0:T(8,128)(2,1)},...) custom-call(s32[17]{0:T(128)S(1)} %copy-done, ...), custom_call_target="tpu_custom_call" | custom-call | flops 1000 | bytes 1000 | tf_op jit(solution)/shard_map/self_back/pallas_call | solution.py:935
  268.3 7.0 %grads_self.1 = (bf16[3,768,192]{2,1,0:T(8,128)(2,1)}, bf16[3,1024,256]{2,1,0:T(8,128)(2,1)}, bf16[192,768]{1,0:T(8,128)(2,1)}, bf16[256,1024]{1,0:T(8,128)(2,1)}) custom-call(s32[17]{0:T(128)S(1)} %copy-done, bf16[256,768]{1,0:T(8,128)(2,1)} %get-tuple-element.212.refs_1_, bf16[3,256,192]{2,1,0:T(8,128)(2,1)} %get-tuple-element.213.refs_2_, ...), custom_call_target="tpu_custom_call" | custom-call | flops 1000 | bytes 1000 | tf_op jit(solution)/shard_map/grads_self/pallas_call | solution.py:935
  275.2 12.0 %collective-permute-done.30.refs_2_ = bf16[208,1024]{1,0:T(8,128)(2,1)S(1)} collective-permute-done((bf16[208,1024]{1,0:T(8,128)(2,1)}, bf16[208,1024]{1,0:T(8,128)(2,1)S(1)}, u32[]{:S(2)}, u32[]{:S(2)}) %collective-permute-start.30) | collective-permute-done | bytes 426016 | tf_op jit(solution)/shard_map/ppermute | solution.py:1001
  287.9 3.5 text_norm1_back.1
  294.9 9.7 %image_mid_back.1 = (bf16[160,1024]{1,0:T(8,128)(2,1)}, bf16[160,1024]{1,0:T(8,128)(2,1)}, f32[160,1024]{1,0:T(8,128)}, bf16[160,1024]{1,0:T(8,128)(2,1)}, f32[4,1024]{1,0:T(4,128)}) custom-call(s32[17]{0:T(128)S(1)} %copy-done, bf16[208,1024]{1,0:T(8,128)(2,1)} %get-tuple-element.206.refs_1_, bf16[208,1024]{1,0:T(8,128)(2,1)S(1)} %collective-permute-done.30.refs_2_, ...), custom_call_target="tpu_custom_call" | custom-call | flops 1000 | bytes 1000 | tf_op jit(solution)/shard_map/image_mid_back/pallas_call | solution.py:935
  304.7 7.3 %text_ffn1_back.1 = (bf16[256,768]{1,0:T(8,128)(2,1)}, bf16[256,768]{1,0:T(8,128)(2,1)}, bf16[64,768]{1,0:T(8,128)(2,1)}, bf16[64,768]{1,0:T(8,128)(2,1)}, bf16[...) custom-call(s32[17]{0:T(128)S(1)} %copy-done, bf16[64,768]{1,0:T(8,128)(2,1)} %get-tuple-element.221.refs_1_, ...), custom_call_target="tpu_custom_call" | custom-call | flops 1000 | bytes 1000 | tf_op jit(solution)/shard_map/text_ffn1_back/pallas_call | solution.py:935
  312.0 4.9 grads_mid.1
  323.4 2.6 collective-permute-done.37.refs_3_
  326.1 3.3 text_norm0_back.1
  329.5 2.9 collective-permute-start.41
  333.8 3.8 grads_ffn1.1
  340.0 3.6 core_sum_mid.1
  348.1 16.0 %collective-permute-done.41.refs_4_.refs_8_ = bf16[224,1024]{1,0:T(8,128)(2,1)S(1)} collective-permute-done((bf16[224,1024]{1,0:T(8,128)(2,1)}, bf16[224,1024]{1,0:T(8,128)(2,1)S(1)}, u32[]{:S(2)}, u32[]{:S(2)}) %collective-permute-start.41) | collective-permute-done | bytes 458784 | tf_op jit(solution)/shard_map/ppermute | solution.py:1001
  364.1 3.7 collective-permute-start.51
  369.3 12.2 %collective-permute-done.43.refs_2_ = bf16[208,256]{1,0:T(8,128)(2,1)S(1)} collective-permute-done((bf16[208,256]{1,0:T(8,128)(2,1)S(1)}, bf16[208,256]{1,0:T(8,128)(2,1)S(1)}, u32[]{:S(2)}, u32[]{:S(2)}) %collective-permute-start.43) | collective-permute-done | bytes 106528 | tf_op jit(solution)/shard_map/ppermute | solution.py:1001
  382.5 14.0 %co_back.1 = (bf16[3,256,256]{2,1,0:T(8,128)(2,1)}, bf16[3,640,256]{2,1,0:T(8,128)(2,1)}, bf16[3,768,256]{2,1,0:T(8,128)(2,1)}, bf16[3,1024,256]{2,1,0:T(8,128)(...) custom-call(s32[17]{0:T(128)S(1)} %copy-done, bf16[224,1024]{1,0:T(8,128)(2,1)} %get-tuple-element.244.refs_1_.refs_5_, ...), custom_call_target="tpu_custom_call" | custom-call | flops 1000 | bytes 1000 | tf_op jit(solution)/shard_map/co_back/pallas_call | solution.py:935
  396.6 3.3 place_end.1.refs_7_.refs_9_
  399.9 10.0 %co_back_in.1 = (bf16[832,256]{1,0:T(8,128)(2,1)}, bf16[832,256]{1,0:T(8,128)(2,1)}, bf16[832,256]{1,0:T(8,128)(2,1)}, bf16[832,256]{1,0:T(8,128)(2,1)}) custom-call(s32[17]{0:T(128)S(1)} %copy-done, bf16[3,256,256]{2,1,0:T(8,128)(2,1)} %get-tuple-element.259.refs_1_, bf16[3,640,256]{2,1,0:T(8,128)(2,1)} %get-tuple-element.260.refs_2_, ...), custom_call_target="tpu_custom_call" | custom-call | flops 1000 | bytes 1000 | tf_op jit(solution)/shard_map/co_back_in/pallas_call | solution.py:935
  409.9 3.2 tensor_sum_mid.1
  419.3 3.0 collective-permute-done.25
  430.6 15.0 %collective-permute-done.46 = bf16[832,256]{1,0:T(8,128)(2,1)S(1)} collective-permute-done((bf16[832,256]{1,0:T(8,128)(2,1)}, bf16[832,256]{1,0:T(8,128)(2,1)S(1)}, u32[]{:S(2)}, u32[]{:S(2)}) %collective-permute-start.46) | collective-permute-done | bytes 426016 | tf_op jit(solution)/shard_map/ppermute | solution.py:1001
  448.9 107.9 %all-reduce.7.cloned.1.call-done = (bf16[3,768,192]{2,1,0:T(8,128)(2,1)}, bf16[768,768]{1,0:T(8,128)(2,1)}, bf16[768,768]{1,0:T(8,128)(2,1)}, bf16[3,1024,256]{2...) async-done(((bf16[3,768,192]{2,1,0:T(8,128)(2,1)}, ...) | async-done | bytes 13795344 | tf_op jit(solution)/shard_map/psum | solution.py:1264
  556.8 14.3 %finish.1 = (f32[3,192,768]{2,1,0:T(8,128)}, f32[768,768]{1,0:T(8,128)}, f32[768,768]{1,0:T(8,128)}, f32[3,1024,256]{2,1,0:T(8,128)}, f32[192,768]{1,0:T(8,128)}...) custom-call(s32[17]{0:T(128)S(1)} %copy-done, ...), custom_call_target="tpu_custom_call" | custom-call | flops 1000 | bytes 1000 | tf_op jit(solution)/shard_map/finish/pallas_call | solution.py:935
  (198 shorter events, 86.5 us)
Async XLA Ops:
  7.2 109.5 %all-gather.3.cloned.1.call-start = ((), (), s32[]{:S(2)}) async-start(), calls=%async_computation.1 | async-start | bytes 4325376 | tf_op jit(solution)/shard_map/all_gather | solution.py:1097
  15.4 10.4 %collective-permute-start.14 = (bf16[272,256]{1,0:T(8,128)(2,1)}, bf16[272,256]{1,0:T(8,128)(2,1)S(1)}, u32[]{:S(2)}, u32[]{:S(2)}) collective-permute-start(bf16[272,256]{1,0:T(8,128)(2,1)} %cut_weights.1), channel_id=1, source_target_pairs={{0,96},{32,0},{64,32},{96,64},{1,97},{33,1},{65,33},{97,65},{2,98}... | collective-permute-start | bytes 417800 | tf_op jit(solution)/shard_map/ppermute | solution.py:1001
  19.6 9.5 %collective-permute-start.12 = (bf16[272,256]{1,0:T(8,128)(2,1)}, bf16[272,256]{1,0:T(8,128)(2,1)S(1)}, u32[]{:S(2)}, u32[]{:S(2)}) collective-permute-start(bf16[272,256]{1,0:T(8,128)(2,1)} %cut_weights.1), channel_id=1, source_target_pairs={{0,32},{32,64},{64,96},{96,0},{1,33},{33,65},{65,97},{97,1},{2,34}... | collective-permute-start | bytes 417800 | tf_op jit(solution)/shard_map/ppermute | solution.py:1001
  29.9 155.1 %all-gather.5.cloned.1.call-start = ((), (), s32[]{:S(2)}) async-start(), calls=%async_computation.2 | async-start | bytes 14057472 | tf_op jit(solution)/shard_map/all_gather | solution.py:1100
  31.7 305.9 %reduce-scatter.2.cloned.1.call-start = ((), (), s32[]{:S(2)}) async-start(), calls=%async_computation.3 | async-start | bytes 14057472 | tf_op jit(solution)/shard_map/reduce_scatter | solution.py:1189
  32.3 12.8 %collective-permute-start.2 = (bf16[832,256]{1,0:T(8,128)(2,1)S(1)}, bf16[832,256]{1,0:T(8,128)(2,1)S(1)}, u32[]{:S(2)}, u32[]{:S(2)}) collective-permute-start(bf16[832,256]{1,0:T(8,128)(2,1)S(1)} %maximum_bitcast_fusion.refs_1_), channel_id=1, source_target_pairs={{0,96},{32,0},{64,32},{96,64},{1,97},{33,1},{65,33},{97,65},{2,98}... | collective-permute-start | bytes 1277960 | tf_op jit(solution)/shard_map/ppermute | solution.py:1001
  33.3 14.3 %collective-permute-start.1 = (bf16[832,256]{1,0:T(8,128)(2,1)S(1)}, bf16[832,256]{1,0:T(8,128)(2,1)S(1)}, u32[]{:S(2)}, u32[]{:S(2)}) collective-permute-start(bf16[832,256]{1,0:T(8,128)(2,1)S(1)} %maximum_bitcast_fusion.refs_1_), channel_id=1, source_target_pairs={{0,64},{32,96},{64,0},{96,32},{1,65},{33,97},{65,1},{97,33},{2,66}... | collective-permute-start | bytes 1277960 | tf_op jit(solution)/shard_map/ppermute | solution.py:1001
  33.6 21.0 %collective-permute-start = (bf16[832,256]{1,0:T(8,128)(2,1)S(1)}, bf16[832,256]{1,0:T(8,128)(2,1)S(1)}, u32[]{:S(2)}, u32[]{:S(2)}) collective-permute-start(bf16[832,256]{1,0:T(8,128)(2,1)S(1)} %maximum_bitcast_fusion.refs_1_), channel_id=1, source_target_pairs={{0,32},{32,64},{64,96},{96,0},{1,33},{33,65},{65,97},{97,1},{2,34}... | collective-permute-start | bytes 1277960 | tf_op jit(solution)/shard_map/ppermute | solution.py:1001
  64.3 22.4 %collective-permute-start.3 = (bf16[208,1024]{1,0:T(8,128)(2,1)}, bf16[208,1024]{1,0:T(8,128)(2,1)S(1)}, u32[]{:S(2)}, u32[]{:S(2)}) collective-permute-start(bf16[208,1024]{1,0:T(8,128)(2,1)} %get-tuple-element.163), channel_id=1, source_target_pairs={{0,32},{32,64},{64,96},{96,0},{1,33},{33,65},{65,97},{97,1},{2,34}... | collective-permute-start | bytes 1277960 | tf_op jit(solution)/shard_map/ppermute | solution.py:1001
  64.4 22.3 %collective-permute-start.4 = (bf16[208,1024]{1,0:T(8,128)(2,1)}, bf16[208,1024]{1,0:T(8,128)(2,1)S(1)}, u32[]{:S(2)}, u32[]{:S(2)}) collective-permute-start(bf16[208,1024]{1,0:T(8,128)(2,1)} %get-tuple-element.164), channel_id=1, source_target_pairs={{0,64},{32,96},{64,0},{96,32},{1,65},{33,97},{65,1},{97,33},{2,66}... | collective-permute-start | bytes 1277960 | tf_op jit(solution)/shard_map/ppermute | solution.py:1001
  67.0 20.4 %collective-permute-start.5 = (bf16[208,1024]{1,0:T(8,128)(2,1)}, bf16[208,1024]{1,0:T(8,128)(2,1)S(1)}, u32[]{:S(2)}, u32[]{:S(2)}) collective-permute-start(bf16[208,1024]{1,0:T(8,128)(2,1)} %get-tuple-element.165), channel_id=1, source_target_pairs={{0,96},{32,0},{64,32},{96,64},{1,97},{33,1},{65,33},{97,65},{2,98}... | collective-permute-start | bytes 1277960 | tf_op jit(solution)/shard_map/ppermute | solution.py:1001
  90.6 9.5 %collective-permute-start.8 = (bf16[64,768]{1,0:T(8,128)(2,1)}, bf16[64,768]{1,0:T(8,128)(2,1)S(1)}, u32[]{:S(2)}, u32[]{:S(2)}) collective-permute-start(bf16[64,768]{1,0:T(8,128)(2,1)} %get-tuple-element.167.refs_1_.refs_2_), channel_id=1, source_target_pairs={{0,96},{32,0},{64,32},{96,64},{1,97},{33,1},{65,33},{97,65},{2,98}... | collective-permute-start | bytes 294920 | tf_op jit(solution)/shard_map/ppermute | solution.py:1001
  95.4 19.1 %collective-permute-start.15 = (bf16[208,256]{1,0:T(8,128)(2,1)}, bf16[208,256]{1,0:T(8,128)(2,1)S(1)}, u32[]{:S(2)}, u32[]{:S(2)}) collective-permute-start(bf16[208,256]{1,0:T(8,128)(2,1)} %get-tuple-element.175), channel_id=1, source_target_pairs={{0,32},{32,64},{64,96},{96,0},{1,33},{33,65},{65,97},{97,1},{2,34}... | collective-permute-start | bytes 319496 | tf_op jit(solution)/shard_map/ppermute | solution.py:1001
  96.9 10.7 %collective-permute-start.6 = (bf16[64,768]{1,0:T(8,128)(2,1)}, bf16[64,768]{1,0:T(8,128)(2,1)S(1)}, u32[]{:S(2)}, u32[]{:S(2)}) collective-permute-start(bf16[64,768]{1,0:T(8,128)(2,1)} %get-tuple-element.167.refs_1_.refs_2_), channel_id=1, source_target_pairs={{0,32},{32,64},{64,96},{96,0},{1,33},{33,65},{65,97},{97,1},{2,34}... | collective-permute-start | bytes 294920 | tf_op jit(solution)/shard_map/ppermute | solution.py:1001
  99.6 24.8 %collective-permute-start.16 = (bf16[208,256]{1,0:T(8,128)(2,1)}, bf16[208,256]{1,0:T(8,128)(2,1)S(1)}, u32[]{:S(2)}, u32[]{:S(2)}) collective-permute-start(bf16[208,256]{1,0:T(8,128)(2,1)} %get-tuple-element.176), channel_id=1, source_target_pairs={{0,64},{32,96},{64,0},{96,32},{1,65},{33,97},{65,1},{97,33},{2,66}... | collective-permute-start | bytes 319496 | tf_op jit(solution)/shard_map/ppermute | solution.py:1001
  100.2 24.2 %collective-permute-start.17 = (bf16[208,256]{1,0:T(8,128)(2,1)}, bf16[208,256]{1,0:T(8,128)(2,1)S(1)}, u32[]{:S(2)}, u32[]{:S(2)}) collective-permute-start(bf16[208,256]{1,0:T(8,128)(2,1)} %get-tuple-element.177), channel_id=1, source_target_pairs={{0,96},{32,0},{64,32},{96,64},{1,97},{33,1},{65,33},{97,65},{2,98}... | collective-permute-start | bytes 319496 | tf_op jit(solution)/shard_map/ppermute | solution.py:1001
  113.0 11.4 %collective-permute-start.9 = (bf16[64,768]{1,0:T(8,128)(2,1)}, bf16[64,768]{1,0:T(8,128)(2,1)S(1)}, u32[]{:S(2)}, u32[]{:S(2)}) collective-permute-start(bf16[64,768]{1,0:T(8,128)(2,1)} %get-tuple-element.169), channel_id=1, source_target_pairs={{0,32},{32,64},{64,96},{96,0},{1,33},{33,65},{65,97},{97,1},{2,34}... | collective-permute-start | bytes 294920 | tf_op jit(solution)/shard_map/ppermute | solution.py:1001
  113.1 11.3 %collective-permute-start.10 = (bf16[64,768]{1,0:T(8,128)(2,1)}, bf16[64,768]{1,0:T(8,128)(2,1)S(1)}, u32[]{:S(2)}, u32[]{:S(2)}) collective-permute-start(bf16[64,768]{1,0:T(8,128)(2,1)} %get-tuple-element.170), channel_id=1, source_target_pairs={{0,64},{32,96},{64,0},{96,32},{1,65},{33,97},{65,1},{97,33},{2,66}... | collective-permute-start | bytes 294920 | tf_op jit(solution)/shard_map/ppermute | solution.py:1001
  114.5 10.0 %collective-permute-start.11 = (bf16[64,768]{1,0:T(8,128)(2,1)}, bf16[64,768]{1,0:T(8,128)(2,1)S(1)}, u32[]{:S(2)}, u32[]{:S(2)}) collective-permute-start(bf16[64,768]{1,0:T(8,128)(2,1)} %get-tuple-element.171), channel_id=1, source_target_pairs={{0,96},{32,0},{64,32},{96,64},{1,97},{33,1},{65,33},{97,65},{2,98}... | collective-permute-start | bytes 294920 | tf_op jit(solution)/shard_map/ppermute | solution.py:1001
  127.6 13.0 %collective-permute-start.20 = (bf16[208,1024]{1,0:T(8,128)(2,1)}, bf16[208,1024]{1,0:T(8,128)(2,1)S(1)}, u32[]{:S(2)}, u32[]{:S(2)}) collective-permute-start(bf16[208,1024]{1,0:T(8,128)(2,1)} %get-tuple-element.178.refs_1_), channel_id=1, source_target_pairs={{0,96},{32,0},{64,32},{96,64},{1,97},{33,1},{65,33},{97,65},{2,98}... | collective-permute-start | bytes 1277960 | tf_op jit(solution)/shard_map/ppermute | solution.py:1001
  128.7 14.5 %collective-permute-start.19 = (bf16[208,1024]{1,0:T(8,128)(2,1)}, bf16[208,1024]{1,0:T(8,128)(2,1)S(1)}, u32[]{:S(2)}, u32[]{:S(2)}) collective-permute-start(bf16[208,1024]{1,0:T(8,128)(2,1)} %get-tuple-element.178.refs_1_), channel_id=1, source_target_pairs={{0,64},{32,96},{64,0},{96,32},{1,65},{33,97},{65,1},{97,33},{2,66}... | collective-permute-start | bytes 1277960 | tf_op jit(solution)/shard_map/ppermute | solution.py:1001
  130.5 18.6 %collective-permute-start.18 = (bf16[208,1024]{1,0:T(8,128)(2,1)}, bf16[208,1024]{1,0:T(8,128)(2,1)S(1)}, u32[]{:S(2)}, u32[]{:S(2)}) collective-permute-start(bf16[208,1024]{1,0:T(8,128)(2,1)} %get-tuple-element.178.refs_1_), channel_id=1, source_target_pairs={{0,32},{32,64},{64,96},{96,0},{1,33},{33,65},{65,97},{97,1},{2,34}... | collective-permute-start | bytes 1277960 | tf_op jit(solution)/shard_map/ppermute | solution.py:1001
  161.9 22.4 %collective-permute-start.21 = (bf16[208,1024]{1,0:T(8,128)(2,1)}, bf16[208,1024]{1,0:T(8,128)(2,1)S(1)}, u32[]{:S(2)}, u32[]{:S(2)}) collective-permute-start(bf16[208,1024]{1,0:T(8,128)(2,1)} %get-tuple-element.180), channel_id=1, source_target_pairs={{0,32},{32,64},{64,96},{96,0},{1,33},{33,65},{65,97},{97,1},{2,34}... | collective-permute-start | bytes 1277960 | tf_op jit(solution)/shard_map/ppermute | solution.py:1001
  162.9 21.4 %collective-permute-start.22 = (bf16[208,1024]{1,0:T(8,128)(2,1)}, bf16[208,1024]{1,0:T(8,128)(2,1)S(1)}, u32[]{:S(2)}, u32[]{:S(2)}) collective-permute-start(bf16[208,1024]{1,0:T(8,128)(2,1)} %get-tuple-element.181), channel_id=1, source_target_pairs={{0,64},{32,96},{64,0},{96,32},{1,65},{33,97},{65,1},{97,33},{2,66}... | collective-permute-start | bytes 1277960 | tf_op jit(solution)/shard_map/ppermute | solution.py:1001
  164.1 20.8 %collective-permute-start.23 = (bf16[208,1024]{1,0:T(8,128)(2,1)}, bf16[208,1024]{1,0:T(8,128)(2,1)S(1)}, u32[]{:S(2)}, u32[]{:S(2)}) collective-permute-start(bf16[208,1024]{1,0:T(8,128)(2,1)} %get-tuple-element.182), channel_id=1, source_target_pairs={{0,96},{32,0},{64,32},{96,64},{1,97},{33,1},{65,33},{97,65},{2,98}... | collective-permute-start | bytes 1277960 | tf_op jit(solution)/shard_map/ppermute | solution.py:1001
  221.0 335.8 %all-reduce.7.cloned.1.call-start = ((), (), s32[]{:S(2)}) async-start(), calls=%async_computation.4 | async-start | bytes 28180480 | tf_op jit(solution)/shard_map/psum | solution.py:1264
  221.9 21.0 %collective-permute-start.29 = (bf16[208,1024]{1,0:T(8,128)(2,1)S(1)}, bf16[208,1024]{1,0:T(8,128)(2,1)S(1)}, u32[]{:S(2)}, u32[]{:S(2)}) collective-permute-start(bf16[208,1024]{1,0:T(8,128)(2,1)S(1)} %copy-done.5), channel_id=1, source_target_pairs={{0,96},{32,0},{64,32},{96,64},{1,97},{33,1},{65,33},{97,65},{2,98}... | collective-permute-start | bytes 1277960 | tf_op jit(solution)/shard_map/ppermute | solution.py:1001
  224.6 18.4 %collective-permute-start.28 = (bf16[208,1024]{1,0:T(8,128)(2,1)S(1)}, bf16[208,1024]{1,0:T(8,128)(2,1)S(1)}, u32[]{:S(2)}, u32[]{:S(2)}) collective-permute-start(bf16[208,1024]{1,0:T(8,128)(2,1)S(1)} %copy-done.5), channel_id=1, source_target_pairs={{0,64},{32,96},{64,0},{96,32},{1,65},{33,97},{65,1},{97,33},{2,66}... | collective-permute-start | bytes 1277960 | tf_op jit(solution)/shard_map/ppermute | solution.py:1001
  224.9 21.7 %collective-permute-start.27 = (bf16[208,1024]{1,0:T(8,128)(2,1)S(1)}, bf16[208,1024]{1,0:T(8,128)(2,1)S(1)}, u32[]{:S(2)}, u32[]{:S(2)}) collective-permute-start(bf16[208,1024]{1,0:T(8,128)(2,1)S(1)} %copy-done.5), channel_id=1, source_target_pairs={{0,32},{32,64},{64,96},{96,0},{1,33},{33,65},{65,97},{97,1},{2,34}... | collective-permute-start | bytes 1277960 | tf_op jit(solution)/shard_map/ppermute | solution.py:1001
  264.9 22.3 %collective-permute-start.30 = (bf16[208,1024]{1,0:T(8,128)(2,1)}, bf16[208,1024]{1,0:T(8,128)(2,1)S(1)}, u32[]{:S(2)}, u32[]{:S(2)}) collective-permute-start(bf16[208,1024]{1,0:T(8,128)(2,1)} %get-tuple-element.207), channel_id=1, source_target_pairs={{0,32},{32,64},{64,96},{96,0},{1,33},{33,65},{65,97},{97,1},{2,34}... | collective-permute-start | bytes 1277960 | tf_op jit(solution)/shard_map/ppermute | solution.py:1001
  265.0 22.2 %collective-permute-start.31 = (bf16[208,1024]{1,0:T(8,128)(2,1)}, bf16[208,1024]{1,0:T(8,128)(2,1)S(1)}, u32[]{:S(2)}, u32[]{:S(2)}) collective-permute-start(bf16[208,1024]{1,0:T(8,128)(2,1)} %get-tuple-element.208), channel_id=1, source_target_pairs={{0,64},{32,96},{64,0},{96,32},{1,65},{33,97},{65,1},{97,33},{2,66}... | collective-permute-start | bytes 1277960 | tf_op jit(solution)/shard_map/ppermute | solution.py:1001
  267.2 20.6 %collective-permute-start.32 = (bf16[208,1024]{1,0:T(8,128)(2,1)}, bf16[208,1024]{1,0:T(8,128)(2,1)S(1)}, u32[]{:S(2)}, u32[]{:S(2)}) collective-permute-start(bf16[208,1024]{1,0:T(8,128)(2,1)} %get-tuple-element.209), channel_id=1, source_target_pairs={{0,96},{32,0},{64,32},{96,64},{1,97},{33,1},{65,33},{97,65},{2,98}... | collective-permute-start | bytes 1277960 | tf_op jit(solution)/shard_map/ppermute | solution.py:1001
  291.3 13.3 %collective-permute-start.35 = (bf16[64,768]{1,0:T(8,128)(2,1)}, bf16[64,768]{1,0:T(8,128)(2,1)S(1)}, u32[]{:S(2)}, u32[]{:S(2)}) collective-permute-start(bf16[64,768]{1,0:T(8,128)(2,1)} %get-tuple-element.221.refs_1_), channel_id=1, source_target_pairs={{0,96},{32,0},{64,32},{96,64},{1,97},{33,1},{65,33},{97,65},{2,98}... | collective-permute-start | bytes 294920 | tf_op jit(solution)/shard_map/ppermute | solution.py:1001
  293.8 10.9 %collective-permute-start.34 = (bf16[64,768]{1,0:T(8,128)(2,1)}, bf16[64,768]{1,0:T(8,128)(2,1)S(1)}, u32[]{:S(2)}, u32[]{:S(2)}) collective-permute-start(bf16[64,768]{1,0:T(8,128)(2,1)} %get-tuple-element.221.refs_1_), channel_id=1, source_target_pairs={{0,64},{32,96},{64,0},{96,32},{1,65},{33,97},{65,1},{97,33},{2,66}... | collective-permute-start | bytes 294920 | tf_op jit(solution)/shard_map/ppermute | solution.py:1001
  293.8 10.9 %collective-permute-start.33 = (bf16[64,768]{1,0:T(8,128)(2,1)}, bf16[64,768]{1,0:T(8,128)(2,1)S(1)}, u32[]{:S(2)}, u32[]{:S(2)}) collective-permute-start(bf16[64,768]{1,0:T(8,128)(2,1)} %get-tuple-element.221.refs_1_), channel_id=1, source_target_pairs={{0,32},{32,64},{64,96},{96,0},{1,33},{33,65},{65,97},{97,1},{2,34}... | collective-permute-start | bytes 294920 | tf_op jit(solution)/shard_map/ppermute | solution.py:1001
  316.9 23.1 %collective-permute-start.42 = (bf16[4096,256]{1,0:T(8,128)(2,1)}, bf16[4096,256]{1,0:T(8,128)(2,1)S(1)}, u32[]{:S(2)}, u32[]{:S(2)}) collective-permute-start(bf16[4096,256]{1,0:T(8,128)(2,1)} %get-tuple-element.251), channel_id=1, source_target_pairs={{0,1},{1,0},{2,3},{3,2},{4,5},{5,4},{6,7},{7,6},{8,9},{9,8},{10,11... | collective-permute-start | bytes 6291464 | tf_op jit(solution)/shard_map/ppermute | solution.py:1020
  329.5 34.6 %collective-permute-start.41 = (bf16[224,1024]{1,0:T(8,128)(2,1)}, bf16[224,1024]{1,0:T(8,128)(2,1)S(1)}, u32[]{:S(2)}, u32[]{:S(2)}) collective-permute-start(bf16[224,1024]{1,0:T(8,128)(2,1)} %get-tuple-element.244.refs_1_.refs_5_), channel_id=1, source_target_pairs={{0,96},{32,0},{64,32},{96,64},{1,97},{33,1},{65,33},{97,65},{2,98}... | collective-permute-start | bytes 1376264 | tf_op jit(solution)/shard_map/ppermute | solution.py:1001
  332.4 35.4 %collective-permute-start.40 = (bf16[224,1024]{1,0:T(8,128)(2,1)}, bf16[224,1024]{1,0:T(8,128)(2,1)S(1)}, u32[]{:S(2)}, u32[]{:S(2)}) collective-permute-start(bf16[224,1024]{1,0:T(8,128)(2,1)} %get-tuple-element.244.refs_1_.refs_5_), channel_id=1, source_target_pairs={{0,64},{32,96},{64,0},{96,32},{1,65},{33,97},{65,1},{97,33},{2,66}... | collective-permute-start | bytes 1376264 | tf_op jit(solution)/shard_map/ppermute | solution.py:1001
  333.4 34.4 %collective-permute-start.39 = (bf16[224,1024]{1,0:T(8,128)(2,1)}, bf16[224,1024]{1,0:T(8,128)(2,1)S(1)}, u32[]{:S(2)}, u32[]{:S(2)}) collective-permute-start(bf16[224,1024]{1,0:T(8,128)(2,1)} %get-tuple-element.244.refs_1_.refs_5_), channel_id=1, source_target_pairs={{0,32},{32,64},{64,96},{96,0},{1,33},{33,65},{65,97},{97,1},{2,34}... | collective-permute-start | bytes 1376264 | tf_op jit(solution)/shard_map/ppermute | solution.py:1001
  343.7 66.2 %collective-permute-start.49 = (bf16[1024,256]{1,0:T(8,128)(2,1)}, bf16[1024,256]{1,0:T(8,128)(2,1)S(1)}, u32[]{:S(2)}, u32[]{:S(2)}) collective-permute-start(bf16[1024,256]{1,0:T(8,128)(2,1)} %get-tuple-element.277), channel_id=1, source_target_pairs={{0,32},{32,64},{64,96},{96,0},{1,33},{33,65},{65,97},{97,1},{2,34}... | collective-permute-start | bytes 1572872 | tf_op jit(solution)/shard_map/ppermute | solution.py:1001
  345.8 64.1 %collective-permute-start.50 = (bf16[1024,256]{1,0:T(8,128)(2,1)}, bf16[1024,256]{1,0:T(8,128)(2,1)S(1)}, u32[]{:S(2)}, u32[]{:S(2)}) collective-permute-start(bf16[1024,256]{1,0:T(8,128)(2,1)} %get-tuple-element.278), channel_id=1, source_target_pairs={{0,64},{32,96},{64,0},{96,32},{1,65},{33,97},{65,1},{97,33},{2,66}... | collective-permute-start | bytes 1572872 | tf_op jit(solution)/shard_map/ppermute | solution.py:1001
  364.1 45.8 %collective-permute-start.51 = (bf16[1024,256]{1,0:T(8,128)(2,1)}, bf16[1024,256]{1,0:T(8,128)(2,1)S(1)}, u32[]{:S(2)}, u32[]{:S(2)}) collective-permute-start(bf16[1024,256]{1,0:T(8,128)(2,1)} %get-tuple-element.279), channel_id=1, source_target_pairs={{0,96},{32,0},{64,32},{96,64},{1,97},{33,1},{65,33},{97,65},{2,98}... | collective-permute-start | bytes 1572872 | tf_op jit(solution)/shard_map/ppermute | solution.py:1001
  367.8 13.7 %collective-permute-start.43 = (bf16[208,256]{1,0:T(8,128)(2,1)S(1)}, bf16[208,256]{1,0:T(8,128)(2,1)S(1)}, u32[]{:S(2)}, u32[]{:S(2)}) collective-permute-start(bf16[208,256]{1,0:T(8,128)(2,1)S(1)} %copy-done.17), channel_id=1, source_target_pairs={{0,32},{32,64},{64,96},{96,0},{1,33},{33,65},{65,97},{97,1},{2,34}... | collective-permute-start | bytes 319496 | tf_op jit(solution)/shard_map/ppermute | solution.py:1001
  367.8 28.7 %collective-permute-start.44 = (bf16[208,256]{1,0:T(8,128)(2,1)S(1)}, bf16[208,256]{1,0:T(8,128)(2,1)S(1)}, u32[]{:S(2)}, u32[]{:S(2)}) collective-permute-start(bf16[208,256]{1,0:T(8,128)(2,1)S(1)} %copy-done.16), channel_id=1, source_target_pairs={{0,64},{32,96},{64,0},{96,32},{1,65},{33,97},{65,1},{97,33},{2,66}... | collective-permute-start | bytes 319496 | tf_op jit(solution)/shard_map/ppermute | solution.py:1001
  381.5 15.1 %collective-permute-start.45 = (bf16[208,256]{1,0:T(8,128)(2,1)S(1)}, bf16[208,256]{1,0:T(8,128)(2,1)S(1)}, u32[]{:S(2)}, u32[]{:S(2)}) collective-permute-start(bf16[208,256]{1,0:T(8,128)(2,1)S(1)} %copy-done.15), channel_id=1, source_target_pairs={{0,96},{32,0},{64,32},{96,64},{1,97},{33,1},{65,33},{97,65},{2,98}... | collective-permute-start | bytes 319496 | tf_op jit(solution)/shard_map/ppermute | solution.py:1001
  424.1 21.6 %collective-permute-start.46 = (bf16[832,256]{1,0:T(8,128)(2,1)}, bf16[832,256]{1,0:T(8,128)(2,1)S(1)}, u32[]{:S(2)}, u32[]{:S(2)}) collective-permute-start(bf16[832,256]{1,0:T(8,128)(2,1)} %get-tuple-element.267), channel_id=1, source_target_pairs={{0,32},{32,64},{64,96},{96,0},{1,33},{33,65},{65,97},{97,1},{2,34}... | collective-permute-start | bytes 1277960 | tf_op jit(solution)/shard_map/ppermute | solution.py:1001
  424.4 21.2 %collective-permute-start.47 = (bf16[832,256]{1,0:T(8,128)(2,1)S(1)}, bf16[832,256]{1,0:T(8,128)(2,1)S(1)}, u32[]{:S(2)}, u32[]{:S(2)}) collective-permute-start(bf16[832,256]{1,0:T(8,128)(2,1)S(1)} %copy-done.11), channel_id=1, source_target_pairs={{0,64},{32,96},{64,0},{96,32},{1,65},{33,97},{65,1},{97,33},{2,66}... | collective-permute-start | bytes 1277960 | tf_op jit(solution)/shard_map/ppermute | solution.py:1001
  425.7 20.3 %collective-permute-start.48 = (bf16[832,256]{1,0:T(8,128)(2,1)S(1)}, bf16[832,256]{1,0:T(8,128)(2,1)S(1)}, u32[]{:S(2)}, u32[]{:S(2)}) collective-permute-start(bf16[832,256]{1,0:T(8,128)(2,1)S(1)} %copy-done.10), channel_id=1, source_target_pairs={{0,96},{32,0},{64,32},{96,64},{1,97},{33,1},{65,33},{97,65},{2,98}... | collective-permute-start | bytes 1277960 | tf_op jit(solution)/shard_map/ppermute | solution.py:1001
  (29 other events, 367.4 us)
Sparse Core Ops, SparseCore 0:
  30.0 45.1 all-gather.2
  78.1 64.7 all-gather.4
  221.1 108.1 reduce-scatter.1
  413.3 143.4 all-reduce.6

commit v3 on v2

--- a/solution.py
+++ b/solution.py
@@ -18,7 +18,7 @@
 F32 = jnp.float32
 BF = jnp.bfloat16
 Z = 4
-SHORT = pl.CostEstimate(flops=1000, bytes_accessed=1000, transcendentals=0)
+COST = pl.CostEstimate(flops=20_000_000_000, bytes_accessed=1000, transcendentals=0)
 LENGTHS = 5
 
 
@@ -123,6 +123,18 @@
         return self.ref.at
 
 
+class Scalars:
+    def __init__(self, places, *lengths):
+        self.places, self.lengths = places, lengths
+
+    def __getitem__(self, i):
+        if i < LENGTHS:
+            return self.places[i]
+        micro, samples = self.lengths[0].shape
+        which, at = divmod(i - LENGTHS, micro * samples)
+        return self.lengths[which][at // samples, at % samples]
+
+
 class View:
     def __init__(self, array, index, shape):
         self.array, self.index, self.shape, self.dtype = array, index, shape, array.dtype
@@ -187,9 +199,9 @@
 
 
 def rows_in_order(full, refs, r):
-    size = refs[0].shape[0]
+    size = full.shape[0] // Z
     for k, ref in enumerate(refs):
-        full[part((r - k) & 3, size), :] = ref[...]
+        full[part((r - k) & 3, size), :] = ref[0:size, :]
 
 
 def packed_rows(rows, width, wide):
@@ -220,14 +232,6 @@
     return jnp.concatenate([ref[at : at + main, 0:width], jnp.concatenate(tail, axis=1)], axis=0)
 
 
-def both_in_order(xt, xv, both, r):
-    ct, cv = xt.shape[0] // Z, xv.shape[0] // Z
-    for k, ref in enumerate(both):
-        src = (r - k) & 3
-        xv[part(src, cv), :] = ref[0:cv, :]
-        xt[part(src, ct), :] = get_text(ref, cv, ct, xt.shape[1])
-
-
 def split(refs, *counts):
     found, at = [], 0
     for count in counts:
@@ -238,8 +242,8 @@
 
 
 def co_fwd(dims, *refs):
-    rank, both, wt, wv, pt, pv, xt, xv, bt, bv, qt, qv, ot, ov, s = split(
-        refs, 0, 4, 0, 0, 0, 0, 0, 0, 0, 0, 0, 0, 0, 0, 4
+    rank, both, wt, wv, pt, pv, xt, xv, bt, bv, qt, qv, ot, ov, st, sv = split(
+        refs, 0, 4, 0, 0, 0, 0, 0, 0, 0, 0, 0, 0, 0, 0, 4, 4
     )
     samples, text, regions, nt, nv = dims
     r = rank[0]
@@ -275,20 +279,21 @@
             ov[rv, c] = head_fwd(qv[0, rv, c], qt[1, rt, c], qt[2, rt, c], same_vt, scale)
     for k in range(Z):
         c = (r + k) & 3
-        s[k][0:cv, :] = dot(ov[part(c, cv), :], pv[...]).astype(BF)
-        put_text(s[k], cv, dot(ot[part(c, ct), :], pt[...]).astype(BF))
-        send(s[k])
+        st[k][...] = dot(ot[part(c, ct), :], pt[...]).astype(BF)
+        sv[k][...] = dot(ov[part(c, cv), :], pv[...]).astype(BF)
+        send(st[k], sv[k])
 
 
 def co_bwd(dims, *refs):
-    (rank, both, qt, qv, pt, pv, xt, xv, ot, ov,
+    (rank, dt, dv, qt, qv, pt, pv, xt, xv, ot, ov,
      dqt, dqv, tq, vq, to, vo, zt, zv, dot_s, dov_s) = split(
-        refs, 0, 4, *([0] * 18)
+        refs, 0, 4, 4, *([0] * 18)
     )
     samples, text, regions, nt, nv = dims
     r = rank[0]
     cv = zv.shape[0] // Z
-    both_in_order(zt, zv, both, r)
+    rows_in_order(zt, dt, r)
+    rows_in_order(zv, dv, r)
     dot_s[...] = dot_nt(zt[...], pt[...]).astype(BF)
 
     def back_out(rows):
@@ -349,91 +354,72 @@
         send(s[k])
 
 
-def self_fwd(dims_t, dims_v, *refs):
-    rank, both, wt, wv, pt, pv, xt, xv, qt, qv, ot, ov, s = split(
-        refs, 0, 4, 0, 0, 0, 0, 0, 0, 0, 0, 0, 0, 4
-    )
+def self_fwd(dims, *refs):
+    rank, xin, w, po, x, q, o, s = split(refs, 0, 4, 0, 0, 0, 0, 0, 4)
+    samples, step, n, head, first = dims
     r = rank[0]
-    ct, cv = xt.shape[0] // Z, xv.shape[0] // Z
-    both_in_order(xt, xv, both, r)
-    send(xt, xv)
-    for dims, x, w, q, o in ((dims_v, xv, wv, qv, ov), (dims_t, xt, wt, qt, ot)):
-        samples, step, n, head, first = dims
-
-        def project(rows, x=x, w=w, q=q):
-            for i in range(3):
-                q[i, rows, :] = dot(x[rows, :], w[i]).astype(BF)
-
-        ready(w)
-        tiles(x.shape[0], x.shape[0] // Z, project)
-        send(q)
-        rid = row_ids(n, step, samples)
-        for m in range(2):
-            rm = slice(m * n, (m + 1) * n)
-            same = rid == key_ids(rank, first, m, step, samples, n)
-            for h in range(q.shape[2] // head):
-                c = slice(h * head, (h + 1) * head)
-                o[rm, c] = head_fwd(q[0, rm, c], q[1, rm, c], q[2, rm, c], same, head ** (-0.5))
+    size = xin[0].shape[0]
+    rows_in_order(x, xin, r)
+    send(x)
+
+    def project(rows):
+        for i in range(3):
+            q[i, rows, :] = dot(x[rows, :], w[i]).astype(BF)
+
+    ready(w)
+    tiles(x.shape[0], size, project)
+    send(q)
+    rid = row_ids(n, step, samples)
+    for m in range(2):
+        rm = slice(m * n, (m + 1) * n)
+        same = rid == key_ids(rank, first, m, step, samples, n)
+        for h in range(q.shape[2] // head):
+            c = slice(h * head, (h + 1) * head)
+            o[rm, c] = head_fwd(q[0, rm, c], q[1, rm, c], q[2, rm, c], same, head ** (-0.5))
+    send(o)
     for k in range(Z):
-        c = (r + k) & 3
-        s[k][0:cv, :] = dot(ov[part(c, cv), :], pv[...]).astype(BF)
-        put_text(s[k], cv, dot(ot[part(c, ct), :], pt[...]).astype(BF))
+        s[k][...] = dot(o[part((r + k) & 3, size), :], po[...]).astype(BF)
         send(s[k])
 
 
-def self_bwd(dims_t, dims_v, *refs):
-    (rank, both, qt, qv, wt, wv, pt, pv,
-     zt, zv, dqt, dqv, s, dot_s, dov_s) = split(
-        refs, 0, 4, 0, 0, 0, 0, 0, 0, 0, 0, 0, 0, 4, 0, 0
-    )
+def self_bwd(dims, *refs):
+    rank, din, q, w, po, z, dq, s, do = split(refs, 0, 4, 0, 0, 0, 0, 0, 4, 0)
+    samples, step, n, head, first = dims
     r = rank[0]
-    ct, cv = zt.shape[0] // Z, zv.shape[0] // Z
-    both_in_order(zt, zv, both, r)
-    send(zt, zv)
-    for dims, z, po, q, do, dq in (
-        (dims_v, zv, pv, qv, dov_s, dqv),
-        (dims_t, zt, pt, qt, dot_s, dqt),
-    ):
-        samples, step, n, head, first = dims
-
-        def back_out(rows, z=z, po=po, do=do):
-            do[rows, :] = dot_nt(z[rows, :], po[...]).astype(BF)
-
-        ready(po)
-        tiles(z.shape[0], z.shape[0] // Z, back_out)
-        rid = row_ids(n, step, samples)
-        for m in range(2):
-            rm = slice(m * n, (m + 1) * n)
-            same = rid == key_ids(rank, first, m, step, samples, n)
-            for h in range(q.shape[2] // head):
-                c = slice(h * head, (h + 1) * head)
-                a, b, d = head_bwd(
-                    q[0, rm, c], q[1, rm, c], q[2, rm, c], same, head ** (-0.5), do[rm, c]
-                )
-                dq[0, rm, c], dq[1, rm, c], dq[2, rm, c] = a, b, d
+    size = din[0].shape[0]
+    rows_in_order(z, din, r)
+    send(z)
+
+    def back_out(rows):
+        do[rows, :] = dot_nt(z[rows, :], po[...]).astype(BF)
+
+    ready(po)
+    tiles(z.shape[0], size, back_out)
+    rid = row_ids(n, step, samples)
+    for m in range(2):
+        rm = slice(m * n, (m + 1) * n)
+        same = rid == key_ids(rank, first, m, step, samples, n)
+        for h in range(q.shape[2] // head):
+            c = slice(h * head, (h + 1) * head)
+            a, b, d = head_bwd(
+                q[0, rm, c], q[1, rm, c], q[2, rm, c], same, head ** (-0.5), do[rm, c]
+            )
+            dq[0, rm, c], dq[1, rm, c], dq[2, rm, c] = a, b, d
+    send(dq)
     for k in range(Z):
-        c = (r + k) & 3
-        rows = part(c, cv)
-        s[k][0:cv, :] = sum(dot_nt(dqv[i, rows, :], wv[i]) for i in range(3)).astype(BF)
-        rows = part(c, ct)
-        put_text(s[k], cv, sum(dot_nt(dqt[i, rows, :], wt[i]) for i in range(3)).astype(BF))
+        rows = part((r + k) & 3, size)
+        s[k][...] = sum(dot_nt(dq[i, rows, :], w[i]) for i in range(3)).astype(BF)
+        send(s[k])
 
 
 def text_total(base, s):
-    rows, width = base.shape
-    at = s[0].shape[0] - packed_rows(rows, width, s[0].shape[1])
-    acc = base[...].astype(F32)
-    for ref in s:
-        acc = acc + get_text(ref, at, rows, width).astype(F32)
-    return acc
-
-
-def send_text(out, value, image):
-    if image is not None:
-        out[0 : image.shape[0], :] = image[...]
-        put_text(out, image.shape[0], value)
-    else:
-        out[...] = value
+    return base[...].astype(F32) + total(s, slice(None))
+
+
+def stat_rows(out, at, *stats):
+    every = jnp.concatenate([ref[...] for ref in stats], axis=0)
+    pad = jnp.zeros((out.shape[0] - at - every.shape[0], out.shape[1]), F32)
+    out[at : out.shape[0], :] = jnp.concatenate([every, pad], axis=0).astype(BF)
 
 
 def cut(*refs):
@@ -442,53 +428,45 @@
         out[k][...] = whole[(pos[0] + k) & 3]
 
 
-def text_norm(position, joint, *refs):
-    rank, s, base, gains, shifts, image, z, y, out = split(
-        refs if joint else list(refs[:8]) + [None] + list(refs[8:]), 0, 4, 0, 0, 0, 0, 0, 0, 0
-    )
+def text_norm(position, *refs):
+    rank, s, base, gains, shifts, z, y, out = split(refs, 0, 4, 0, 0, 0, 0, 0, 0)
     zz = text_total(base, s)
     z[...] = zz
     yy = normalise(zz)[0] * gains[position : position + 1, :] + shifts[position : position + 1, :]
     y[...] = yy
-    send_text(out, yy.astype(BF), image)
-
-
-def text_norm_back(position, joint, *refs):
-    rank, s, base, z, gains, image, dz, out, stat = split(
-        refs if joint else list(refs[:8]) + [None] + list(refs[8:]), 0, 4, 0, 0, 0, 0, 0, 0, 0
-    )
+    out[...] = yy.astype(BF)
+
+
+def text_norm_back(position, *refs):
+    rank, s, base, z, gains, dz, out, stat = split(refs, 0, 4, 0, 0, 0, 0, 0, 0)
     d, dg, ds = norm_back(z[...], gains[position : position + 1, :], text_total(base, s))
     dz[...] = d
-    send_text(out, d.astype(BF), image)
+    out[...] = d.astype(BF)
     stat[0:1, :] = dg
     stat[1:2, :] = ds
 
 
 def text_norm_back_stats(position, *refs):
-    rank, s, base, z, gains, image, stats_t, stats_v, dz, out = split(
-        refs, 0, 4, 0, 0, 0, 0, 2, 2, 0, 0
+    rank, s, base, z, gains, stat_1, stat_2, dz, out, stat = split(
+        refs, 0, 4, 0, 0, 0, 0, 0, 0, 0, 0
     )
     d, dg, ds = norm_back(z[...], gains[position : position + 1, :], text_total(base, s))
     dz[...] = d
-    send_text(out, d.astype(BF), image)
-    wide = out.shape[1]
-    short = [dg, ds] + [ref[...] for ref in stats_t]
-    short = jnp.concatenate(short, axis=0)
-    short = jnp.concatenate(
-        [short, jnp.zeros((short.shape[0], wide - short.shape[1]), F32)], axis=1
-    )
-    every = jnp.concatenate([short] + [ref[...] for ref in stats_v], axis=0)
-    out[out.shape[0] - every.shape[0] : out.shape[0], :] = every.astype(BF)
+    rows = d.shape[0]
+    out[0:rows, :] = d.astype(BF)
+    stat[0:1, :] = dg
+    stat[1:2, :] = ds
+    stat_rows(out, rows, stat, stat_1, stat_2)
 
 
 def text_turn(position, *refs):
-    (rank, s, base, cot, image, image_back, w, gains, shifts, out, a, g, d1b, du, dz, send_on, stat,
-     u, x, d1) = split(refs, 0, 4, 0, 4, 4, 0, 0, 0, 0, 4, 0, 0, 0, 0, 0, 0, 0, 0, 0, 0)
+    (rank, s, base, cot, w, gains, shifts, out, a, g, d1b, du, dz, send_on, stat,
+     u, x, d1) = split(refs, 0, 4, 0, 4, 0, 0, 0, 4, 0, 0, 0, 0, 0, 0, 0, 0, 0, 0)
     r = rank[0]
     g0, b0 = gains[position : position + 1, :], shifts[position : position + 1, :]
     g1, b1 = gains[position + 1 : position + 2, :], shifts[position + 1 : position + 2, :]
     rows, width = base.shape[0], base.shape[1] // Z
-    at = image[0].shape[0]
+    at = cot[0].shape[0] - packed_rows(rows, width, cot[0].shape[1])
     wide, deep = w.shape[2], base.shape[1]
     blocks = deep // wide
     z0 = text_total(base, s)
@@ -513,7 +491,7 @@
     z1 = x[...]
     y = lanes_from_own(normalise(z1)[0] * g1 + b1, r, width)
     for k in range(Z):
-        send_text(out[k], y[:, k * width : (k + 1) * width].astype(BF), image[k])
+        out[k][...] = y[:, k * width : (k + 1) * width].astype(BF)
         send(out[k])
     dy = lanes_in_order([get_text(ref, at, rows, width) for ref in cot], r, width)
     d, dg, ds = norm_back(z1, g1, dy)
@@ -540,7 +518,7 @@
             back = back + dot_nt(du[:, cols], w[c, j * deep : (j + 1) * deep, :])
     d, dg, ds = norm_back(z0, g0, back)
     dz[...] = d
-    send_text(send_on, d.astype(BF), image_back)
+    send_on[...] = d.astype(BF)
     stat[0:1, :] = dg
     stat[1:2, :] = ds
 
@@ -661,8 +639,8 @@
 
 
 def image_mid_back(position, *refs):
-    rank, s, base, z1, z0, u, w, gains, d1b, du, d0, d0b, stat, d1, da = split(
-        refs, 0, 4, 0, 0, 0, 0, 0, 0, 0, 0, 0, 0, 0, 0, 0
+    rank, s, base, z1, z0, u, w, gains, stat_1, d1b, du, d0, d0b, stat, d1, da = split(
+        refs, 0, 4, 0, 0, 0, 0, 0, 0, 0, 0, 0, 0, 0, 0, 0, 0
     )
     g0 = gains[position : position + 1, :]
     g1 = gains[position + 1 : position + 2, :]
@@ -689,6 +667,7 @@
         stat[1:2, :] += ds
 
     tiles(z0.shape[0], 32, second)
+    stat_rows(d0b, z0.shape[0], stat, stat_1)
 
 
 def image_turn(position, *refs):
@@ -834,12 +813,17 @@
 
 
 def tensor_sum_stats(*refs):
-    pos, s, both, out = split(refs, 0, 4, 4, 0)
+    pos, s, text, image, out = split(refs, 0, 4, 4, 4, 0)
     size, rows = s[0].shape[0], 16
     out[pos[3], 0:size, :] = total(s, slice(None)).astype(BF)
     out[1 - pos[3], 0:size, :] = jnp.zeros(s[0].shape, BF)
-    stats = total(both, slice(both[0].shape[0] - rows, both[0].shape[0])).astype(BF)
-    wide = out.shape[2]
+    last = [slice(x[0].shape[0] - rows, x[0].shape[0] - rows // 2) for x in (text, image)]
+    wide, tall = out.shape[2], image[0].shape[1]
+    narrow = total(text, last[0])
+    narrow = jnp.concatenate(
+        [narrow, jnp.zeros((narrow.shape[0], tall - narrow.shape[1]), F32)], axis=1
+    )
+    stats = jnp.concatenate([narrow, total(image, last[1])], axis=0).astype(BF)
     for j in range(Z):
         at = size + (j % 2) * rows
         out[j // 2, at : at + rows, :] = stats[:, j * wide : (j + 1) * wide]
@@ -892,9 +876,17 @@
     return pltpu.with_memory_space_constraint(array, pltpu.HBM)
 
 
+latest = []
+
+
+def follow(results):
+    latest[:] = [min(results, key=lambda x: x.size)]
+
+
 def run(name, body, outs, args, scratch=(), after=()):
-    flat = []
-    for arg in args:
+    after = latest + list(after)
+    flat = [None]
+    for arg in args[1:]:
         flat.extend(arg if isinstance(arg, (list, tuple)) else [arg])
     shapes, groups = [], []
     for shape, dtype, count in outs:
@@ -902,7 +894,7 @@
         shapes.extend([pltpu.HBM(shape, dtype)] * max(count, 1))
     scratch = [jax.ShapeDtypeStruct(shape, dtype) for shape, dtype in scratch]
     held = sum(
-        math.prod(x.shape) * jnp.dtype(x.dtype).itemsize for x in flat + shapes + scratch
+        math.prod(x.shape) * jnp.dtype(x.dtype).itemsize for x in flat[1:] + shapes + scratch
     )
     n_in, n_out = len(flat) - 1, len(shapes)
     first = 1 + n_in + len(after)
@@ -910,6 +902,7 @@
     indices = [x.index if isinstance(x, View) else None for x in flat[1:]]
 
     def staged_body(*refs):
+        refs = (Scalars(*refs[:3]), *refs[3:])
         sems = refs[-1]
         moves = [
             pltpu.make_async_copy(ref if index is None else ref.at[index], place, sems.at[i])
@@ -935,21 +928,22 @@
     results = pl.pallas_call(
         staged_body,
         out_shape=shapes,
-        in_specs=[pl.BlockSpec(memory_space=pltpu.SMEM)] + [free] * (first - 1),
+        in_specs=[pl.BlockSpec(memory_space=pltpu.SMEM)] * 3 + [free] * (first - 1),
         out_specs=[hbm] * n_out,
         scratch_shapes=[pltpu.VMEM(x.shape, x.dtype) for x in flat[1:] + shapes + scratch]
         + [pltpu.SemaphoreType.DMA((n_in + n_out,))],
         compiler_params=pltpu.CompilerParams(
             vmem_limit_bytes=min(60 << 20, max(16 << 20, held + (8 << 20)))
         ),
-        cost_estimate=SHORT,
+        cost_estimate=COST,
         name=name,
     )(
-        flat[0], *[placed(x) for x in arrays + list(after)])
+        *args[0], *[placed(x) for x in arrays + after])
+    follow(results)
     return split(list(results), *groups)
 
 
-def cut_weights(pos, groups, n_dp, wide, after):
+def cut_weights(scalars, groups, n_dp, wide):
     flat = [matrix for group in groups for matrix in group]
     sizes = [sum(math.prod(m.shape) for m in group) // wide // n_dp for group in groups]
     step = 16
@@ -983,15 +977,18 @@
         pltpu.make_async_copy(out, out, sem).wait()
 
     hbm, free = pl.BlockSpec(memory_space=pltpu.HBM), pl.BlockSpec(memory_space=pl.ANY)
-    return pl.pallas_call(
+    after = list(latest)
+    result = pl.pallas_call(
         body,
         out_shape=pltpu.HBM((sum(sizes), wide), BF),
         in_specs=[pl.BlockSpec(memory_space=pltpu.SMEM)] + [free] * (len(flat) + len(after)),
         out_specs=hbm,
         scratch_shapes=[pltpu.SemaphoreType.DMA(())],
-        cost_estimate=SHORT,
+        cost_estimate=COST,
         name="cut_weights",
-    )(pos, *[placed(x) for x in flat + list(after)])
+    )(scalars[0], *[placed(x) for x in flat + after])
+    follow([result])
+    return result
 
 
 arrived = []
@@ -1069,11 +1066,12 @@
     text_gains, text_shifts, image_gains, image_shifts,
 ):
     arrived.clear()
+    latest.clear()
     rank = lax.axis_index("tensor")
     place = lax.axis_index("dp")
     n_dp = lax.axis_size("dp")
     pos = jnp.stack([rank, (place // 2) % 4, place // 8, place % 2, place]).astype(jnp.int32)
-    pos = jnp.concatenate([pos, caption_len.reshape(-1), region_count.reshape(-1)])
+    scalars = [pos, caption_len, region_count]
     micro, samples, text, wt = text_in.shape
     regions, wv = image_in.shape[2:]
     dt, dv = wt * Z, wv * Z
@@ -1085,185 +1083,169 @@
     st_w = self_text_qkv.shape[2]
     si_w = self_image_qkv.shape[2]
     ft = co_text_up.shape[1]
-    chunk = ((cv + packed_rows(ct, dt, dv), dv), BF)
     shard = ((cv + packed_rows(ct, wt, wv), wv), BF)
     whole = ((rv + packed_rows(rt, wt, wv), wv), BF)
 
-    both = spread(joined(pad_rows(text_in, nt), pad_rows(image_in, nv), 1)[0])
     groups = [(co_image_up, co_image_down), (text_up, text_down, image_up, image_down)]
-    cuts = cut_weights(pos, groups, n_dp, wv, [])
-    n_cut = 2 * dv // n_dp
-    pieces = spread(cuts)
+    cuts = cut_weights(scalars, groups, n_dp, wv)
+    shards_in = joined(pad_rows(text_in, nt), pad_rows(image_in, nv), 1)[0]
+    both = spread(jnp.concatenate([shards_in, cuts], axis=0))
+    first, last = whole[0][0], whole[0][0] + 2 * dv // n_dp
     w_mid = lax.all_gather(
-        jnp.stack([piece[:n_cut] for piece in pieces]), "dp", axis=1, tiled=True
+        jnp.stack([piece[first:last] for piece in both]), "dp", axis=1, tiled=True
     )
     w_end = lax.all_gather(
-        jnp.stack([piece[n_cut:] for piece in pieces]), "dp", axis=1, tiled=True
+        jnp.stack([piece[last:] for piece in both]), "dp", axis=1, tiled=True
+    )
+    co_dims = (samples, text, regions, nt, nv)
+    text_dims = (samples, text, nt, TEXT_HEAD, LENGTHS)
+    image_dims = (samples, regions, nv, IMAGE_HEAD, LENGTHS + micro * samples)
+    xt0, xv0, bt, bv, qt0, qv0, ot0, ov0, st, sv = run(
+        "co_fwd", functools.partial(co_fwd, co_dims),
+        [((rt, dt), BF, 0), ((rv, dv), BF, 0), ((ct, dt), BF, 0), ((cv, dv), BF, 0),
+         ((3, rt, co_w), BF, 0), ((3, rv, co_w), BF, 0), ((rt, co_w), BF, 0),
+         ((rv, co_w), BF, 0), ((ct, dt), BF, Z), ((cv, dv), BF, Z)],
+        [scalars, both, co_text_qkv, co_image_qkv, co_text_out, co_image_out],
     )
     n_text = 2 * dt * (ft // wv)
     w_text = View(w_end, (slice(None), pl.ds(0, n_text)), (Z, n_text, wv))
     w_image = View(w_end, (slice(None), pl.ds(n_text, 2 * dv)), (Z, 2 * dv, wv))
-
-    co_dims = (samples, text, regions, nt, nv)
-    text_dims = (samples, text, nt, TEXT_HEAD, LENGTHS)
-    image_dims = (samples, regions, nv, IMAGE_HEAD, LENGTHS + micro * samples)
-
-    xt0, xv0, bt, bv, qt0, qv0, ot0, ov0, s = run(
-        "co_fwd", functools.partial(co_fwd, co_dims),
-        [((rt, dt), BF, 0), ((rv, dv), BF, 0), ((ct, dt), BF, 0), ((cv, dv), BF, 0),
-         ((3, rt, co_w), BF, 0), ((3, rv, co_w), BF, 0), ((rt, co_w), BF, 0),
-         ((rv, co_w), BF, 0), (*chunk, Z)],
-        [pos, both, co_text_qkv, co_image_qkv, co_text_out, co_image_out],
-    )
-    s = swap(s)
-    norm_t = [((ct, dt), F32, 0), ((ct, dt), F32, 0)]
+    norm_t = [((ct, dt), F32, 0), ((ct, dt), F32, 0), ((ct, dt), BF, 0)]
+    ffn_t = [((rt, dt), BF, 0), ((rt, ft), F32, 0), ((rt, ft), BF, 0), ((ct, dt), BF, Z)]
     zt0, at, atb = run(
-        "text_norm0", functools.partial(text_norm, 0, False), norm_t + [((ct, dt), BF, 0)],
-        [pos, s, bt, text_gains, text_shifts],
-    )
-    cot = joined(pad_rows(text_cot, nt), pad_rows(image_cot, nv), Z)
-    (cot,) = run("cut", cut, [(*shard, Z)], [pos, cot], after=[atb])
-    cot = swap(cot)
-    ffn_t = [((rt, dt), BF, 0), ((rt, ft), F32, 0), ((rt, ft), BF, 0), ((ct, dt), BF, Z)]
+        "text_norm0", functools.partial(text_norm, 0), norm_t,
+        [scalars, swap(st), bt, text_gains, text_shifts],
+    )
     xt1, ut1, gt1, st = run(
-        "text_ffn1", text_ffn, ffn_t, [pos, spread(atb), co_text_up, co_text_down]
+        "text_ffn1", text_ffn, ffn_t, [scalars, spread(atb), co_text_up, co_text_down]
     )
     zv0, av, uv1, gv1, zv1, bv, bvb = run(
         "image_mid", functools.partial(image_mid, 0),
         [((cv, dv), F32, 0), ((cv, dv), BF, 0), ((cv, dv), F32, 0), ((cv, dv), BF, 0),
          ((cv, dv), F32, 0), ((cv, dv), F32, 0), ((cv, dv), BF, 0)],
-        [pos, s, bv, w_mid, image_gains, image_shifts],
+        [scalars, swap(sv), bv, w_mid, image_gains, image_shifts],
         [((cv, dv), F32)],
-        after=[st[0]],
-    )
-    zt1, bt, both = run(
-        "text_norm1", functools.partial(text_norm, 1, True), norm_t + [(*chunk, 0)],
-        [pos, swap(st), at, text_gains, text_shifts, bvb],
-        after=cot[1:],
-    )
-    both = spread(both)
-    xt2, xv2, qt2, qv2, ot2, ov2, s = run(
-        "self_fwd", functools.partial(self_fwd, text_dims, image_dims),
-        [((rt, dt), BF, 0), ((rv, dv), BF, 0), ((3, rt, st_w), BF, 0),
-         ((3, rv, si_w), BF, 0), ((rt, st_w), BF, 0), ((rv, si_w), BF, 0), (*chunk, Z)],
-        [pos, both, self_text_qkv, self_image_qkv, self_text_out, self_image_out],
-    )
-    s = swap(s)
+    )
+    zt1, bt, btb = run(
+        "text_norm1", functools.partial(text_norm, 1), norm_t,
+        [scalars, swap(st), at, text_gains, text_shifts],
+    )
+    cot = joined(pad_rows(text_cot, nt), pad_rows(image_cot, nv), Z)
+    (cot,) = run("cut", cut, [(*shard, Z)], [scalars, cot])
+    cot = swap(cot)
+    xt2, qt2, ot2, st = run(
+        "text_self", functools.partial(self_fwd, text_dims),
+        [((rt, dt), BF, 0), ((3, rt, st_w), BF, 0), ((rt, st_w), BF, 0), ((ct, dt), BF, Z)],
+        [scalars, spread(btb), self_text_qkv, self_text_out],
+    )
+    xv2, qv2, ov2, sv = run(
+        "image_self", functools.partial(self_fwd, image_dims),
+        [((rv, dv), BF, 0), ((3, rv, si_w), BF, 0), ((rv, si_w), BF, 0), ((cv, dv), BF, Z)],
+        [scalars, spread(bvb), self_image_qkv, self_image_out],
+    )
+    hidden = Z * ft
+    out_t, at3, gt3, dt3, dut3, gt, gtb, stat_t1 = run(
+        "text_turn", functools.partial(text_turn, 2),
+        [((ct, wt), BF, Z), ((ct, dt), BF, 0), ((ct, hidden), BF, 0), ((ct, dt), BF, 0),
+         ((ct, hidden), BF, 0), ((ct, dt), F32, 0), ((ct, dt), BF, 0), ((4, dt), F32, 0)],
+        [scalars, swap(st), bt, cot, w_text, text_gains, text_shifts],
+        [((ct, hidden), F32), ((ct, dt), F32), ((ct, dt), F32)],
+    )
     out_v, av3, gv3, dv3, duv3, gv, gvb, stat_v1 = run(
         "image_turn", functools.partial(image_turn, 2),
         [((cv, wv), BF, Z), ((cv, dv), BF, 0), ((cv, dv), BF, 0), ((cv, dv), BF, 0),
          ((cv, dv), BF, 0), ((cv, dv), F32, 0), ((cv, dv), BF, 0), ((4, dv), F32, 0)],
-        [pos, s, bv, cot, w_image, image_gains, image_shifts],
+        [scalars, swap(sv), bv, cot, w_image, image_gains, image_shifts],
         [((cv, dv), F32)] * 8,
     )
-    hidden = Z * ft
-    outs, at3, gt3, dt3, dut3, gt, both, stat_t1 = run(
-        "text_turn", functools.partial(text_turn, 2),
-        [(*shard, Z), ((ct, dt), BF, 0), ((ct, hidden), BF, 0), ((ct, dt), BF, 0),
-         ((ct, hidden), BF, 0), ((ct, dt), F32, 0), (*chunk, 0), ((4, dt), F32, 0)],
-        [pos, s, bt, cot, out_v, gvb, w_text, text_gains, text_shifts],
-        [((ct, hidden), F32), ((ct, dt), F32), ((ct, dt), F32)],
-    )
-
     back_ffn = [((rt, dt), BF, 0), ((rt, ft), BF, 0), ((ct, dt), BF, Z)]
     stat_shape = ((2, dt), F32, 0)
-
-    def image_ffn_grads(name, *saved, after):
+    def image_ffn_grads(name, *saved):
         keep, give = run(
-            "grads_" + name, grads_image_ffn, [((Z * dv, wv), BF, 0)] * 2, [pos, *saved],
-            after=after,
+            "grads_" + name, grads_image_ffn, [((Z * dv, wv), BF, 0)] * 2, [scalars, *saved]
         )
         return keep, along(give, 0, 0, 1)
-
     def core_summed(name, halves, after):
         (chunks,) = run(
-            "core_sum_" + name, core_sum, [((dv, wv), BF, Z)], [pos, *halves], after=after
+            "core_sum_" + name, core_sum, [((dv, wv), BF, Z)], [scalars, *halves], after=after
         )
         return chunks
-
-    both = spread(both)
     (end,) = run(
         "grads_end", grads_end, [((n_dp, Z, (n_text + 2 * dv) // n_dp, wv), BF, 0)],
-        [pos, at3, dut3, gt3, dt3, av3, duv3, gv3, dv3],
+        [scalars, at3, dut3, gt3, dt3, av3, duv3, gv3, dv3],
     )
     end_cut = lax.psum_scatter(end, "dp", scatter_dimension=0, tiled=False)
-    dt2, dv2, dqt2, dqv2, s = run(
-        "self_back", functools.partial(self_bwd, text_dims, image_dims),
-        [((rt, dt), BF, 0), ((rv, dv), BF, 0), ((3, rt, st_w), BF, 0), ((3, rv, si_w), BF, 0),
-         (*chunk, Z)],
-        [pos, both, qt2, qv2, self_text_qkv, self_image_qkv,
-         self_text_out, self_image_out],
-        [((rt, st_w), BF), ((rv, si_w), BF)],
-        after=[end],
-    )
-    s = swap(s)
+    dt2, dqt2, st = run(
+        "text_self_back", functools.partial(self_bwd, text_dims),
+        [((rt, dt), BF, 0), ((3, rt, st_w), BF, 0), ((ct, dt), BF, Z)],
+        [scalars, spread(gtb), qt2, self_text_qkv, self_text_out],
+        [((rt, st_w), BF)],
+    )
+    dv2, dqv2, sv = run(
+        "image_self_back", functools.partial(self_bwd, image_dims),
+        [((rv, dv), BF, 0), ((3, rv, si_w), BF, 0), ((cv, dv), BF, Z)],
+        [scalars, spread(gvb), qv2, self_image_qkv, self_image_out],
+        [((rv, si_w), BF)],
+    )
+    gt, gtb, stat_t2 = run(
+        "text_norm1_back", functools.partial(text_norm_back, 1),
+        [((ct, dt), F32, 0), ((ct, dt), BF, 0), stat_shape],
+        [scalars, swap(st), gt, zt1, text_gains],
+    )
     st_q, sv_q, st_o, sv_o = run(
         "grads_self", grads_attention,
         [((3, dt, st_w), BF, 0), ((3, dv, si_w), BF, 0), ((st_w, dt), BF, 0), ((si_w, dv), BF, 0)],
-        [pos, xt2, dqt2, xv2, dqv2, ot2, dt2, ov2, dv2],
-    )
-    gt, gtb, stat_t2 = run(
-        "text_norm1_back", functools.partial(text_norm_back, 1, False),
-        [((ct, dt), F32, 0), ((ct, dt), BF, 0), stat_shape],
-        [pos, s, gt, zt1, text_gains],
-        after=[st_o],
-    )
-    g = spread(gtb)
-    dv1, duv1, gv, gvb, stat_v0 = run(
-        "image_mid_back", functools.partial(image_mid_back, 0),
-        [((cv, dv), BF, 0), ((cv, dv), BF, 0), ((cv, dv), F32, 0), ((cv, dv), BF, 0),
-         ((4, dv), F32, 0)],
-        [pos, s, gv, zv1, zv0, uv1, w_mid, image_gains],
-        [((cv, dv), F32)] * 2,
-        after=[stat_t2],
+        [scalars, xt2, dqt2, xv2, dqv2, ot2, dt2, ov2, dv2],
     )
     dt1, dut1, st = run(
         "text_ffn1_back", text_ffn_back, back_ffn,
-        [pos, g, co_text_up, co_text_down, ut1],
-        after=[stat_v0],
-    )
-    st = swap(st)
-    mid_f = image_ffn_grads("mid", av, duv1, gv1, dv1, after=[dt1])
-    gt, both = run(
+        [scalars, spread(gtb), co_text_up, co_text_down, ut1],
+    )
+    dv1, duv1, gv, gvb, _ = run(
+        "image_mid_back", functools.partial(image_mid_back, 0),
+        [((cv, dv), BF, 0), ((cv, dv), BF, 0), ((cv, dv), F32, 0), ((cv + 16, dv), BF, 0),
+         ((4, dv), F32, 0)],
+        [scalars, swap(sv), gv, zv1, zv0, uv1, w_mid, image_gains, stat_v1],
+        [((cv, dv), F32)] * 2,
+    )
+    mid_f = image_ffn_grads("mid", av, duv1, gv1, dv1)
+    gt, gtb, _ = run(
         "text_norm0_back", functools.partial(text_norm_back_stats, 0),
-        [((ct, dt), F32, 0), ((chunk[0][0] + 16, dv), BF, 0)],
-        [pos, st, gt, zt0, text_gains, gvb, stat_t2, stat_t1, stat_v0, stat_v1],
-        after=[mid_f[0]],
-    )
-    both = spread(both)
-    (end_cut,) = run(
-        "cut_end", cut_static, [(end_cut.shape[1:], BF, Z)], [pos, end_cut], after=[gt]
-    )
-    end_cut = swap(end_cut)
+        [((ct, dt), F32, 0), ((ct + 16, dt), BF, 0), stat_shape],
+        [scalars, swap(st), gt, zt0, text_gains, stat_t2, stat_t1],
+    )
     t1_up, t1_down = run(
         "grads_ffn1", grads_text_ffn, [((dt, ft), BF, 0), ((ft, dt), BF, 0)],
-        [pos, xt1, dut1, gt1, dt1], after=[gt],
-    )
-    mid_f = core_summed("mid", mid_f, [t1_up, end_cut[0]])
+        [scalars, xt1, dut1, gt1, dt1],
+    )
+    zt, zv = spread(gtb), spread(gvb)
+    mid_f = core_summed("mid", mid_f, zt[1:] + zv[1:])
     dqt0, dqv0, tq, vq, to, vo = run(
         "co_back", functools.partial(co_bwd, co_dims),
         [((3, rt, co_w), BF, 0), ((3, rv, co_w), BF, 0),
          ((3, dt, co_w), BF, 0), ((3, dv, co_w), BF, 0), ((co_w, dt), BF, 0), ((co_w, dv), BF, 0)],
-        [pos, both, qt0, qv0, co_text_out, co_image_out, xt0, xv0, ot0, ov0],
+        [scalars, zt, zv, qt0, qv0, co_text_out, co_image_out, xt0, xv0, ot0, ov0],
         [((rt, dt), BF), ((rv, dv), BF), ((rt, co_w), BF), ((rv, co_w), BF)],
-        after=[mid_f[0]],
-    )
-    (end,) = run(
-        "place_end", place_rows, [((n_text + 2 * dv, wv), BF, 0)], [pos, end_cut], after=[to]
-    )
+    )
+    (end_cut,) = run(
+        "cut_end", cut_static, [(end_cut.shape[1:], BF, Z)], [scalars, end_cut]
+    )
+    end_cut = swap(end_cut)
     (s,) = run(
         "co_back_in", co_bwd_in, [(*whole, Z)],
-        [pos, dqt0, dqv0, co_text_qkv, co_image_qkv, gt, gv],
+        [scalars, dqt0, dqv0, co_text_qkv, co_image_qkv, gt, gv],
         [((rt, wt), F32), ((rv, wv), F32)],
-        after=[end],
     )
     (mid_f,) = run(
         "tensor_sum_mid", tensor_sum_stats, [((2, dv + 32, wv), BF, 0)],
-        [pos, swap(mid_f), both], after=[end, s[0]],
+        [scalars, swap(mid_f), zt, zv],
+    )
+    (end,) = run(
+        "place_end", place_rows, [((n_text + 2 * dv, wv), BF, 0)], [scalars, end_cut]
     )
     late = lax.psum((st_q, t1_up, t1_down, sv_q, st_o, sv_o, tq, vq, to, vo, mid_f, end), "dp")
     s = swap(s)
-    outs = swap(outs)
+    out_t, out_v = swap(out_t), swap(out_v)
     ffn_out = [((dt, ft), F32, 0), ((ft, dt), F32, 0)]
     image_out_shapes = [((dv, wv), F32, 0), ((wv, dv), F32, 0)]
     (st_q, t1_up, t1_down, sv_q, st_o, sv_o, tq, vq, to, vo, mid_up, mid_down, tg, ts, vg, vs,
@@ -1274,11 +1256,12 @@
            ((3, dt, co_w), F32, 0), ((3, dv, co_w), F32, 0),
            ((co_w, dt), F32, 0), ((co_w, dv), F32, 0)] + image_out_shapes
         + [((4, dt), F32, 0)] * 2 + [((4, dv), F32, 0)] * 2 + ffn_out + image_out_shapes,
-        [pos, *late],
+        [scalars, *late],
     )
     st_q = st_q.transpose(0, 2, 1)
 
-    text_out, image_out = parted(in_order(outs, rank), ct, wt)
+    text_out = in_order(out_t, rank).reshape(rt, wt)
+    image_out = in_order(out_v, rank).reshape(rv, wv)
     text_grad, image_grad = parted(sum(member.astype(F32) for member in s)[None], rt, wt)
     return (
         unpad_rows(text_out, text_in.shape, nt).astype(F32),

time: 587 us -> 528 us (0.90)
  waiting for transfers between devices: 280 us -> 194 us
  starting transfers between devices: 72.1 us -> 98.7 us
    ppermute x51 -> x69, waiting for transfers between devices: 172 us -> 75.1 us  [shift(): lax.ppermute(values, 'tensor', [(i, (i + k) % Z) for i in range(Z)])]
    ppermute x51 -> x69, starting transfers between devices: 71.8 us -> 98.5 us  [shift(): lax.ppermute(values, 'tensor', [(i, (i + k) % Z) for i in range(Z)])]
    all_gather x2, waiting for transfers between devices: 0.01 us -> 11.2 us  [the longest x1 11.2 us: shards(): lax.all_gather(jnp.stack([piece[last:] for piece in both]), 'dp', axis=1,...]
    pallas_call x25 -> x27, Pallas kernels: 189 us -> 189 us  [run(): pl.pallas_call(staged_body, out_shape=shapes, in_specs=[pl.BlockSpec(memo...]
  transfers between devices with their start and end apart: 56 -> 74, of which waited for: 30 -> 16; matrix products, arithmetic and copies ran while one was open for 2% -> 2% of each run, Pallas kernels for 23% -> 33%
where the time goes in v3:
time: 528 us; the launch traced here: 519 us
  Pallas kernels  195 us (37%)
  waiting for transfers between devices  194 us (37%)
  starting transfers between devices  98.7 us (19%)
  between operations  15.5 us (3%)
  local copies, waits for them, and re-layouts  11.8 us (2%)
    pallas_call x27, Pallas kernels, run(): pl.pallas_call(staged_body, out_shape=shapes, in_specs=[pl.BlockSpec(memo...  189 us
    psum x1, waiting for transfers between devices, shards(): lax.psum((st_q, t1_up, t1_down, sv_q, st_o, sv_o, tq, vq, to, vo, mid_f,...  107 us
    ppermute x69, starting transfers between devices, shift(): lax.ppermute(values, 'tensor', [(i, (i + k) % Z) for i in range(Z)])  98.5 us
    ppermute x69, waiting for transfers between devices, shift(): lax.ppermute(values, 'tensor', [(i, (i + k) % Z) for i in range(Z)])  75.1 us
    all_gather x1, waiting for transfers between devices, shards(): lax.all_gather(jnp.stack([piece[last:] for piece in both]), 'dp', axis=1,...  11.2 us
  transfers between devices with their start and end apart: 74, of which 16 were waited for; matrix products, arithmetic and copies ran while one was open for 2% of the time, Pallas kernels for 33%

profile of v3, /device:TPU:0, one launch (start us, length us, event | category | flops | bytes accessed | tf_op | source)
XLA Modules:
  0.0 518.8 jit_solution(10486272624467582371)
XLA Ops:
  10.2 6.0 %cut_weights.1.refs_11_ = bf16[272,256]{1,0:T(8,128)(2,1)} custom-call(s32[5]{0:T(128)} %stack.91.pos_ref.refs_0_, bf16[1024,256]{1,0:T(8,128)(2,1)} %refs_0_.1, bf16[256,1024]{1,0:T(8,128)(2,1)} %refs_1_.28, bf16[768,768]{1,0:T(8,128)(2,1)} %refs_2_.28, bf16[768,768]{1,0:T(8,128)(2,1)} %refs_3_.1, bf16[1024,256]{1,0:T(8,128)(2,1)} %refs_4_.1, ...), custom_call_target="tpu_custom_call" | custom-call | flops 20000000000 | bytes 1000 | tf_op jit(solution)/shard_map/cut_weights/pallas_call | solution.py:981
  17.3 4.2 collective-permute-start.2
  23.5 22.2 %collective-permute-done.2.refs_6_ = bf16[1104,256]{1,0:T(8,128)(2,1)S(1)} collective-permute-done((bf16[1104,256]{1,0:T(8,128)(2,1)S(1)}, bf16[1104,256]{1,0:T(8,128)(2,1)S(1)}, u32[]{:S(2)}, u32[]{:S(2)}) %collective-permute-start.2) | collective-permute-done | bytes 565280 | tf_op jit(solution)/shard_map/ppermute | solution.py:998
  45.7 3.4 collective-permute-done.refs_4_
  50.9 9.5 %co_fwd.1 = (bf16[256,768]{1,0:T(8,128)(2,1)}, bf16[640,1024]{1,0:T(8,128)(2,1)}, bf16[64,768]{1,0:T(8,128)(2,1)}, bf16[160,1024]{1,0:T(8,128)(2,1)}, bf16[3,256...) custom-call(s32[5]{0:T(128)S(1)} %copy-done, ...), custom_call_target="tpu_custom_call" | custom-call | flops 20000000000 | bytes 1000 | tf_op jit(solution)/shard_map/co_fwd/pallas_call | solution.py:928
  65.5 3.0 collective-permute-done.3.refs_4_
  69.0 3.0 text_norm0.1
  83.0 5.4 %text_ffn1.1 = (bf16[256,768]{1,0:T(8,128)(2,1)}, f32[256,768]{1,0:T(8,128)}, bf16[256,768]{1,0:T(8,128)(2,1)}, bf16[64,768]{1,0:T(8,128)(2,1)}, bf16[64,768]{1,...) custom-call(s32[5]{0:T(128)S(1)} %copy-done, s32[2,3]{1,0:T(2,128)S(1)} %copy-done.1, ...), custom_call_target="tpu_custom_call" | custom-call | flops 20000000000 | bytes 1000 | tf_op jit(solution)/shard_map/text_ffn1/pallas_call | solution.py:928
  88.4 3.0 collective-permute-start.10
  92.1 6.0 %collective-permute-done.13.refs_5_ = bf16[160,1024]{1,0:T(8,128)(2,1)S(1)} collective-permute-done((bf16[160,1024]{1,0:T(8,128)(2,1)S(1)}, bf16[160,1024]{1,0:T(8,128)(2,1)S(1)}, u32[]{:S(2)}, u32[]{:S(2)}) %collective-permute-start.13) | collective-permute-done | bytes 327712 | tf_op jit(solution)/shard_map/ppermute | solution.py:998
  98.2 7.1 %image_mid.1 = (f32[160,1024]{1,0:T(8,128)}, bf16[160,1024]{1,0:T(8,128)(2,1)}, f32[160,1024]{1,0:T(8,128)}, bf16[160,1024]{1,0:T(8,128)(2,1)}, f32[160,1024]{1,...) custom-call(s32[5]{0:T(128)S(1)} %copy-done, s32[2,3]{1,0:T(2,128)S(1)} %copy-done.1, s32[2,3]{1,0:T(2,128)S(1)} %copy-done.2, ...), custom_call_target="tpu_custom_call" | custom-call | flops 20000000000 | bytes 1000 | tf_op jit(solution)/shard_map/image_mid/pallas_call | solution.py:928
  105.3 3.0 text_norm1.1
  110.5 2.7 collective-permute-start.26
  119.1 2.7 collective-permute-start.22
  121.8 6.8 %text_self.1 = (bf16[256,768]{1,0:T(8,128)(2,1)}, bf16[3,256,192]{2,1,0:T(8,128)(2,1)}, bf16[256,192]{1,0:T(8,128)(2,1)}, bf16[64,768]{1,0:T(8,128)(2,1)}, bf16[...) custom-call(s32[5]{0:T(128)S(1)} %copy-done, s32[2,3]{1,0:T(2,128)S(1)} %copy-done.1, ...), custom_call_target="tpu_custom_call" | custom-call | flops 20000000000 | bytes 1000 | tf_op jit(solution)/shard_map/text_self/pallas_call | solution.py:928
  128.6 5.8 %collective-permute-done.21.refs_9_ = bf16[208,256]{1,0:T(8,128)(2,1)S(1)} collective-permute-done((bf16[208,256]{1,0:T(8,128)(2,1)}, bf16[208,256]{1,0:T(8,128)(2,1)S(1)}, u32[]{:S(2)}, u32[]{:S(2)}) %collective-permute-start.21) | collective-permute-done | bytes 106528 | tf_op jit(solution)/shard_map/ppermute | solution.py:998
  139.1 7.3 %image_self.1 = (bf16[640,1024]{1,0:T(8,128)(2,1)}, bf16[3,640,256]{2,1,0:T(8,128)(2,1)}, bf16[640,256]{1,0:T(8,128)(2,1)}, bf16[160,1024]{1,0:T(8,128)(2,1)}, b...) custom-call(s32[5]{0:T(128)S(1)} %copy-done, s32[2,3]{1,0:T(2,128)S(1)} %copy-done.1, ...), custom_call_target="tpu_custom_call" | custom-call | flops 20000000000 | bytes 1000 | tf_op jit(solution)/shard_map/image_self/pallas_call | solution.py:928
  146.8 2.8 collective-permute-start.31
  151.4 11.2 %all-gather.5.cloned.1.call-done.refs_12_ = bf16[4,6656,256]{2,1,0:T(8,128)(2,1)} async-done(((bf16[4,208,256]{2,1,0:T(8,128)(2,1)}), bf16[4,6656,256]{2,1,0:T(8,128)(2,1)}) %all-gather.5.cloned.1.call-update) | async-done | bytes 13631504 | tf_op jit(solution)/shard_map/all_gather | solution.py:1097
  162.7 12.2 %text_turn.1 = (bf16[64,192]{1,0:T(8,128)(2,1)}, bf16[64,192]{1,0:T(8,128)(2,1)}, bf16[64,192]{1,0:T(8,128)(2,1)}, bf16[64,192]{1,0:T(8,128)(2,1)}, bf16[64,768]...) custom-call(s32[5]{0:T(128)S(1)} %copy-done, ...), custom_call_target="tpu_custom_call" | custom-call | flops 20000000000 | bytes 1000 | tf_op jit(solution)/shard_map/text_turn/pallas_call | solution.py:928
  174.9 3.0 collective-permute-start.38
  179.5 11.5 %image_turn.1 = (bf16[160,256]{1,0:T(8,128)(2,1)}, bf16[160,256]{1,0:T(8,128)(2,1)}, bf16[160,256]{1,0:T(8,128)(2,1)}, bf16[160,256]{1,0:T(8,128)(2,1)}, bf16[16...) custom-call(s32[5]{0:T(128)S(1)} %copy-done, ...), custom_call_target="tpu_custom_call" | custom-call | flops 20000000000 | bytes 1000 | tf_op jit(solution)/shard_map/image_turn/pallas_call | solution.py:928
  195.1 10.9 %grads_end.1.refs_10_ = bf16[32,4,208,256]{3,2,1,0:T(8,128)(2,1)} custom-call(s32[5]{0:T(128)S(1)} %copy-done, s32[2,3]{1,0:T(2,128)S(1)} %copy-done.1, s32[2,3]{1,0:T(2,128)S(1)} %copy-done.2, bf16[64,768]{1,0:T(8,128)(2,1)} %get-tuple-element.223.refs_3_, bf16[64,3072]{1,0:T(8,128)(2,1)} %get-tuple-element.224.refs_4_, ...), custom_call_target="tpu_custom_call" | custom-call | flops 20000000000 | bytes 1000 | tf_op jit(solution)/shard_map/grads_end/pallas_call | solution.py:928
  207.4 8.6 %text_self_back.1 = (bf16[256,768]{1,0:T(8,128)(2,1)}, bf16[3,256,192]{2,1,0:T(8,128)(2,1)}, bf16[64,768]{1,0:T(8,128)(2,1)}, bf16[64,768]{1,0:T(8,128)(2,1)}, b...) custom-call(s32[5]{0:T(128)S(1)} %copy-done, s32[2,3]{1,0:T(2,128)S(1)} %copy-done.1, s32[2,3]{1,0:T(2,128)S(1)} %copy-done.2, ...), custom_call_target="tpu_custom_call" | custom-call | flops 20000000000 | bytes 1000 | tf_op jit(solution)/shard_map/text_self_back/pallas_call | solution.py:928
  217.8 2.9 collective-permute-start.40
  220.8 11.6 %image_self_back.1 = (bf16[640,1024]{1,0:T(8,128)(2,1)}, bf16[3,640,256]{2,1,0:T(8,128)(2,1)}, bf16[160,1024]{1,0:T(8,128)(2,1)}, bf16[160,1024]{1,0:T(8,128)(2,...) custom-call(s32[5]{0:T(128)S(1)} %copy-done, s32[2,3]{1,0:T(2,128)S(1)} %copy-done.1, s32[2,3]{1,0:T(2,128)S(1)} %copy-done.2, ...), custom_call_target="tpu_custom_call" | custom-call | flops 20000000000 | bytes 1000 | tf_op jit(solution)/shard_map/image_self_back/pallas_call | solution.py:928
  232.5 3.2 text_norm1_back.1
  236.8 2.8 collective-permute-start.46
  240.3 4.2 collective-permute-start.52
  244.5 6.9 %grads_self.1 = (bf16[3,768,192]{2,1,0:T(8,128)(2,1)}, bf16[3,1024,256]{2,1,0:T(8,128)(2,1)}, bf16[192,768]{1,0:T(8,128)(2,1)}, bf16[256,1024]{1,0:T(8,128)(2,1)}) custom-call(s32[5]{0:T(128)S(1)} %copy-done, s32[2,3]{1,0:T(2,128)S(1)} %copy-done.1, s32[2,3]{1,0:T(2,128)S(1)} %copy-done.2, bf16[256,768]{1,0:T(8,128)(2,1)} %get-tuple-element.242.refs_3_, ...), custom_call_target="tpu_custom_call" | custom-call | flops 20000000000 | bytes 1000 | tf_op jit(solution)/shard_map/grads_self/pallas_call | solution.py:928
  251.9 7.1 %text_ffn1_back.1 = (bf16[256,768]{1,0:T(8,128)(2,1)}, bf16[256,768]{1,0:T(8,128)(2,1)}, bf16[64,768]{1,0:T(8,128)(2,1)}, bf16[64,768]{1,0:T(8,128)(2,1)}, bf16[...) custom-call(s32[5]{0:T(128)S(1)} %copy-done, s32[2,3]{1,0:T(2,128)S(1)} %copy-done.1, s32[2,3]{1,0:T(2,128)S(1)} %copy-done.2, ...), custom_call_target="tpu_custom_call" | custom-call | flops 20000000000 | bytes 1000 | tf_op jit(solution)/shard_map/text_ffn1_back/pallas_call | solution.py:928
  263.5 9.8 %image_mid_back.1 = (bf16[160,1024]{1,0:T(8,128)(2,1)}, bf16[160,1024]{1,0:T(8,128)(2,1)}, f32[160,1024]{1,0:T(8,128)}, bf16[176,1024]{1,0:T(8,128)(2,1)}, f32[4,1024]{1,0:T(4,128)}) custom-call(s32[5]{0:T(128)S(1)} %copy-done, s32[2,3]{1,0:T(2,128)S(1)} %copy-done.1, s32[2,3]{1,0:T(2,128)S(1)} %copy-done.2, ...), custom_call_target="tpu_custom_call" | custom-call | flops 20000000000 | bytes 1000 | tf_op jit(solution)/shard_map/image_mid_back/pallas_call | solution.py:928
  273.2 5.0 grads_mid.1
  278.3 3.2 text_norm0_back.1
  283.5 2.8 collective-permute-start.59
  292.0 3.8 grads_ffn1.1
  295.8 12.4 %collective-permute-done.54.refs_6_.refs_4_.refs_8_ = bf16[80,768]{1,0:T(8,128)(2,1)S(1)} collective-permute-done((bf16[80,768]{1,0:T(8,128)(2,1)}, bf16[80,768]{1,0:T(8,128)(2,1)S(1)}, u32[]{:S(2)}, u32[]{:S(2)}) %collective-permute-start.54) | collective-permute-done | bytes 122912 | tf_op jit(solution)/shard_map/ppermute | solution.py:998
  308.2 3.7 core_sum_mid.1
  315.5 14.2 %co_back.1 = (bf16[3,256,256]{2,1,0:T(8,128)(2,1)}, bf16[3,640,256]{2,1,0:T(8,128)(2,1)}, bf16[3,768,256]{2,1,0:T(8,128)(2,1)}, bf16[3,1024,256]{2,1,0:T(8,128)(...) custom-call(s32[5]{0:T(128)S(1)} %copy-done, s32[2,3]{1,0:T(2,128)S(1)} %copy-done.1, s32[2,3]{1,0:T(2,128)S(1)} %copy-done.2, ...), custom_call_target="tpu_custom_call" | custom-call | flops 20000000000 | bytes 1000 | tf_op jit(solution)/shard_map/co_back/pallas_call | solution.py:928
  334.9 10.0 %co_back_in.1 = (bf16[832,256]{1,0:T(8,128)(2,1)}, bf16[832,256]{1,0:T(8,128)(2,1)}, bf16[832,256]{1,0:T(8,128)(2,1)}, bf16[832,256]{1,0:T(8,128)(2,1)}) custom-call(s32[5]{0:T(128)S(1)} %copy-done, s32[2,3]{1,0:T(2,128)S(1)} %copy-done.1, s32[2,3]{1,0:T(2,128)S(1)} %copy-done.2, bf16[3,256,256]{2,1,0:T(8,128)(2,1)} %get-tuple-element.283.refs_4_.refs_3_, ...), custom_call_target="tpu_custom_call" | custom-call | flops 20000000000 | bytes 1000 | tf_op jit(solution)/shard_map/co_back_in/pallas_call | solution.py:928
  345.0 2.9 collective-permute-start.69
  347.9 3.3 tensor_sum_mid.1.refs_7_
  351.2 3.4 place_end.1.refs_15_
  355.3 2.6 collective-permute-start.27
  367.2 2.9 collective-permute-done.35
  375.1 12.4 %collective-permute-done.61 = bf16[832,256]{1,0:T(8,128)(2,1)S(1)} collective-permute-done((bf16[832,256]{1,0:T(8,128)(2,1)S(1)}, bf16[832,256]{1,0:T(8,128)(2,1)S(1)}, u32[]{:S(2)}, u32[]{:S(2)}) %collective-permute-start.61) | collective-permute-done | bytes 426016 | tf_op jit(solution)/shard_map/ppermute | solution.py:998
  390.2 107.2 %all-reduce.7.cloned.1.call-done = (bf16[3,768,192]{2,1,0:T(8,128)(2,1)}, bf16[768,768]{1,0:T(8,128)(2,1)}, bf16[768,768]{1,0:T(8,128)(2,1)}, bf16[3,1024,256]{2...) async-done(((bf16[3,768,192]{2,1,0:T(8,128)(2,1)}, ...) | async-done | bytes 13795344 | tf_op jit(solution)/shard_map/psum | solution.py:1246
  497.5 14.3 %finish.1 = (f32[3,192,768]{2,1,0:T(8,128)}, f32[768,768]{1,0:T(8,128)}, f32[768,768]{1,0:T(8,128)}, f32[3,1024,256]{2,1,0:T(8,128)}, f32[192,768]{1,0:T(8,128)}...) custom-call(s32[5]{0:T(128)S(1)} %copy-done, ...), custom_call_target="tpu_custom_call" | custom-call | flops 20000000000 | bytes 1000 | tf_op jit(solution)/shard_map/finish/pallas_call | solution.py:928
  (259 shorter events, 89.7 us)
Async XLA Ops:
  7.2 91.0 %all-gather.3.cloned.1.call-start = ((), (), s32[]{:S(2)}) async-start(), calls=%async_computation.1 | async-start | bytes 4325376 | tf_op jit(solution)/shard_map/all_gather | solution.py:1094
  17.3 28.4 %collective-permute-start.2 = (bf16[1104,256]{1,0:T(8,128)(2,1)S(1)}, bf16[1104,256]{1,0:T(8,128)(2,1)S(1)}, u32[]{:S(2)}, u32[]{:S(2)}) collective-permute-start(bf16[1104,256]{1,0:T(8,128)(2,1)S(1)} %pad_maximum_fusion.refs_3_), channel_id=1, source_target_pairs={{0,96},{32,0},{64,32},{96,64},{1,97},{33,1},{65,33},{97,65},{2,98}... | collective-permute-start | bytes 1695752 | tf_op jit(solution)/shard_map/ppermute | solution.py:998
  21.5 24.2 %collective-permute-start.1 = (bf16[1104,256]{1,0:T(8,128)(2,1)S(1)}, bf16[1104,256]{1,0:T(8,128)(2,1)S(1)}, u32[]{:S(2)}, u32[]{:S(2)}) collective-permute-start(bf16[1104,256]{1,0:T(8,128)(2,1)S(1)} %pad_maximum_fusion.refs_3_), channel_id=1, source_target_pairs={{0,64},{32,96},{64,0},{96,32},{1,65},{33,97},{65,1},{97,33},{2,66}... | collective-permute-start | bytes 1695752 | tf_op jit(solution)/shard_map/ppermute | solution.py:998
  21.5 27.6 %collective-permute-start = (bf16[1104,256]{1,0:T(8,128)(2,1)S(1)}, bf16[1104,256]{1,0:T(8,128)(2,1)S(1)}, u32[]{:S(2)}, u32[]{:S(2)}) collective-permute-start(bf16[1104,256]{1,0:T(8,128)(2,1)S(1)} %pad_maximum_fusion.refs_3_), channel_id=1, source_target_pairs={{0,32},{32,64},{64,96},{96,0},{1,33},{33,65},{65,97},{97,1},{2,34}... | collective-permute-start | bytes 1695752 | tf_op jit(solution)/shard_map/ppermute | solution.py:998
  49.8 112.8 %all-gather.5.cloned.1.call-start = ((), (), s32[]{:S(2)}) async-start(), calls=%async_computation.2 | async-start | bytes 14057472 | tf_op jit(solution)/shard_map/all_gather | solution.py:1097
  50.8 278.9 %reduce-scatter.2.cloned.1.call-start = ((), (), s32[]{:S(2)}) async-start(), calls=%async_computation.3 | async-start | bytes 14057472 | tf_op jit(solution)/shard_map/reduce_scatter | solution.py:1177
  76.3 15.2 %collective-permute-start.12 = (bf16[160,1024]{1,0:T(8,128)(2,1)S(1)}, bf16[160,1024]{1,0:T(8,128)(2,1)S(1)}, u32[]{:S(2)}, u32[]{:S(2)}) collective-permute-start(bf16[160,1024]{1,0:T(8,128)(2,1)S(1)} %copy-done.18), channel_id=1, source_target_pairs={{0,32},{32,64},{64,96},{96,0},{1,33},{33,65},{65,97},{97,1},{2,34}... | collective-permute-start | bytes 983048 | tf_op jit(solution)/shard_map/ppermute | solution.py:998
  78.8 19.4 %collective-permute-start.13 = (bf16[160,1024]{1,0:T(8,128)(2,1)S(1)}, bf16[160,1024]{1,0:T(8,128)(2,1)S(1)}, u32[]{:S(2)}, u32[]{:S(2)}) collective-permute-start(bf16[160,1024]{1,0:T(8,128)(2,1)S(1)} %copy-done.17), channel_id=1, source_target_pairs={{0,64},{32,96},{64,0},{96,32},{1,65},{33,97},{65,1},{97,33},{2,66}... | collective-permute-start | bytes 983048 | tf_op jit(solution)/shard_map/ppermute | solution.py:998
  80.3 17.8 %collective-permute-start.14 = (bf16[160,1024]{1,0:T(8,128)(2,1)S(1)}, bf16[160,1024]{1,0:T(8,128)(2,1)S(1)}, u32[]{:S(2)}, u32[]{:S(2)}) collective-permute-start(bf16[160,1024]{1,0:T(8,128)(2,1)S(1)} %copy-done.15), channel_id=1, source_target_pairs={{0,96},{32,0},{64,32},{96,64},{1,97},{33,1},{65,33},{97,65},{2,98}... | collective-permute-start | bytes 983048 | tf_op jit(solution)/shard_map/ppermute | solution.py:998
  88.3 16.9 %collective-permute-start.9 = (bf16[64,768]{1,0:T(8,128)(2,1)}, bf16[64,768]{1,0:T(8,128)(2,1)S(1)}, u32[]{:S(2)}, u32[]{:S(2)}) collective-permute-start(bf16[64,768]{1,0:T(8,128)(2,1)} %get-tuple-element.183), channel_id=1, source_target_pairs={{0,32},{32,64},{64,96},{96,0},{1,33},{33,65},{65,97},{97,1},{2,34}... | collective-permute-start | bytes 294920 | tf_op jit(solution)/shard_map/ppermute | solution.py:998
  88.4 16.9 %collective-permute-start.10 = (bf16[64,768]{1,0:T(8,128)(2,1)}, bf16[64,768]{1,0:T(8,128)(2,1)S(1)}, u32[]{:S(2)}, u32[]{:S(2)}) collective-permute-start(bf16[64,768]{1,0:T(8,128)(2,1)} %get-tuple-element.184), channel_id=1, source_target_pairs={{0,64},{32,96},{64,0},{96,32},{1,65},{33,97},{65,1},{97,33},{2,66}... | collective-permute-start | bytes 294920 | tf_op jit(solution)/shard_map/ppermute | solution.py:998
  110.5 24.4 %collective-permute-start.26 = (bf16[160,1024]{1,0:T(8,128)(2,1)S(1)}, bf16[160,1024]{1,0:T(8,128)(2,1)S(1)}, u32[]{:S(2)}, u32[]{:S(2)}) collective-permute-start(bf16[160,1024]{1,0:T(8,128)(2,1)S(1)} %copy-done.16), channel_id=1, source_target_pairs={{0,96},{32,0},{64,32},{96,64},{1,97},{33,1},{65,33},{97,65},{2,98}... | collective-permute-start | bytes 983048 | tf_op jit(solution)/shard_map/ppermute | solution.py:998
  113.1 23.2 %collective-permute-start.25 = (bf16[160,1024]{1,0:T(8,128)(2,1)S(1)}, bf16[160,1024]{1,0:T(8,128)(2,1)S(1)}, u32[]{:S(2)}, u32[]{:S(2)}) collective-permute-start(bf16[160,1024]{1,0:T(8,128)(2,1)S(1)} %copy-done.16), channel_id=1, source_target_pairs={{0,64},{32,96},{64,0},{96,32},{1,65},{33,97},{65,1},{97,33},{2,66}... | collective-permute-start | bytes 983048 | tf_op jit(solution)/shard_map/ppermute | solution.py:998
  117.0 20.1 %collective-permute-start.24 = (bf16[160,1024]{1,0:T(8,128)(2,1)S(1)}, bf16[160,1024]{1,0:T(8,128)(2,1)S(1)}, u32[]{:S(2)}, u32[]{:S(2)}) collective-permute-start(bf16[160,1024]{1,0:T(8,128)(2,1)S(1)} %copy-done.16), channel_id=1, source_target_pairs={{0,32},{32,64},{64,96},{96,0},{1,33},{33,65},{65,97},{97,1},{2,34}... | collective-permute-start | bytes 983048 | tf_op jit(solution)/shard_map/ppermute | solution.py:998
  118.5 15.9 %collective-permute-start.21 = (bf16[208,256]{1,0:T(8,128)(2,1)}, bf16[208,256]{1,0:T(8,128)(2,1)S(1)}, u32[]{:S(2)}, u32[]{:S(2)}) collective-permute-start(bf16[208,256]{1,0:T(8,128)(2,1)} %get-tuple-element.201), channel_id=1, source_target_pairs={{0,32},{32,64},{64,96},{96,0},{1,33},{33,65},{65,97},{97,1},{2,34}... | collective-permute-start | bytes 319496 | tf_op jit(solution)/shard_map/ppermute | solution.py:998
  119.1 27.4 %collective-permute-start.22 = (bf16[208,256]{1,0:T(8,128)(2,1)}, bf16[208,256]{1,0:T(8,128)(2,1)S(1)}, u32[]{:S(2)}, u32[]{:S(2)}) collective-permute-start(bf16[208,256]{1,0:T(8,128)(2,1)} %get-tuple-element.202), channel_id=1, source_target_pairs={{0,64},{32,96},{64,0},{96,32},{1,65},{33,97},{65,1},{97,33},{2,66}... | collective-permute-start | bytes 319496 | tf_op jit(solution)/shard_map/ppermute | solution.py:998
  134.9 14.7 %collective-permute-start.18 = (bf16[64,768]{1,0:T(8,128)(2,1)}, bf16[64,768]{1,0:T(8,128)(2,1)S(1)}, u32[]{:S(2)}, u32[]{:S(2)}) collective-permute-start(bf16[64,768]{1,0:T(8,128)(2,1)} %get-tuple-element.197), channel_id=1, source_target_pairs={{0,32},{32,64},{64,96},{96,0},{1,33},{33,65},{65,97},{97,1},{2,34}... | collective-permute-start | bytes 294920 | tf_op jit(solution)/shard_map/ppermute | solution.py:998
  136.4 15.0 %collective-permute-start.19 = (bf16[64,768]{1,0:T(8,128)(2,1)}, bf16[64,768]{1,0:T(8,128)(2,1)S(1)}, u32[]{:S(2)}, u32[]{:S(2)}) collective-permute-start(bf16[64,768]{1,0:T(8,128)(2,1)} %get-tuple-element.198), channel_id=1, source_target_pairs={{0,64},{32,96},{64,0},{96,32},{1,65},{33,97},{65,1},{97,33},{2,66}... | collective-permute-start | bytes 294920 | tf_op jit(solution)/shard_map/ppermute | solution.py:998
  146.5 32.1 %collective-permute-start.30 = (bf16[160,1024]{1,0:T(8,128)(2,1)}, bf16[160,1024]{1,0:T(8,128)(2,1)S(1)}, u32[]{:S(2)}, u32[]{:S(2)}) collective-permute-start(bf16[160,1024]{1,0:T(8,128)(2,1)} %get-tuple-element.212), channel_id=1, source_target_pairs={{0,32},{32,64},{64,96},{96,0},{1,33},{33,65},{65,97},{97,1},{2,34}... | collective-permute-start | bytes 983048 | tf_op jit(solution)/shard_map/ppermute | solution.py:998
  146.8 32.8 %collective-permute-start.31 = (bf16[160,1024]{1,0:T(8,128)(2,1)}, bf16[160,1024]{1,0:T(8,128)(2,1)S(1)}, u32[]{:S(2)}, u32[]{:S(2)}) collective-permute-start(bf16[160,1024]{1,0:T(8,128)(2,1)} %get-tuple-element.213), channel_id=1, source_target_pairs={{0,64},{32,96},{64,0},{96,32},{1,65},{33,97},{65,1},{97,33},{2,66}... | collective-permute-start | bytes 983048 | tf_op jit(solution)/shard_map/ppermute | solution.py:998
  149.6 29.9 %collective-permute-start.32 = (bf16[160,1024]{1,0:T(8,128)(2,1)}, bf16[160,1024]{1,0:T(8,128)(2,1)S(1)}, u32[]{:S(2)}, u32[]{:S(2)}) collective-permute-start(bf16[160,1024]{1,0:T(8,128)(2,1)} %get-tuple-element.214), channel_id=1, source_target_pairs={{0,96},{32,0},{64,32},{96,64},{1,97},{33,1},{65,33},{97,65},{2,98}... | collective-permute-start | bytes 983048 | tf_op jit(solution)/shard_map/ppermute | solution.py:998
  174.9 31.2 %collective-permute-start.38 = (bf16[64,768]{1,0:T(8,128)(2,1)}, bf16[64,768]{1,0:T(8,128)(2,1)S(1)}, u32[]{:S(2)}, u32[]{:S(2)}) collective-permute-start(bf16[64,768]{1,0:T(8,128)(2,1)} %get-tuple-element.221.refs_3_), channel_id=1, source_target_pairs={{0,96},{32,0},{64,32},{96,64},{1,97},{33,1},{65,33},{97,65},{2,98}... | collective-permute-start | bytes 294920 | tf_op jit(solution)/shard_map/ppermute | solution.py:998
  177.9 29.4 %collective-permute-start.37 = (bf16[64,768]{1,0:T(8,128)(2,1)}, bf16[64,768]{1,0:T(8,128)(2,1)S(1)}, u32[]{:S(2)}, u32[]{:S(2)}) collective-permute-start(bf16[64,768]{1,0:T(8,128)(2,1)} %get-tuple-element.221.refs_3_), channel_id=1, source_target_pairs={{0,64},{32,96},{64,0},{96,32},{1,65},{33,97},{65,1},{97,33},{2,66}... | collective-permute-start | bytes 294920 | tf_op jit(solution)/shard_map/ppermute | solution.py:998
  178.6 28.8 %collective-permute-start.36 = (bf16[64,768]{1,0:T(8,128)(2,1)}, bf16[64,768]{1,0:T(8,128)(2,1)S(1)}, u32[]{:S(2)}, u32[]{:S(2)}) collective-permute-start(bf16[64,768]{1,0:T(8,128)(2,1)} %get-tuple-element.221.refs_3_), channel_id=1, source_target_pairs={{0,32},{32,64},{64,96},{96,0},{1,33},{33,65},{65,97},{97,1},{2,34}... | collective-permute-start | bytes 294920 | tf_op jit(solution)/shard_map/ppermute | solution.py:998
  191.1 29.6 %collective-permute-start.44 = (bf16[160,1024]{1,0:T(8,128)(2,1)}, bf16[160,1024]{1,0:T(8,128)(2,1)S(1)}, u32[]{:S(2)}, u32[]{:S(2)}) collective-permute-start(bf16[160,1024]{1,0:T(8,128)(2,1)} %get-tuple-element.237.refs_3_), channel_id=1, source_target_pairs={{0,96},{32,0},{64,32},{96,64},{1,97},{33,1},{65,33},{97,65},{2,98}... | collective-permute-start | bytes 983048 | tf_op jit(solution)/shard_map/ppermute | solution.py:998
  193.4 27.4 %collective-permute-start.43 = (bf16[160,1024]{1,0:T(8,128)(2,1)}, bf16[160,1024]{1,0:T(8,128)(2,1)S(1)}, u32[]{:S(2)}, u32[]{:S(2)}) collective-permute-start(bf16[160,1024]{1,0:T(8,128)(2,1)} %get-tuple-element.237.refs_3_), channel_id=1, source_target_pairs={{0,64},{32,96},{64,0},{96,32},{1,65},{33,97},{65,1},{97,33},{2,66}... | collective-permute-start | bytes 983048 | tf_op jit(solution)/shard_map/ppermute | solution.py:998
  206.0 291.5 %all-reduce.7.cloned.1.call-start = ((), (), s32[]{:S(2)}) async-start(), calls=%async_computation.4 | async-start | bytes 28180480 | tf_op jit(solution)/shard_map/psum | solution.py:1246
  215.9 16.5 %collective-permute-start.39 = (bf16[64,768]{1,0:T(8,128)(2,1)}, bf16[64,768]{1,0:T(8,128)(2,1)S(1)}, u32[]{:S(2)}, u32[]{:S(2)}) collective-permute-start(bf16[64,768]{1,0:T(8,128)(2,1)} %get-tuple-element.233), channel_id=1, source_target_pairs={{0,32},{32,64},{64,96},{96,0},{1,33},{33,65},{65,97},{97,1},{2,34}... | collective-permute-start | bytes 294920 | tf_op jit(solution)/shard_map/ppermute | solution.py:998
  235.7 15.7 %collective-permute-start.47 = (bf16[64,768]{1,0:T(8,128)(2,1)}, bf16[64,768]{1,0:T(8,128)(2,1)S(1)}, u32[]{:S(2)}, u32[]{:S(2)}) collective-permute-start(bf16[64,768]{1,0:T(8,128)(2,1)} %get-tuple-element.240.refs_3_), channel_id=1, source_target_pairs={{0,96},{32,0},{64,32},{96,64},{1,97},{33,1},{65,33},{97,65},{2,98}... | collective-permute-start | bytes 294920 | tf_op jit(solution)/shard_map/ppermute | solution.py:998
  236.8 15.0 %collective-permute-start.46 = (bf16[64,768]{1,0:T(8,128)(2,1)}, bf16[64,768]{1,0:T(8,128)(2,1)S(1)}, u32[]{:S(2)}, u32[]{:S(2)}) collective-permute-start(bf16[64,768]{1,0:T(8,128)(2,1)} %get-tuple-element.240.refs_3_), channel_id=1, source_target_pairs={{0,64},{32,96},{64,0},{96,32},{1,65},{33,97},{65,1},{97,33},{2,66}... | collective-permute-start | bytes 294920 | tf_op jit(solution)/shard_map/ppermute | solution.py:998
  239.7 21.3 %collective-permute-start.51 = (bf16[160,1024]{1,0:T(8,128)(2,1)S(1)}, bf16[160,1024]{1,0:T(8,128)(2,1)S(1)}, u32[]{:S(2)}, u32[]{:S(2)}) collective-permute-start(bf16[160,1024]{1,0:T(8,128)(2,1)S(1)} %copy-done.21), channel_id=1, source_target_pairs={{0,32},{32,64},{64,96},{96,0},{1,33},{33,65},{65,97},{97,1},{2,34}... | collective-permute-start | bytes 983048 | tf_op jit(solution)/shard_map/ppermute | solution.py:998
  240.3 23.2 %collective-permute-start.52 = (bf16[160,1024]{1,0:T(8,128)(2,1)S(1)}, bf16[160,1024]{1,0:T(8,128)(2,1)S(1)}, u32[]{:S(2)}, u32[]{:S(2)}) collective-permute-start(bf16[160,1024]{1,0:T(8,128)(2,1)S(1)} %copy-done.20), channel_id=1, source_target_pairs={{0,64},{32,96},{64,0},{96,32},{1,65},{33,97},{65,1},{97,33},{2,66}... | collective-permute-start | bytes 983048 | tf_op jit(solution)/shard_map/ppermute | solution.py:998
  259.0 19.3 %collective-permute-start.48 = (bf16[64,768]{1,0:T(8,128)(2,1)}, bf16[64,768]{1,0:T(8,128)(2,1)S(1)}, u32[]{:S(2)}, u32[]{:S(2)}) collective-permute-start(bf16[64,768]{1,0:T(8,128)(2,1)} %get-tuple-element.251), channel_id=1, source_target_pairs={{0,32},{32,64},{64,96},{96,0},{1,33},{33,65},{65,97},{97,1},{2,34}... | collective-permute-start | bytes 294920 | tf_op jit(solution)/shard_map/ppermute | solution.py:998
  260.7 17.6 %collective-permute-start.49 = (bf16[64,768]{1,0:T(8,128)(2,1)}, bf16[64,768]{1,0:T(8,128)(2,1)S(1)}, u32[]{:S(2)}, u32[]{:S(2)}) collective-permute-start(bf16[64,768]{1,0:T(8,128)(2,1)} %get-tuple-element.252), channel_id=1, source_target_pairs={{0,64},{32,96},{64,0},{96,32},{1,65},{33,97},{65,1},{97,33},{2,66}... | collective-permute-start | bytes 294920 | tf_op jit(solution)/shard_map/ppermute | solution.py:998
  260.9 17.4 %collective-permute-start.50 = (bf16[64,768]{1,0:T(8,128)(2,1)}, bf16[64,768]{1,0:T(8,128)(2,1)S(1)}, u32[]{:S(2)}, u32[]{:S(2)}) collective-permute-start(bf16[64,768]{1,0:T(8,128)(2,1)} %get-tuple-element.253), channel_id=1, source_target_pairs={{0,96},{32,0},{64,32},{96,64},{1,97},{33,1},{65,33},{97,65},{2,98}... | collective-permute-start | bytes 294920 | tf_op jit(solution)/shard_map/ppermute | solution.py:998
  278.2 30.0 %collective-permute-start.60 = (bf16[4096,256]{1,0:T(8,128)(2,1)}, bf16[4096,256]{1,0:T(8,128)(2,1)S(1)}, u32[]{:S(2)}, u32[]{:S(2)}) collective-permute-start(bf16[4096,256]{1,0:T(8,128)(2,1)} %get-tuple-element.275), channel_id=1, source_target_pairs={{0,1},{1,0},{2,3},{3,2},{4,5},{5,4},{6,7},{7,6},{8,9},{9,8},{10,11... | collective-permute-start | bytes 6291464 | tf_op jit(solution)/shard_map/ppermute | solution.py:1017
  283.5 24.7 %collective-permute-start.59 = (bf16[176,1024]{1,0:T(8,128)(2,1)S(1)}, bf16[176,1024]{1,0:T(8,128)(2,1)S(1)}, u32[]{:S(2)}, u32[]{:S(2)}) collective-permute-start(bf16[176,1024]{1,0:T(8,128)(2,1)S(1)} %copy-done.14), channel_id=1, source_target_pairs={{0,96},{32,0},{64,32},{96,64},{1,97},{33,1},{65,33},{97,65},{2,98}... | collective-permute-start | bytes 1081352 | tf_op jit(solution)/shard_map/ppermute | solution.py:998
  286.3 21.9 %collective-permute-start.58 = (bf16[176,1024]{1,0:T(8,128)(2,1)S(1)}, bf16[176,1024]{1,0:T(8,128)(2,1)S(1)}, u32[]{:S(2)}, u32[]{:S(2)}) collective-permute-start(bf16[176,1024]{1,0:T(8,128)(2,1)S(1)} %copy-done.14), channel_id=1, source_target_pairs={{0,64},{32,96},{64,0},{96,32},{1,65},{33,97},{65,1},{97,33},{2,66}... | collective-permute-start | bytes 1081352 | tf_op jit(solution)/shard_map/ppermute | solution.py:998
  287.9 20.3 %collective-permute-start.57 = (bf16[176,1024]{1,0:T(8,128)(2,1)S(1)}, bf16[176,1024]{1,0:T(8,128)(2,1)S(1)}, u32[]{:S(2)}, u32[]{:S(2)}) collective-permute-start(bf16[176,1024]{1,0:T(8,128)(2,1)S(1)} %copy-done.14), channel_id=1, source_target_pairs={{0,32},{32,64},{64,96},{96,0},{1,33},{33,65},{65,97},{97,1},{2,34}... | collective-permute-start | bytes 1081352 | tf_op jit(solution)/shard_map/ppermute | solution.py:998
  290.1 18.1 %collective-permute-start.54 = (bf16[80,768]{1,0:T(8,128)(2,1)}, bf16[80,768]{1,0:T(8,128)(2,1)S(1)}, u32[]{:S(2)}, u32[]{:S(2)}) collective-permute-start(bf16[80,768]{1,0:T(8,128)(2,1)} %get-tuple-element.267.refs_3_.refs_7_), channel_id=1, source_target_pairs={{0,32},{32,64},{64,96},{96,0},{1,33},{33,65},{65,97},{97,1},{2,34}... | collective-permute-start | bytes 368648 | tf_op jit(solution)/shard_map/ppermute | solution.py:998
  311.9 33.0 %collective-permute-start.64 = (bf16[1024,256]{1,0:T(8,128)(2,1)}, bf16[1024,256]{1,0:T(8,128)(2,1)S(1)}, u32[]{:S(2)}, u32[]{:S(2)}) collective-permute-start(bf16[1024,256]{1,0:T(8,128)(2,1)} %get-tuple-element.300), channel_id=1, source_target_pairs={{0,32},{32,64},{64,96},{96,0},{1,33},{33,65},{65,97},{97,1},{2,34}... | collective-permute-start | bytes 1572872 | tf_op jit(solution)/shard_map/ppermute | solution.py:998
  312.0 35.9 %collective-permute-start.65 = (bf16[1024,256]{1,0:T(8,128)(2,1)}, bf16[1024,256]{1,0:T(8,128)(2,1)S(1)}, u32[]{:S(2)}, u32[]{:S(2)}) collective-permute-start(bf16[1024,256]{1,0:T(8,128)(2,1)} %get-tuple-element.301), channel_id=1, source_target_pairs={{0,64},{32,96},{64,0},{96,32},{1,65},{33,97},{65,1},{97,33},{2,66}... | collective-permute-start | bytes 1572872 | tf_op jit(solution)/shard_map/ppermute | solution.py:998
  314.1 33.8 %collective-permute-start.66 = (bf16[1024,256]{1,0:T(8,128)(2,1)}, bf16[1024,256]{1,0:T(8,128)(2,1)S(1)}, u32[]{:S(2)}, u32[]{:S(2)}) collective-permute-start(bf16[1024,256]{1,0:T(8,128)(2,1)} %get-tuple-element.302), channel_id=1, source_target_pairs={{0,96},{32,0},{64,32},{96,64},{1,97},{33,1},{65,33},{97,65},{2,98}... | collective-permute-start | bytes 1572872 | tf_op jit(solution)/shard_map/ppermute | solution.py:998
  332.1 19.1 %collective-permute-start.67 = (bf16[208,256]{1,0:T(8,128)(2,1)}, bf16[208,256]{1,0:T(8,128)(2,1)S(1)}, u32[]{:S(2)}, u32[]{:S(2)}) collective-permute-start(bf16[208,256]{1,0:T(8,128)(2,1)} %get-tuple-element.303), channel_id=1, source_target_pairs={{0,32},{32,64},{64,96},{96,0},{1,33},{33,65},{65,97},{97,1},{2,34}... | collective-permute-start | bytes 319496 | tf_op jit(solution)/shard_map/ppermute | solution.py:998
  332.8 18.4 %collective-permute-start.68 = (bf16[208,256]{1,0:T(8,128)(2,1)}, bf16[208,256]{1,0:T(8,128)(2,1)S(1)}, u32[]{:S(2)}, u32[]{:S(2)}) collective-permute-start(bf16[208,256]{1,0:T(8,128)(2,1)} %get-tuple-element.304), channel_id=1, source_target_pairs={{0,64},{32,96},{64,0},{96,32},{1,65},{33,97},{65,1},{97,33},{2,66}... | collective-permute-start | bytes 319496 | tf_op jit(solution)/shard_map/ppermute | solution.py:998
  370.2 17.2 %collective-permute-start.61 = (bf16[832,256]{1,0:T(8,128)(2,1)S(1)}, bf16[832,256]{1,0:T(8,128)(2,1)S(1)}, u32[]{:S(2)}, u32[]{:S(2)}) collective-permute-start(bf16[832,256]{1,0:T(8,128)(2,1)S(1)} %copy-done.13), channel_id=1, source_target_pairs={{0,32},{32,64},{64,96},{96,0},{1,33},{33,65},{65,97},{97,1},{2,34}... | collective-permute-start | bytes 1277960 | tf_op jit(solution)/shard_map/ppermute | solution.py:998
  370.4 17.0 %collective-permute-start.62 = (bf16[832,256]{1,0:T(8,128)(2,1)S(1)}, bf16[832,256]{1,0:T(8,128)(2,1)S(1)}, u32[]{:S(2)}, u32[]{:S(2)}) collective-permute-start(bf16[832,256]{1,0:T(8,128)(2,1)S(1)} %copy-done.12), channel_id=1, source_target_pairs={{0,64},{32,96},{64,0},{96,32},{1,65},{33,97},{65,1},{97,33},{2,66}... | collective-permute-start | bytes 1277960 | tf_op jit(solution)/shard_map/ppermute | solution.py:998
  371.3 16.1 %collective-permute-start.63 = (bf16[832,256]{1,0:T(8,128)(2,1)S(1)}, bf16[832,256]{1,0:T(8,128)(2,1)S(1)}, u32[]{:S(2)}, u32[]{:S(2)}) collective-permute-start(bf16[832,256]{1,0:T(8,128)(2,1)S(1)} %copy-done.11), channel_id=1, source_target_pairs={{0,96},{32,0},{64,32},{96,64},{1,97},{33,1},{65,33},{97,65},{2,98}... | collective-permute-start | bytes 1277960 | tf_op jit(solution)/shard_map/ppermute | solution.py:998
  (57 other events, 629.6 us)
Sparse Core Ops, SparseCore 0:
  49.9 45.2 all-gather.2
  98.1 64.5 all-gather.4
  206.1 105.3 reduce-scatter.1
  354.8 142.6 all-reduce.6
